TPU v7x, 256 devices: a whole 4x4x8 slice. The times are simulated.
256 devices in a mesh: dp: 128 (over y, x, z), mp: 2 (over core).
Axes of the slice: x: 4, y: 4, z: 8, core: 2. Of those that a mesh axis runs over, the one named last changes fastest.
Arguments:
- query_states: bfloat16 [4096, 4096], P('dp')
- passage_states: bfloat16 [32768, 4096], P('dp')
- head_weight: bfloat16 [4096, 2048], P(None, 'mp'), may hold values from -0.09375 to 0.09375
- positives: int32 [4096], P('dp'), may hold values from 0 to 32767, as said below
- negatives: int32 [4096, 8], P('dp'), may hold values from 0 to 32767, as said below
- search_cost_incoming_slope: float32 [4096], P('dp'), may hold values from 20 to 200
Outputs:
- losses: float32 [4096], P('dp')
- query_grads: bfloat16 [4096, 4096], P('dp', 'mp')
- passage_grads: bfloat16 [32768, 4096], P('dp', 'mp')
Inputs may be any that keep to these rules, and one draw needn't show every extreme that they name: `positives`: the queries of one aligned block of 32 rows name, over their positive and hard negatives together, at most 4 passages of any one aligned block of 256 passages (repeats counted); in every draw one block of passages is named exactly 4 times by the queries of every block. `negatives`: see positives: the bound counts both arguments together.
All inputs are finite; a program needn't handle non-finite values.
Results may differ from a plain program's by a relative error of at most 0.015.
Values may be sent and summed in bfloat16 or wider, within the bound.
No kernel may reach another device: no remote copies, remote signals or barrier semaphores. Data moves between devices by JAX's collectives and lax.ppermute only.
A program may use at most 128 MiB of HBM per device.

v0:
```python
import jax
import jax.numpy as jnp
from jax import lax
from jax.sharding import Mesh, PartitionSpec as P

sharpness_divisor = 0.02
bf16 = jnp.bfloat16
f32 = jnp.float32
AUX = 128


def shifted(value, axis, shift):
    n = lax.axis_size(axis)
    return lax.ppermute(value, axis, [(i, (i + shift) % n) for i in range(n)])


def exchanged(parts, axis):
    return lax.all_to_all(parts, axis, split_axis=0, concat_axis=0, tiled=True)


def to_all(value, axis):
    n = lax.axis_size(axis)
    return exchanged(jnp.broadcast_to(value[None], (n,) + value.shape), axis)


def split_three(value):
    high = lax.reduce_precision(value, 8, 7)
    rest = value - high
    middle = lax.reduce_precision(rest, 8, 7)
    return high, middle, rest - middle


def contract(a, b, dims):
    return lax.dot_general(a, b, (dims, ((), ())), preferred_element_type=f32)


def per_device(query_states, passage_states, head_weight, positives, negatives, slope):
    n_y, n_x, n_z = (lax.axis_size(a) for a in ("y", "x", "z"))
    x, z, core = (lax.axis_index(a) for a in ("x", "z", "mp"))
    q_rows, p_rows = query_states.shape[0], passage_states.shape[0]
    depth, width = head_weight.shape
    out_width = depth // 2
    half = q_rows // 2
    slots = n_x * n_z

    def own_first(rows):
        return jnp.where(core == 0, rows, jnp.roll(rows, half, axis=0))

    weight_kept = lax.dynamic_slice_in_dim(head_weight, core * out_width, out_width, 0)
    weight_sent = lax.dynamic_slice_in_dim(head_weight, (1 - core) * out_width, out_width, 0)
    weight_got = shifted(weight_sent, "mp", 1)
    line_positives = [shifted(positives, "y", s) for s in range(1, n_y)]

    q_proj = contract(query_states, head_weight, ((1,), (0,)))
    p_proj = contract(passage_states, head_weight, ((1,), (0,)))
    q_square, p_square = lax.psum(
        (jnp.sum(q_proj * q_proj, axis=1), jnp.sum(p_proj * p_proj, axis=1)), "mp"
    )
    q_inv = lax.rsqrt(q_square + 1e-06)[:, None]
    p_inv = lax.rsqrt(p_square + 1e-06)[:, None]
    q_unit = q_proj * q_inv
    p_unit = p_proj * p_inv
    p_embed = p_unit.astype(bf16)
    p_all = lax.all_gather(p_embed, "y", axis=0, tiled=True)

    ids = jnp.concatenate(
        [positives[:, None], negatives] + [other[:, None] for other in line_positives], axis=1
    )
    named = ids.shape[1]
    per_query = 1 + negatives.shape[1]
    aux = jnp.concatenate(
        [(ids // 256).astype(f32), (ids % 256).astype(f32)]
        + [part[:, None] for part in split_three(slope)],
        axis=1,
    )
    aux = jnp.pad(aux, ((0, 0), (0, AUX - aux.shape[1])))
    message = own_first(jnp.concatenate([q_unit, aux], axis=1).astype(bf16))
    q_z = to_all(message, "z").reshape(n_z * q_rows, width + AUX)
    q_all = to_all(q_z, "x").reshape(slots, 2, half, width + AUX)
    q_own = q_all[:, 0, :, :width].reshape(slots * half, width)
    q_other = q_all[:, 1, :, :width].reshape(slots * half, width)

    info = q_all[..., width:].astype(f32)
    high, low = info[..., :named], info[..., named : 2 * named]
    blocks = 256 * slots
    column = (x * n_z + z).astype(f32) * p_rows
    place = high * 256.0 + low
    line = jnp.floor(place / blocks)
    offset = place - line * blocks - column
    place = jnp.where((offset >= 0) & (offset < p_rows), line * p_rows + offset, -1.0)
    passages = n_y * p_rows
    row = jnp.arange(passages).astype(f32)
    positive_places = jnp.concatenate(
        [place[..., 0].reshape(-1)]
        + [place[..., k].reshape(-1) for k in range(per_query, named)]
    )
    count = jnp.sum((positive_places[:, None] == row[None, :]).astype(f32), axis=0)
    place_own = place[:, 0].reshape(slots * half, named)
    base = 2 * named
    slope_own = (info[:, 0, :, base] + info[:, 0, :, base + 1]) + info[:, 0, :, base + 2]
    slope_own = slope_own.reshape(slots * half)

    score_other = contract(q_other, p_all, ((1,), (1,)))
    score_own = contract(q_own, p_all, ((1,), (1,)))
    scores = (score_own + shifted(score_other, "mp", 1)) / sharpness_divisor
    match = place_own[:, :1] == row[None, :]
    weight = count[None, :] + sum(
        (place_own[:, k : k + 1] == row[None, :]).astype(f32) for k in range(1, per_query)
    )
    weighted = weight * jnp.exp(scores)
    sums = jnp.concatenate(
        [jnp.sum(weighted, axis=1), jnp.sum(jnp.where(match, scores, 0.0), axis=1)]
    ).reshape(-1, 128)
    sums = jnp.sum(to_all(sums, ("x", "z")).reshape((slots,) + sums.shape), axis=0)
    sums = sums.reshape(2, slots, half)
    own_sums = lax.dynamic_index_in_dim(sums, x * n_z + z, 1, keepdims=False)
    own_loss = jnp.log(own_sums[0]) - own_sums[1]
    losses = own_first(jnp.concatenate([own_loss, shifted(own_loss, "mp", 1)]))
    total = sums[0].reshape(slots * half)

    grad_own = (
        (slope_own / sharpness_divisor)[:, None]
        * (weighted / total[:, None] - match.astype(f32))
    ).astype(bf16)
    grad_other = shifted(grad_own, "mp", 1)

    p_part = (
        contract(grad_own, q_own, ((0,), (0,))) + contract(grad_other, q_other, ((0,), (0,)))
    ).astype(bf16)
    p_grad = lax.psum_scatter(p_part, "y", scatter_dimension=0, tiled=True).astype(f32)
    q_part = jnp.stack(
        [
            contract(grad_own, p_all, ((1,), (0,))).astype(bf16).reshape(slots, half, width),
            contract(grad_other, p_all, ((1,), (0,))).astype(bf16).reshape(slots, half, width),
        ],
        axis=1,
    ).reshape(n_x, n_z * q_rows, width)
    q_part = jnp.sum(exchanged(q_part, "x").astype(f32), axis=0).astype(bf16)
    q_part = q_part.reshape(n_z, q_rows, width)
    q_grad = own_first(jnp.sum(exchanged(q_part, "z").astype(f32), axis=0))

    q_radial, p_radial = lax.psum(
        (jnp.sum(q_unit * q_grad, axis=1), jnp.sum(p_unit * p_grad, axis=1)), "mp"
    )
    q_dir = (q_inv * (q_grad - q_unit * q_radial[:, None])).astype(bf16)
    p_dir = (p_inv * (p_grad - p_unit * p_radial[:, None])).astype(bf16)

    def finish(direction):
        other = shifted(direction, "mp", 1)
        both = contract(direction, weight_kept, ((1,), (1,)))
        return (both + contract(other, weight_got, ((1,), (1,)))).astype(bf16)

    return losses, finish(q_dir), finish(p_dir)


def solution(mesh):
    n_dp, n_core = mesh.devices.shape
    n_z = 8 if n_dp == 128 else 2
    n_x = 4 if n_dp == 128 else 2
    grid = Mesh(
        mesh.devices.reshape(n_dp // (n_x * n_z), n_x, n_z, n_core), ("y", "x", "z", "mp")
    )
    dp = ("y", "x", "z")
    placed = (P(dp, None), P(dp, None), P(None, "mp"), P(dp), P(dp, None), P(dp))
    return jax.shard_map(
        per_device,
        mesh=grid,
        in_specs=placed,
        out_specs=(P(dp), P(dp, "mp"), P(dp, "mp")),
        check_vma=False,
    )
```

profile of v0, /device:TPU:1, one launch (start us, length us, event | category | flops | bytes accessed | tf_op | source)
XLA Modules:
  0.0 244.9 jit_solution(2020458893245613160)
XLA Ops:
  9.4 2.6 %collective-permute-start.1 = (s32[32]{0:T(128)}, s32[32]{0:T(128)S(1)}, u32[]{:S(2)}, u32[]{:S(2)}) collective-permute-start(s32[32]{0:T(128)} %param.9), channel_id=1, source_target_pairs={{0,128},{64,192},{128,0},{192,64},{1,129},{65,193},{129,1},{193,65... | collective-permute-start | bytes 392 | tf_op jit(solution)/shard_map/ppermute | solution.py:14
  13.1 5.1 %multiply_reduce_fusion.2 = (f32[32]{0:T(128)S(1)}, f32[32,1024]{1,0:T(8,128)S(1)}) fusion(bf16[32,4096]{1,0:T(8,128)(2,1)} %param.6, bf16[4096,1024]{1,0:T(8,128)(2,1)} %param.8), kind=kOutput, calls=%fused_computation.49 | convolution fusion | flops 268500960 | bytes 8781952 | tf_op jit(solution)/shard_map/dot_general | solution.py:34
  20.8 3.8 %all-reduce.2 = (f32[32]{0:T(128)S(1)}, f32[256]{0:T(256)S(1)}) all-reduce(f32[32]{0:T(128)S(1)} %get-tuple-element.34, f32[256]{0:T(256)S(1)} %get-tuple-element.36), channel_id=1, replica_groups=mesh['y'=4,'x'=4,'z'=8,'mp'=2] {'mp'}, use_global_device_ids=true, to_apply=%region_1.0 | all-reduce | flops 288 | bytes 2304 | tf_op jit(solution)/shard_map/psum | solution.py:56
  26.8 26.4 %all_to_all.25 = bf16[8,32,1152]{2,1,0:T(8,128)(2,1)S(1)} all-to-all(bf16[8,32,1152]{2,1,0:T(8,128)(2,1)S(1)} %broadcast_in_dim.74), channel_id=1, replica_groups=mesh['y'=4,'x'=4,'z'=8,'mp'=2] {'z'}, dimensions={0} | all-to-all | bytes 1179648 | tf_op jit(solution)/shard_map/all_to_all | solution.py:18
  53.4 31.3 %all_to_all.26 = bf16[4,256,1152]{2,1,0:T(8,128)(2,1)S(1)} all-to-all(bf16[4,256,1152]{2,1,0:T(8,128)(2,1)S(1)} %broadcast_in_dim.76), channel_id=1, replica_groups=mesh['y'=4,'x'=4,'z'=8,'mp'=2] {'x'}, dimensions={0} | all-to-all | bytes 4718592 | tf_op jit(solution)/shard_map/all_to_all | solution.py:18
  87.3 4.6 %fusion.38 = f32[512,1024]{1,0:T(8,128)} fusion(bf16[512,1024]{1,0:T(8,128)(2,1)S(1)} %bitcast.64, bf16[1024,1024]{1,0:T(8,128)(2,1)} %all-gather.2.cloned.1.call-done), kind=kOutput, calls=%fused_computation.93 | convolution fusion | flops 1073741824 | bytes 5242880 | tf_op jit(solution)/shard_map/dot_general | solution.py:34
  91.9 2.6 %collective-permute-start.3 = (f32[512,1024]{1,0:T(8,128)}, f32[512,1024]{1,0:T(8,128)}, u32[]{:S(2)}, u32[]{:S(2)}) collective-permute-start(f32[512,1024]{1,0:T(8,128)} %fusion.38), channel_id=1, source_target_pairs={{0,1},{1,0},{2,3},{3,2},{4,5},{5,4},{6,7},{7,6},{8,9},{9,8},{10,11... | collective-permute-start | bytes 6291464 | tf_op jit(solution)/shard_map/ppermute | solution.py:14
  118.2 6.7 %fusion.33 = (f32[512]{0:T(512)S(1)}, f32[512,1024]{1,0:T(8,128)}, f32[512]{0:T(512)S(1)}) fusion(f32[512]{0:T(512)} %bitcast.74, f32[512]{0:T(512)} %bitcast.75, f32[512]{0:T(512)} %bitcast.76, f32[512]{0:T(512)} %bitcast.77, f32[512]{0:T(512)} %bitcast.78, f32[512]{0:T(512)} %bitcast.79, f32[512]{0:T(512)} %bitcast.80, f32[1024]{0:T(1024)S(1)} %iota_convert_fusion, ...), kind=kOutput, calls=%fused_computation.88 | convolution fusion | flops 1089993728 | bytes 7370752 | tf_op jit(solution)/shard_map/dot_general | solution.py:34
  125.6 3.9 %all-to-all-start.2 = ((f32[32,8,128]{2,1,0:T(8,128)}), f32[32,8,128]{2,1,0:T(8,128)S(1)}, u32[]{:S(2)}, u32[]{:S(2)}) async-start(f32[32,8,128]{2,1,0:T(8,128)} %broadcast_in_dim.79), calls=%async_computation.2 | async-start | bytes 262144 | tf_op jit(solution)/shard_map/all_to_all | solution.py:18
  129.9 8.8 %all-to-all-done.2 = f32[32,8,128]{2,1,0:T(8,128)S(1)} async-done(((f32[32,8,128]{2,1,0:T(8,128)}), f32[32,8,128]{2,1,0:T(8,128)S(1)}, u32[]{:S(2)}, u32[]{:S(2)}) %all-to-all-start.2) | async-done | bytes 131104 | tf_op jit(solution)/shard_map/all_to_all | solution.py:18
  145.7 4.0 %add_convert_fusion = bf16[1024,1024]{1,0:T(8,128)(2,1)} fusion(f32[1024,1024]{1,0:T(8,128)S(1)} %fusion.39, bf16[512,1024]{1,0:T(8,128)(2,1)} %collective-permute-done.5, bf16[512,1024]{1,0:T(8,128)(2,1)S(1)} %bitcast.65), kind=kOutput, calls=%fused_computation.1 | convolution fusion | flops 1075838976 | bytes 8388608 | tf_op jit(solution)/shard_map/dot_general | solution.py:34
  149.7 3.0 %convolution_convert_fusion.1 = bf16[512,1024]{1,0:T(8,128)(2,1)S(1)} fusion(bf16[512,1024]{1,0:T(8,128)(2,1)S(1)} %fusion.9, bf16[1024,1024]{1,0:T(8,128)(2,1)} %all-gather.2.cloned.1.call-done), kind=kOutput, calls=%fused_computation.20 | convolution fusion | flops 1074266112 | bytes 4194304 | tf_op jit(solution)/shard_map/dot_general | solution.py:34
  152.7 2.6 %convolution_convert_fusion = bf16[512,1024]{1,0:T(8,128)(2,1)S(1)} fusion(bf16[512,1024]{1,0:T(8,128)(2,1)} %collective-permute-done.5, bf16[1024,1024]{1,0:T(8,128)(2,1)S(1)} %copy-done.10), kind=kOutput, calls=%fused_computation.19 | convolution fusion | flops 1074266112 | bytes 4194304 | tf_op jit(solution)/shard_map/dot_general | solution.py:34
  156.9 4.5 %all-to-all-start.3 = ((bf16[4,256,1024]{2,1,0:T(8,128)(2,1)}), bf16[4,256,1024]{2,1,0:T(8,128)(2,1)}, u32[]{:S(2)}, u32[]{:S(2)}) async-start(bf16[4,256,1024]{2,1,0:T(8,128)(2,1)} %bitcast.63), calls=%async_computation.3 | async-start | bytes 4194304 | tf_op jit(solution)/shard_map/all_to_all | solution.py:18
  161.4 4.6 %constant_dynamic-slice_fusion.1 = bf16[2048,1024]{1,0:T(8,128)(2,1)} fusion(bf16[4096,1024]{1,0:T(8,128)(2,1)} %param.8, s32[]{:T(128)S(6)} %select_n.70), kind=kLoop, calls=%fused_computation.72 | loop fusion | bytes 8388612 | tf_op jit(solution)/shard_map/dynamic_slice | solution.py:50
  166.0 21.9 %all-to-all-done.3 = bf16[4,256,1024]{2,1,0:T(8,128)(2,1)} async-done(((bf16[4,256,1024]{2,1,0:T(8,128)(2,1)}), bf16[4,256,1024]{2,1,0:T(8,128)(2,1)}, u32[]{:S(2)}, u32[]{:S(2)}) %all-to-all-start.3) | async-done | bytes 2097184 | tf_op jit(solution)/shard_map/all_to_all | solution.py:18
  187.9 2.9 %reduce_sum.99 = bf16[256,1024]{1,0:T(8,128)(2,1)} reduce(bf16[4,256,1024]{2,1,0:T(8,128)(2,1)} %all-to-all-done.3, bf16[]{:T(256)} %constant.66.clone.1), dimensions={0}, to_apply=%region_8.9 | reduce | flops 786432 | bytes 2621442 | tf_op jit(solution)/shard_map/reduce_sum | solution.py:138
  190.8 4.1 %all-to-all-start.4 = ((bf16[8,32,1024]{2,1,0:T(8,128)(2,1)}), bf16[8,32,1024]{2,1,0:T(8,128)(2,1)}, u32[]{:S(2)}, u32[]{:S(2)}) async-start(bf16[8,32,1024]{2,1,0:T(8,128)(2,1)} %bitcast.69), calls=%async_computation.4 | async-start | bytes 1048576 | tf_op jit(solution)/shard_map/all_to_all | solution.py:18
  197.3 15.5 %all-to-all-done.4 = bf16[8,32,1024]{2,1,0:T(8,128)(2,1)} async-done(((bf16[8,32,1024]{2,1,0:T(8,128)(2,1)}), bf16[8,32,1024]{2,1,0:T(8,128)(2,1)}, u32[]{:S(2)}, u32[]{:S(2)}) %all-to-all-start.4) | async-done | bytes 524320 | tf_op jit(solution)/shard_map/all_to_all | solution.py:18
  216.1 3.3 %all-reduce.1 = (f32[32]{0:T(128)}, f32[256]{0:T(256)S(1)}) all-reduce(f32[32]{0:T(128)} %multiply_reduce_fusion.1, f32[256]{0:T(256)S(1)} %fusion.10), channel_id=1, replica_groups=mesh['y'=4,'x'=4,'z'=8,'mp'=2] {'mp'}, use_global_device_ids=true, to_apply=%region_11.12 | all-reduce | flops 288 | bytes 2304 | tf_op jit(solution)/shard_map/psum | solution.py:142
  222.3 3.5 %fusion = f32[256,2048]{1,0:T(8,128)S(1)} fusion(bf16[256,1024]{1,0:T(8,128)(2,1)S(1)} %fusion.12, bf16[4096,1024]{1,0:T(8,128)(2,1)} %param.8, s32[]{:T(128)S(6)} %select_n.69), kind=kOutput, calls=%fused_computation.2 | convolution fusion | flops 1073741824 | bytes 6815748 | tf_op jit(solution)/shard_map/dot_general | solution.py:34
  225.8 3.5 %fusion.2 = f32[32,2048]{1,0:T(8,128)S(1)} fusion(bf16[32,1024]{1,0:T(8,128)(2,1)S(1)} %multiply_convert_fusion.1, bf16[4096,1024]{1,0:T(8,128)(2,1)} %param.8, s32[]{:T(128)S(6)} %select_n.69), kind=kOutput, calls=%fused_computation.4 | convolution fusion | flops 134217728 | bytes 4521988 | tf_op jit(solution)/shard_map/dot_general | solution.py:34
  229.4 4.2 %fusion.5 = bf16[32,2048]{1,0:T(8,128)(2,1)} fusion(f32[32,2048]{1,0:T(8,128)S(1)} %fusion.2, bf16[32,1024]{1,0:T(8,128)(2,1)S(1)} %collective-permute-done.6, bf16[2048,1024]{1,0:T(8,128)(2,1)} %collective-permute-done.7), kind=kOutput, calls=%fused_computation.11 | convolution fusion | flops 134348800 | bytes 4653056 | tf_op jit(solution)/shard_map/dot_general | solution.py:34
  233.6 4.4 %fusion.4 = bf16[256,2048]{1,0:T(8,128)(2,1)} fusion(f32[256,2048]{1,0:T(8,128)S(1)} %fusion, bf16[256,1024]{1,0:T(8,128)(2,1)S(1)} %collective-permute-done.8, bf16[2048,1024]{1,0:T(8,128)(2,1)} %collective-permute-done.7), kind=kOutput, calls=%fused_computation.9 | convolution fusion | flops 1074790400 | bytes 7864320 | tf_op jit(solution)/shard_map/dot_general | solution.py:34
  (106 shorter events, 52.6 us)
Async XLA Ops:
  7.2 11.1 %copy-start = (bf16[256,4096]{1,0:T(8,128)(2,1)S(1)}, bf16[256,4096]{1,0:T(8,128)(2,1)}, u32[]{:S(2)}) copy-start(bf16[256,4096]{1,0:T(8,128)(2,1)} %param.7) | copy-start | bytes 6291460
  7.2 80.2 %all-gather.2.cloned.1.call-start = ((), (), s32[]{:S(2)}) async-start(), calls=%async_computation.6 | async-start | bytes 2621440 | tf_op jit(solution)/shard_map/all_gather | solution.py:64
  7.2 11.1 %copy-start.1 = (bf16[4096,1024]{1,0:T(8,128)(2,1)S(1)}, bf16[4096,1024]{1,0:T(8,128)(2,1)}, u32[]{:S(2)}) copy-start(bf16[4096,1024]{1,0:T(8,128)(2,1)} %param.8) | copy-start | bytes 25165828
  7.2 18.9 %collective-permute-start = (s32[32]{0:T(128)}, s32[32]{0:T(128)S(1)}, u32[]{:S(2)}, u32[]{:S(2)}) collective-permute-start(s32[32]{0:T(128)} %param.9), channel_id=1, source_target_pairs={{0,64},{64,128},{128,192},{192,0},{1,65},{65,129},{129,193},{193,1... | collective-permute-start | bytes 392 | tf_op jit(solution)/shard_map/ppermute | solution.py:14
  9.4 16.8 %collective-permute-start.1 = (s32[32]{0:T(128)}, s32[32]{0:T(128)S(1)}, u32[]{:S(2)}, u32[]{:S(2)}) collective-permute-start(s32[32]{0:T(128)} %param.9), channel_id=1, source_target_pairs={{0,128},{64,192},{128,0},{192,64},{1,129},{65,193},{129,1},{193,65... | collective-permute-start | bytes 392 | tf_op jit(solution)/shard_map/ppermute | solution.py:14
  12.1 14.3 %collective-permute-start.2 = (s32[32]{0:T(128)}, s32[32]{0:T(128)S(1)}, u32[]{:S(2)}, u32[]{:S(2)}) collective-permute-start(s32[32]{0:T(128)} %param.9), channel_id=1, source_target_pairs={{0,192},{64,0},{128,64},{192,128},{1,193},{65,1},{129,65},{193,129... | collective-permute-start | bytes 392 | tf_op jit(solution)/shard_map/ppermute | solution.py:14
  20.8 32.4 %copy-start.2 = (f32[256,1024]{1,0:T(8,128)}, f32[256,1024]{1,0:T(8,128)S(1)}, u32[]{:S(2)}) copy-start(f32[256,1024]{1,0:T(8,128)S(1)} %get-tuple-element.37) | copy-start | bytes 3145732
  20.8 4.8 %copy-start.8 = (s32[32]{0:T(128)S(1)}, s32[32]{0:T(128)}, u32[]{:S(2)}) copy-start(s32[32]{0:T(128)} %param.9) | copy-start | bytes 388
  20.8 4.9 %copy-start.7 = (s32[32,8]{0,1:T(8,128)S(1)}, s32[32,8]{0,1:T(8,128)}, u32[]{:S(2)}) copy-start(s32[32,8]{0,1:T(8,128)} %param.10) | copy-start | bytes 3076
  20.8 4.9 %copy-start.9 = (f32[32]{0:T(128)S(1)}, f32[32]{0:T(128)}, u32[]{:S(2)}) copy-start(f32[32]{0:T(128)} %param.11) | copy-start | bytes 388
  87.3 4.6 %copy-start.5 = (bf16[32,1,16,1024]{3,2,1,0:T(8,128)(2,1)}, bf16[32,1,16,1024]{3,2,1,0:T(8,128)(2,1)S(1)}, u32[]{:S(2)}) copy-start(bf16[32,1,16,1024]{3,2,1,0:T(8,128)(2,1)S(1)} %get-tuple-element.14) | copy-start | bytes 3145732
  91.9 26.2 %collective-permute-start.3 = (f32[512,1024]{1,0:T(8,128)}, f32[512,1024]{1,0:T(8,128)}, u32[]{:S(2)}, u32[]{:S(2)}) collective-permute-start(f32[512,1024]{1,0:T(8,128)} %fusion.38), channel_id=1, source_target_pairs={{0,1},{1,0},{2,3},{3,2},{4,5},{5,4},{6,7},{7,6},{8,9},{9,8},{10,11... | collective-permute-start | bytes 6291464 | tf_op jit(solution)/shard_map/ppermute | solution.py:14
  125.6 13.2 %all-to-all-start.2 = ((f32[32,8,128]{2,1,0:T(8,128)}), f32[32,8,128]{2,1,0:T(8,128)S(1)}, u32[]{:S(2)}, u32[]{:S(2)}) async-start(f32[32,8,128]{2,1,0:T(8,128)} %broadcast_in_dim.79), calls=%async_computation.2 | async-start | bytes 262144 | tf_op jit(solution)/shard_map/all_to_all | solution.py:18
  129.4 85.3 %reduce-scatter.2.cloned.1.call-start = ((), (), s32[]{:S(2)}) async-start(), calls=%async_computation.7 | async-start | bytes 2621440 | tf_op jit(solution)/shard_map/reduce_scatter | solution.py:130
  140.8 4.8 %collective-permute-start.5 = (bf16[512,1024]{1,0:T(8,128)(2,1)S(1)}, bf16[512,1024]{1,0:T(8,128)(2,1)}, u32[]{:S(2)}, u32[]{:S(2)}) collective-permute-start(bf16[512,1024]{1,0:T(8,128)(2,1)S(1)} %fusion.9), channel_id=1, source_target_pairs={{0,1},{1,0},{2,3},{3,2},{4,5},{5,4},{6,7},{7,6},{8,9},{9,8},{10,11... | collective-permute-start | bytes 3145736 | tf_op jit(solution)/shard_map/ppermute | solution.py:14
  143.0 2.6 %copy-start.6 = (bf16[32,1,16,1024]{3,2,1,0:T(8,128)(2,1)S(1)}, bf16[32,1,16,1024]{3,2,1,0:T(8,128)(2,1)}, u32[]{:S(2)}) copy-start(bf16[32,1,16,1024]{3,2,1,0:T(8,128)(2,1)} %copy-done.5) | copy-start | bytes 3145732
  149.7 3.0 %copy-start.10 = (bf16[1024,1024]{1,0:T(8,128)(2,1)S(1)}, bf16[1024,1024]{1,0:T(8,128)(2,1)}, u32[]{:S(2)}) copy-start(bf16[1024,1024]{1,0:T(8,128)(2,1)} %all-gather.2.cloned.1.call-done) | copy-start | bytes 6291460
  156.9 31.0 %all-to-all-start.3 = ((bf16[4,256,1024]{2,1,0:T(8,128)(2,1)}), bf16[4,256,1024]{2,1,0:T(8,128)(2,1)}, u32[]{:S(2)}, u32[]{:S(2)}) async-start(bf16[4,256,1024]{2,1,0:T(8,128)(2,1)} %bitcast.63), calls=%async_computation.3 | async-start | bytes 4194304 | tf_op jit(solution)/shard_map/all_to_all | solution.py:18
  166.0 48.8 %copy-start.3 = (f32[256,1024]{1,0:T(8,128)S(1)}, f32[256,1024]{1,0:T(8,128)}, u32[]{:S(2)}) copy-start(f32[256,1024]{1,0:T(8,128)} %copy-done.2) | copy-start | bytes 3145732
  166.0 63.4 %collective-permute-start.7 = (bf16[2048,1024]{1,0:T(8,128)(2,1)}, bf16[2048,1024]{1,0:T(8,128)(2,1)}, u32[]{:S(2)}, u32[]{:S(2)}) collective-permute-start(bf16[2048,1024]{1,0:T(8,128)(2,1)} %constant_dynamic-slice_fusion.1), channel_id=1, source_target_pairs={{0,1},{1,0},{2,3},{3,2},{4,5},{5,4},{6,7},{7,6},{8,9},{9,8},{10,11... | collective-permute-start | bytes 12582920 | tf_op jit(solution)/shard_map/ppermute | solution.py:14
  190.8 22.1 %all-to-all-start.4 = ((bf16[8,32,1024]{2,1,0:T(8,128)(2,1)}), bf16[8,32,1024]{2,1,0:T(8,128)(2,1)}, u32[]{:S(2)}, u32[]{:S(2)}) async-start(bf16[8,32,1024]{2,1,0:T(8,128)(2,1)} %bitcast.69), calls=%async_computation.4 | async-start | bytes 1048576 | tf_op jit(solution)/shard_map/all_to_all | solution.py:18
  195.0 1.7 collective-permute-start.4
  220.1 9.3 %collective-permute-start.6 = (bf16[32,1024]{1,0:T(8,128)(2,1)S(1)}, bf16[32,1024]{1,0:T(8,128)(2,1)S(1)}, u32[]{:S(2)}, u32[]{:S(2)}) collective-permute-start(bf16[32,1024]{1,0:T(8,128)(2,1)S(1)} %multiply_convert_fusion.1), channel_id=1, source_target_pairs={{0,1},{1,0},{2,3},{3,2},{4,5},{5,4},{6,7},{7,6},{8,9},{9,8},{10,11... | collective-permute-start | bytes 196616 | tf_op jit(solution)/shard_map/ppermute | solution.py:14
  221.8 11.8 %collective-permute-start.8 = (bf16[256,1024]{1,0:T(8,128)(2,1)S(1)}, bf16[256,1024]{1,0:T(8,128)(2,1)S(1)}, u32[]{:S(2)}, u32[]{:S(2)}) collective-permute-start(bf16[256,1024]{1,0:T(8,128)(2,1)S(1)} %fusion.12), channel_id=1, source_target_pairs={{0,1},{1,0},{2,3},{3,2},{4,5},{5,4},{6,7},{7,6},{8,9},{9,8},{10,11... | collective-permute-start | bytes 1572872 | tf_op jit(solution)/shard_map/ppermute | solution.py:14
  (1 other events, 1.4 us)
Sparse Core Ops, SparseCore 0:
  25.7 33.5 all-gather.1
  149.8 24.7 reduce-scatter.1
where the time goes:
time: 246 us; the launch traced here: 245 us
  blocking collectives  64.7 us (26%)
  waiting for transfers between devices  47.1 us (19%)
  matrix products  46.8 us (19%)
  local copies, waits for them, and re-layouts  29.8 us (12%)
  starting transfers between devices  25.2 us (10%)
  other arithmetic  16.8 us (7%)
  between operations  14.4 us (6%)
    all_to_all x2, blocking collectives, exchanged(): return lax.all_to_all(parts, axis, split_axis=0, concat_axis=0, tiled=True)  57.7 us
    dot_general x12, matrix products, contract(): return lax.dot_general(a, b, (dims, ((), ())), preferred_element_type=f32)  46.8 us
    all_to_all x3, waiting for transfers between devices, exchanged(): return lax.all_to_all(parts, axis, split_axis=0, concat_axis=0, tiled=True)  46.2 us
    unnamed x32, local copies, waits for them, and re-layouts  14.8 us
    ppermute x9, starting transfers between devices, shifted(): return lax.ppermute(value, axis, [(i, (i + shift) % n) for i in range(n)])  12.6 us
    all_to_all x3, starting transfers between devices, exchanged(): return lax.all_to_all(parts, axis, split_axis=0, concat_axis=0, tiled=True)  12.5 us
  transfers between devices with their start and end apart: 14, of which 4 were waited for; matrix products, arithmetic and copies ran while one was open for 28% of the time, Pallas kernels for 0%

commit v1 on v0

v1 whole, which is shorter than its diff:
```python
import jax
import jax.numpy as jnp
from jax import lax
from jax.experimental import pallas as pl
from jax.experimental.pallas import tpu as pltpu
from jax.sharding import Mesh, PartitionSpec as P

sharpness = 1.0 / 0.02
bf16 = jnp.bfloat16
f32 = jnp.float32
AUX = 128
TILE = 256
VMEM_LIMIT = 40 * 1024 * 1024


def shifted(value, axis, shift):
    n = lax.axis_size(axis)
    return lax.ppermute(value, axis, [(i, (i + shift) % n) for i in range(n)])


def exchanged(parts, axis):
    return lax.all_to_all(parts, axis, split_axis=0, concat_axis=0, tiled=True)


def to_all(value, axis):
    n = lax.axis_size(axis)
    return exchanged(jnp.broadcast_to(value[None], (n,) + value.shape), axis)


def split_three(value):
    high = lax.reduce_precision(value, 8, 7)
    rest = value - high
    middle = lax.reduce_precision(rest, 8, 7)
    return high, middle, rest - middle


def contract(a, b, dims):
    return lax.dot_general(a, b, (dims, ((), ())), preferred_element_type=f32)


def whole(*shape):
    return pl.BlockSpec(shape, lambda j, meta: (0,) * len(shape))


def struct(shape, dtype=f32):
    return jax.ShapeDtypeStruct(shape, dtype)


def call(body, meta, steps, in_specs, out_specs, out_shape, args, scratch=(), flops=0):
    return pl.pallas_call(
        body,
        grid_spec=pltpu.PrefetchScalarGridSpec(
            num_scalar_prefetch=1,
            grid=(steps,),
            in_specs=in_specs,
            out_specs=out_specs,
            scratch_shapes=list(scratch),
        ),
        out_shape=out_shape,
        compiler_params=pltpu.CompilerParams(
            dimension_semantics=("arbitrary",), vmem_limit_bytes=VMEM_LIMIT
        ),
        cost_estimate=pl.CostEstimate(flops=flops, bytes_accessed=0, transcendentals=0),
    )(meta, *args)


def row_of_lane_sums(block):
    return jnp.sum(block.T, axis=0, keepdims=True)


def lanes_to_rows(row):
    return jnp.broadcast_to(row, (128, row.shape[1])).T


def project_body(meta, q_ref, p_ref, w_ref, qo_ref, po_ref, square_ref, x_ref, acc_ref):
    step = pl.program_id(0)
    n_q = q_ref.shape[0]

    @pl.when(step == 0)
    def _():
        x_ref[:n_q] = q_ref[...]
        x_ref[n_q:] = p_ref[...]
        acc_ref[...] = jnp.zeros_like(acc_ref)

    proj = contract(x_ref[...], w_ref[...], ((1,), (0,)))
    qo_ref[...] = proj[:n_q]
    po_ref[...] = proj[n_q:]
    square = proj * proj
    acc_ref[...] += square[:, :128] + square[:, 128:]

    @pl.when(step == pl.num_programs(0) - 1)
    def _():
        padded = jnp.concatenate([acc_ref[:n_q], jnp.zeros((128 - n_q, 128), f32)], axis=0)
        square_ref[:, :128] = row_of_lane_sums(padded)
        square_ref[:, 128:] = row_of_lane_sums(acc_ref[n_q:])


def project(meta, queries, passages, weight):
    n_q, n_p, (depth, width) = queries.shape[0], passages.shape[0], weight.shape
    column = lambda rows: pl.BlockSpec((rows, TILE), lambda j, meta: (0, j))
    return call(
        project_body,
        meta,
        width // TILE,
        [whole(n_q, depth), whole(n_p, depth), column(depth)],
        [column(n_q), column(n_p), whole(1, 128 + n_p)],
        [struct((n_q, width)), struct((n_p, width)), struct((1, 128 + n_p))],
        (queries, passages, weight),
        [pltpu.VMEM((n_q + n_p, depth), bf16), pltpu.VMEM((n_q + n_p, 128), f32)],
        2 * (n_q + n_p) * depth * width,
    )


def normalize_body(
    meta, q_ref, p_ref, own_ref, got_ref, aux_ref, message_ref, qu_ref, pu_ref, pe_ref, qi_ref, pi_ref
):
    n_q, width = q_ref.shape
    inv = lanes_to_rows(lax.rsqrt(own_ref[...] + got_ref[...] + 1e-06))
    q_inv, p_inv = inv[:n_q], inv[128:]
    qi_ref[...] = q_inv
    pi_ref[...] = p_inv
    q_unit = q_ref[...] * q_inv[:, :1]
    p_unit = p_ref[...] * p_inv[:, :1]
    qu_ref[...] = q_unit
    pu_ref[...] = p_unit
    pe_ref[...] = p_unit.astype(bf16)
    half = n_q // 2
    first = meta[0] == 0

    def store(columns, value):
        top, bottom = value[:half], value[half:]
        message_ref[:half, columns] = jnp.where(first, top, bottom).astype(bf16)
        message_ref[half:, columns] = jnp.where(first, bottom, top).astype(bf16)

    store(slice(0, width), q_unit)
    store(slice(width, width + AUX), aux_ref[...])


def normalize(meta, q_proj, p_proj, square, square_got, aux):
    (n_q, width), n_p = q_proj.shape, p_proj.shape[0]
    shapes = [
        struct((n_q, width + AUX), bf16),
        struct((n_q, width)),
        struct((n_p, width)),
        struct((n_p, width), bf16),
        struct((n_q, 128)),
        struct((n_p, 128)),
    ]
    args = (q_proj, p_proj, square, square_got, aux)
    return call(
        normalize_body,
        meta,
        1,
        [whole(*a.shape) for a in args],
        [whole(*s.shape) for s in shapes],
        shapes,
        args,
    )


def flat(block):
    return block.reshape(-1, block.shape[-1])


def score_sent_body(meta, q_ref, p_ref, score_ref):
    width = p_ref.shape[1]
    score_ref[...] = contract(flat(q_ref[:, 0, :, :width]), p_ref[...], ((1,), (1,)))


def score_sent(meta, q_all, p_all, n_y):
    slots, _, half, full = q_all.shape
    passages, width = p_all.shape
    rows, block = slots * half, passages // n_y
    return call(
        score_sent_body,
        meta,
        n_y,
        [
            pl.BlockSpec((slots, 1, half, full), lambda j, meta: (0, 1, 0, 0)),
            pl.BlockSpec((block, width), lambda j, meta: (j, 0)),
        ],
        pl.BlockSpec((rows, block), lambda j, meta: (0, j)),
        struct((rows, passages)),
        (q_all, p_all),
        flops=2 * rows * passages * width,
    )


def places(info, step, meta, slots, named):
    owner = (step * slots + meta[1]).astype(f32)
    return jnp.where(info == owner, pltpu.roll(info, AUX - named, 1), -1.0)


def score_kept_body(per_query, named, meta, q_ref, p_ref, score_ref, weight_ref, info_ref, place_ref):
    step = pl.program_id(0)
    slots, _, half, full = q_ref.shape
    block, width = p_ref.shape
    rows = slots * half
    score_ref[...] = contract(flat(q_ref[:, 0, :, :width]), p_ref[...], ((1,), (1,)))
    info = flat(q_ref[:, 0, :, width:]).astype(f32)
    info_ref[...] = info
    place_ref[:rows] = places(info, step, meta, slots, named)
    place_ref[rows:] = places(flat(q_ref[:, 1, :, width:]).astype(f32), step, meta, slots, named)
    chunk = 32
    column = lax.broadcasted_iota(jnp.int32, (chunk, block), 1).astype(f32)

    def hits(start, columns):
        place = place_ref[pl.ds(pl.multiple_of(start, chunk), chunk), :]
        return sum((place[:, k : k + 1] == column).astype(f32) for k in columns)

    def add(i, total):
        return total + hits(i * chunk, [0] + list(range(per_query, named)))

    total = lax.fori_loop(0, 2 * rows // chunk, add, jnp.zeros((chunk, block), f32))
    count = jnp.sum(total, axis=0, keepdims=True)

    def put(i, carry):
        at = pl.ds(pl.multiple_of(i * chunk, chunk), chunk)
        weight_ref[at, :] = hits(i * chunk, range(1, per_query)) + count
        return carry

    lax.fori_loop(0, rows // chunk, put, 0)


def score_kept(meta, q_all, p_all, n_y, per_query, named):
    slots, _, half, full = q_all.shape
    passages, width = p_all.shape
    rows, block = slots * half, passages // n_y
    out = pl.BlockSpec((rows, block), lambda j, meta: (0, j))

    def body(*refs):
        score_kept_body(per_query, named, *refs)

    return call(
        body,
        meta,
        n_y,
        [
            whole(slots, 2, half, full),
            pl.BlockSpec((block, width), lambda j, meta: (j, 0)),
        ],
        [out, out, whole(rows, AUX)],
        [struct((rows, passages)), struct((rows, passages)), struct((rows, AUX))],
        (q_all, p_all),
        [pltpu.VMEM((2 * rows, AUX), f32)],
        4 * rows * passages * width,
    )


def matches(info, step, meta, slots, named, block):
    place = places(info, step, meta, slots, named)
    column = lax.broadcasted_iota(jnp.int32, (info.shape[0], block), 1).astype(f32)
    return place[:, :1] == column


def weigh_body(slots, named, meta, kept_ref, got_ref, weight_ref, info_ref, e_ref, sum_ref, acc_ref):
    step = pl.program_id(0)

    @pl.when(step == 0)
    def _():
        acc_ref[...] = jnp.zeros_like(acc_ref)

    score = (kept_ref[...] + got_ref[...]) * sharpness
    weighted = weight_ref[...] * jnp.exp(score)
    e_ref[...] = weighted
    match = matches(info_ref[...], step, meta, slots, named, score.shape[1])
    own = jnp.where(match, score, 0.0)
    acc_ref[0] += weighted[:, :128] + weighted[:, 128:]
    acc_ref[1] += own[:, :128] + own[:, 128:]

    @pl.when(step == pl.num_programs(0) - 1)
    def _():
        sum_ref[0:1] = row_of_lane_sums(acc_ref[0])
        sum_ref[1:2] = row_of_lane_sums(acc_ref[1])


def weigh(meta, kept, got, weight, info, n_y, slots, named):
    rows, passages = kept.shape
    block = pl.BlockSpec((rows, passages // n_y), lambda j, meta: (0, j))

    def body(*refs):
        weigh_body(slots, named, *refs)

    return call(
        body,
        meta,
        n_y,
        [block, block, block, whole(rows, AUX)],
        [block, whole(2, rows)],
        [struct((rows, passages)), struct((2, rows))],
        (kept, got, weight, info),
        [pltpu.VMEM((2, rows, 128), f32)],
    )


def slope_body(slots, named, meta, e_ref, sums_ref, info_ref, grad_ref, loss_ref, scale_ref, inv_ref):
    step = pl.program_id(0)

    @pl.when(step == 0)
    def _():
        sums = jnp.sum(sums_ref[...], axis=0)
        total = sums[0:1]
        loss_ref[...] = jnp.log(total) - sums[1:2]
        inv_ref[...] = 1.0 / lanes_to_rows(total)
        base = 2 * named
        info = info_ref[...]
        slope = (info[:, base : base + 1] + info[:, base + 1 : base + 2]) + info[:, base + 2 : base + 3]
        scale_ref[...] = jnp.broadcast_to(slope * sharpness, scale_ref.shape)

    match = matches(info_ref[...], step, meta, slots, named, e_ref.shape[1])
    likelihood = e_ref[...] * inv_ref[:, :1]
    grad_ref[...] = (scale_ref[:, :1] * (likelihood - match.astype(f32))).astype(bf16)


def slopes(meta, e, sums, info, n_y, slots, named):
    rows, passages = e.shape
    block = pl.BlockSpec((rows, passages // n_y), lambda j, meta: (0, j))

    def body(*refs):
        slope_body(slots, named, *refs)

    return call(
        body,
        meta,
        n_y,
        [block, whole(*sums.shape), whole(rows, AUX)],
        [block, whole(1, rows)],
        [struct((rows, passages), bf16), struct((1, rows))],
        (e, sums, info),
        [pltpu.VMEM((rows, 128), f32), pltpu.VMEM((rows, 128), f32)],
    )


def grads_first_body(meta, grad_ref, p_ref, q_ref, qo_ref, po_ref, turned_ref):
    @pl.when(pl.program_id(0) == 0)
    def _():
        turned_ref[...] = grad_ref[...].T

    qo_ref[...] = contract(grad_ref[...], p_ref[...], ((1,), (0,))).astype(bf16)
    po_ref[...] = contract(turned_ref[...], flat(q_ref[:, 0]), ((1,), (0,)))


def grads_first(meta, grad, p_all, q_all):
    rows, passages = grad.shape
    width = p_all.shape[1]
    slots, _, half, _ = q_all.shape
    column = lambda r: pl.BlockSpec((r, TILE), lambda j, meta: (0, j))
    return call(
        grads_first_body,
        meta,
        width // TILE,
        [
            whole(rows, passages),
            column(passages),
            pl.BlockSpec((slots, 1, half, TILE), lambda j, meta: (0, 0, 0, j)),
        ],
        [column(rows), column(passages)],
        [struct((rows, width), bf16), struct((passages, width))],
        (grad, p_all, q_all),
        [pltpu.VMEM((passages, rows), bf16)],
        4 * rows * passages * width,
    )


def grads_second_body(meta, grad_ref, p_ref, q_ref, qi_ref, pi_ref, qo_ref, po_ref, turned_ref):
    @pl.when(pl.program_id(0) == 0)
    def _():
        turned_ref[...] = grad_ref[...].T

    slots, _, half, tile = qo_ref.shape
    po_ref[...] = (
        pi_ref[...] + contract(turned_ref[...], flat(q_ref[:, 0]), ((1,), (0,)))
    ).astype(bf16)
    qo_ref[:, 0] = qi_ref[...].reshape(slots, half, tile)
    second = contract(grad_ref[...], p_ref[...], ((1,), (0,))).astype(bf16)
    qo_ref[:, 1] = second.reshape(slots, half, tile)


def grads_second(meta, grad, p_all, q_all, q_part, p_part):
    rows, passages = grad.shape
    width = p_all.shape[1]
    slots, _, half, _ = q_all.shape
    column = lambda r: pl.BlockSpec((r, TILE), lambda j, meta: (0, j))
    return call(
        grads_second_body,
        meta,
        width // TILE,
        [
            whole(rows, passages),
            column(passages),
            pl.BlockSpec((slots, 1, half, TILE), lambda j, meta: (0, 1, 0, j)),
            column(rows),
            column(passages),
        ],
        [pl.BlockSpec((slots, 2, half, TILE), lambda j, meta: (0, 0, 0, j)), column(passages)],
        [struct((slots, 2, half, width), bf16), struct((passages, width), bf16)],
        (grad, p_all, q_all, q_part, p_part),
        [pltpu.VMEM((passages, rows), bf16)],
        4 * rows * passages * width,
    )


def finish_body(
    meta, qg_ref, qgo_ref, qu_ref, quo_ref, qi_ref, pg_ref, pgo_ref, pu_ref, puo_ref, pi_ref,
    w_ref, wo_ref, q_out, p_out, dir_ref
):
    n_q, width = qg_ref.shape

    @pl.when(pl.program_id(0) == 0)
    def _():
        def tangent(at, grad_ref, grad_other, unit_ref, unit_other, inv_ref):
            grad, other = grad_ref[...].astype(f32), grad_other[...].astype(f32)
            unit, beyond = unit_ref[...], unit_other[...]
            radial = jnp.sum(unit * grad + beyond * other, axis=1, keepdims=True)
            inv = inv_ref[:, :1]
            dir_ref[at, :width] = (inv * (grad - unit * radial)).astype(bf16)
            dir_ref[at, width:] = (inv * (other - beyond * radial)).astype(bf16)

        tangent(slice(0, n_q), qg_ref, qgo_ref, qu_ref, quo_ref, qi_ref)
        tangent(slice(n_q, dir_ref.shape[0]), pg_ref, pgo_ref, pu_ref, puo_ref, pi_ref)

    state = contract(dir_ref[:, :width], w_ref[...], ((1,), (1,)))
    state = (state + contract(dir_ref[:, width:], wo_ref[...], ((1,), (1,)))).astype(bf16)
    q_out[...] = state[:n_q]
    p_out[...] = state[n_q:]


def finish(meta, rows_in, weight, weight_got):
    depth, width = weight.shape
    n_q, n_p = rows_in[0].shape[0], rows_in[5].shape[0]
    tile = min(512, depth // 2)
    steps = depth // 2 // tile
    rows = pl.BlockSpec((tile, width), lambda j, meta: (meta[0] * steps + j, 0))
    column = lambda r: pl.BlockSpec((r, tile), lambda j, meta: (0, j))
    return call(
        finish_body,
        meta,
        steps,
        [whole(*a.shape) for a in rows_in] + [rows, rows],
        [column(n_q), column(n_p)],
        [struct((n_q, depth // 2), bf16), struct((n_p, depth // 2), bf16)],
        (*rows_in, weight, weight_got),
        [pltpu.VMEM((n_q + n_p, 2 * width), bf16)],
        2 * (n_q + n_p) * depth * width,
    )


def per_device(query_states, passage_states, head_weight, positives, negatives, slope):
    n_y, n_x, n_z = (lax.axis_size(a) for a in ("y", "x", "z"))
    x, z, core = (lax.axis_index(a) for a in ("x", "z", "mp"))
    q_rows, p_rows = query_states.shape[0], passage_states.shape[0]
    width = head_weight.shape[1]
    half = q_rows // 2
    slots = n_x * n_z
    column = x * n_z + z
    meta = jnp.stack([core, column]).astype(jnp.int32)

    def own_first(rows):
        return jnp.where(core == 0, rows, jnp.roll(rows, half, axis=0))

    q_proj, p_proj, square = project(meta, query_states, passage_states, head_weight)
    square_got = shifted(square, "mp", 1)
    line_positives = [shifted(positives, "y", s) for s in range(1, n_y)]
    ids = jnp.concatenate(
        [positives[:, None], negatives] + [other[:, None] for other in line_positives], axis=1
    )
    named = ids.shape[1]
    per_query = 1 + negatives.shape[1]
    aux = jnp.concatenate(
        [(ids // p_rows).astype(f32), (ids % p_rows).astype(f32)]
        + [part[:, None] for part in split_three(slope)],
        axis=1,
    )
    aux = jnp.pad(aux, ((0, 0), (0, AUX - aux.shape[1])))
    message, q_unit, p_unit, p_embed, q_inv, p_inv = normalize(
        meta, q_proj, p_proj, square, square_got, aux
    )
    p_all = lax.all_gather(p_embed, "y", axis=0, tiled=True)
    weight_got = shifted(lax.optimization_barrier((head_weight, square_got))[0], "mp", 1)
    q_unit_got, p_unit_got = shifted(q_unit, "mp", 1), shifted(p_unit, "mp", 1)

    q_z = to_all(message, "z").reshape(n_z * q_rows, width + AUX)
    q_all = to_all(q_z, "x").reshape(slots, 2, half, width + AUX)

    sent = score_sent(meta, q_all, p_all, n_y)
    got = shifted(sent, "mp", 1)
    kept, weight, info = score_kept(meta, q_all, p_all, n_y, per_query, named)
    e, sums = weigh(meta, kept, got, weight, info, n_y, slots, named)
    sums = to_all(sums, ("x", "z")).reshape((slots,) + sums.shape)
    grad, loss = slopes(meta, e, sums, info, n_y, slots, named)
    grad_got = shifted(grad, "mp", 1)
    own_loss = lax.dynamic_slice_in_dim(loss[0], column * half, half, 0)
    losses = own_first(jnp.concatenate([own_loss, shifted(own_loss, "mp", 1)]))

    q_part, p_part = grads_first(meta, grad, p_all, q_all)
    q_part, p_part = grads_second(meta, grad_got, p_all, q_all, q_part, p_part)
    p_grad = lax.psum_scatter(p_part, "y", scatter_dimension=0, tiled=True)
    back = exchanged(q_part.reshape(n_x, n_z * q_rows, width), "x")
    q_part = sum(back[s].astype(f32) for s in range(n_x)).astype(bf16)
    back = exchanged(q_part.reshape(n_z, q_rows, width), "z")
    q_grad = own_first(sum(back[s].astype(f32) for s in range(n_z)))

    q_grad_got, p_grad_got = shifted(q_grad, "mp", 1), shifted(p_grad, "mp", 1)
    query_grads, passage_grads = finish(
        meta,
        (q_grad, q_grad_got, q_unit, q_unit_got, q_inv, p_grad, p_grad_got, p_unit, p_unit_got, p_inv),
        head_weight,
        weight_got,
    )
    return losses, query_grads, passage_grads


def solution(mesh):
    n_dp, n_core = mesh.devices.shape
    n_z = 8 if n_dp == 128 else 2
    n_x = 4 if n_dp == 128 else 2
    grid = Mesh(
        mesh.devices.reshape(n_dp // (n_x * n_z), n_x, n_z, n_core), ("y", "x", "z", "mp")
    )
    dp = ("y", "x", "z")
    placed = (P(dp, None), P(dp, None), P(None, "mp"), P(dp), P(dp, None), P(dp))
    return jax.shard_map(
        per_device,
        mesh=grid,
        in_specs=placed,
        out_specs=(P(dp), P(dp, "mp"), P(dp, "mp")),
        check_vma=False,
    )
```

time: 246 us -> 228 us (0.927)
  Pallas kernels: 0 us -> 54.8 us
  matrix products: 46.8 us -> 0 us
  other arithmetic: 16.8 us -> 2 us
  local copies, waits for them, and re-layouts: 29.8 us -> 22.2 us
  waiting for transfers between devices: 47.1 us -> 42.9 us
  blocking collectives: 64.7 us -> 67.7 us
    pallas_call x0 -> x9, Pallas kernels: none -> 54.8 us  [call(): pl.pallas_call(body, grid_spec=pltpu.PrefetchScalarGridSpec(num_scalar_pr...]
    dot_general x12 -> x0, matrix products: 46.8 us -> none  [contract(): return lax.dot_general(a, b, (dims, ((), ())), preferred_element_type=f32)]
    all_to_all x2 -> x3, blocking collectives: 57.7 us -> 67.7 us  [exchanged(): return lax.all_to_all(parts, axis, split_axis=0, concat_axis=0, tiled=True)]
    reduce_sum x6 -> x0, other arithmetic: 7.81 us -> none  [the longest x1 2.92 us: per_device(): q_part = jnp.sum(exchanged(q_part, 'x').astype(f32), axis=0).astype(bf16)]
    psum x2 -> x0, blocking collectives: 7.03 us -> none  [the longest x1 3.77 us: per_device(): lax.psum((jnp.sum(q_proj * q_proj, axis=1), jnp.sum(p_proj * p_proj, axis...]
    convert_element_type x6 -> x1, other arithmetic: 6.01 us -> 0.03 us  [per_device(): (ids % p_rows).astype(f32)]
    slice x4 -> x0, local copies, waits for them, and re-layouts: 5.09 us -> none  [the longest x1 1.94 us: per_device(): place_own[:, k:k + 1] == row[None, :]]
    all_to_all x3 -> x2, starting transfers between devices: 12.5 us -> 7.51 us  [exchanged(): return lax.all_to_all(parts, axis, split_axis=0, concat_axis=0, tiled=True)]
  transfers between devices with their start and end apart: 14 -> 16, of which waited for: 4 -> 3; matrix products, arithmetic and copies ran while one was open for 28% -> 2% of each run, Pallas kernels for 0% -> 20%
where the time goes in v1:
time: 228 us
  blocking collectives  67.7 us (30%)
  Pallas kernels  54.8 us (24%)
  waiting for transfers between devices  42.9 us (19%)
  starting transfers between devices  23.8 us (10%)
  local copies, waits for them, and re-layouts  22.2 us (10%)
  between operations  14.2 us (6%)
    all_to_all x3, blocking collectives, exchanged(): return lax.all_to_all(parts, axis, split_axis=0, concat_axis=0, tiled=True)  67.7 us
    pallas_call x9, Pallas kernels, call(): pl.pallas_call(body, grid_spec=pltpu.PrefetchScalarGridSpec(num_scalar_pr...  54.8 us
    all_to_all x2, waiting for transfers between devices, exchanged(): return lax.all_to_all(parts, axis, split_axis=0, concat_axis=0, tiled=True)  41.9 us
    unnamed x37, local copies, waits for them, and re-layouts  19.6 us
    ppermute x12, starting transfers between devices, shifted(): return lax.ppermute(value, axis, [(i, (i + shift) % n) for i in range(n)])  16.2 us
    all_to_all x2, starting transfers between devices, exchanged(): return lax.all_to_all(parts, axis, split_axis=0, concat_axis=0, tiled=True)  7.51 us
  transfers between devices with their start and end apart: 16, of which 3 were waited for; matrix products, arithmetic and copies ran while one was open for 2% of the time, Pallas kernels for 20%

profile of v1, /device:TPU:1, one launch (start us, length us, event | category | flops | bytes accessed | tf_op | source)
XLA Modules:
  0.0 227.6 jit_solution(16663148407235499827)
XLA Ops:
  7.2 2.2 collective-permute-start.1
  9.4 2.6 %collective-permute-start.2 = (s32[32]{0:T(128)}, s32[32]{0:T(128)S(1)}, u32[]{:S(2)}, u32[]{:S(2)}) collective-permute-start(s32[32]{0:T(128)} %param.9), channel_id=1, source_target_pairs={{0,128},{64,192},{128,0},{192,64},{1,129},{65,193},{129,1},{193,65... | collective-permute-start | bytes 392 | tf_op jit(solution)/shard_map/ppermute | solution.py:18
  13.2 3.4 %copy-done = bf16[4096,1024]{1,0:T(8,128)(2,1)S(1)} copy-done((bf16[4096,1024]{1,0:T(8,128)(2,1)S(1)}, bf16[4096,1024]{1,0:T(8,128)(2,1)}, u32[]{:S(2)}) %copy-start) | copy-done | bytes 8388632
  19.1 5.2 %shard_map.85 = (f32[32,1024]{1,0:T(8,128)S(1)}, f32[256,1024]{1,0:T(8,128)S(1)}, f32[1,384]{1,0:T(1,128)S(1)}) custom-call(s32[2]{0:T(128)S(1)} %pad_add_fusion.meta.refs_0_, bf16[32,4096]{1,0:T(8,128)(2,1)S(1)} %copy-done.10, bf16[256,4096]{1,0:T(8,128)(2,1)S(1)} %copy-done.8, bf16[4096,1024]{1,0:T(8,128)(2,1)S(1)} %copy-done), custom_call_target="tpu_custom_call" | custom-call | flops 2415919104 | tf_op jit(solution)/shard_map/pallas_call | solution.py:50
  26.9 1.6 shard_map.86
  29.8 26.7 %all_to_all.25 = bf16[8,32,1152]{2,1,0:T(8,128)(2,1)S(1)} all-to-all(bf16[8,32,1152]{2,1,0:T(8,128)(2,1)S(1)} %broadcast_in_dim.47), channel_id=1, replica_groups=mesh['y'=4,'x'=4,'z'=8,'mp'=2] {'z'}, dimensions={0} | all-to-all | bytes 1179648 | tf_op jit(solution)/shard_map/all_to_all | solution.py:22
  56.5 1.6 broadcast_in_dim.49
  58.1 4.0 %all-to-all-start.1 = ((bf16[4,256,1152]{2,1,0:T(8,128)(2,1)}), bf16[4,256,1152]{2,1,0:T(8,128)(2,1)S(1)}, u32[]{:S(2)}, u32[]{:S(2)}) async-start(bf16[4,256,1152]{2,1,0:T(8,128)(2,1)} %broadcast_in_dim.49), calls=%async_computation.1 | async-start | bytes 4718592 | tf_op jit(solution)/shard_map/all_to_all | solution.py:22
  63.6 26.3 %all-to-all-done.1 = bf16[4,256,1152]{2,1,0:T(8,128)(2,1)S(1)} async-done(((bf16[4,256,1152]{2,1,0:T(8,128)(2,1)}), bf16[4,256,1152]{2,1,0:T(8,128)(2,1)S(1)}, u32[]{:S(2)}, u32[]{:S(2)}) %all-to-all-start.1) | async-done | bytes 2359328 | tf_op jit(solution)/shard_map/all_to_all | solution.py:22
  91.4 2.7 %shard_map.88 = f32[512,1024]{1,0:T(8,128)S(1)} custom-call(s32[2]{0:T(128)S(1)} %pad_add_fusion.meta.refs_0_, bf16[32,2,16,1152]{3,2,1,0:T(8,128)(2,1)S(1)} %bitcast.24, bf16[1024,1024]{1,0:T(8,128)(2,1)S(1)} %copy-done.2), custom_call_target="tpu_custom_call" | custom-call | flops 1073741824 | tf_op jit(solution)/shard_map/pallas_call | solution.py:50
  94.1 2.5 %collective-permute-start.4 = (f32[512,1024]{1,0:T(8,128)S(1)}, f32[512,1024]{1,0:T(8,128)S(1)}, u32[]{:S(2)}, u32[]{:S(2)}) collective-permute-start(f32[512,1024]{1,0:T(8,128)S(1)} %shard_map.88), channel_id=1, source_target_pairs={{0,1},{1,0},{2,3},{3,2},{4,5},{5,4},{6,7},{7,6},{8,9},{9,8},{10,11... | collective-permute-start | bytes 6291464 | tf_op jit(solution)/shard_map/ppermute | solution.py:18
  96.6 21.8 %shard_map.87 = (f32[512,1024]{1,0:T(8,128)S(1)}, f32[512,1024]{1,0:T(8,128)S(1)}, f32[512,128]{1,0:T(8,128)S(1)}) custom-call(s32[2]{0:T(128)S(1)} %pad_add_fusion.meta.refs_0_, bf16[32,2,16,1152]{3,2,1,0:T(8,128)(2,1)S(1)} %bitcast.25, bf16[1024,1024]{1,0:T(8,128)(2,1)S(1)} %copy-done.2), custom_call_target="tpu_custom_call" | custom-call | flops 2147483648 | tf_op jit(solution)/shard_map/pallas_call | solution.py:50
  118.4 2.6 %shard_map.89 = (f32[512,1024]{1,0:T(8,128)S(1)}, f32[2,512]{1,0:T(2,128)S(1)}) custom-call(s32[2]{0:T(128)S(1)} %pad_add_fusion.meta.refs_0_, f32[512,1024]{1,0:T(8,128)S(1)} %get-tuple-element.31.refs_1_, f32[512,1024]{1,0:T(8,128)S(1)} %collective-permute-done.4.refs_2_, f32[512,1024]{1,0:T(8,128)S(1)} %get-tuple-element.32.refs_3_, ...), custom_call_target="tpu_custom_call" | custom-call | tf_op jit(solution)/shard_map/pallas_call | solution.py:50
  121.0 12.4 %all_to_all.26.refs_2_ = f32[32,2,512]{2,1,0:T(2,128)S(1)} all-to-all(f32[32,2,512]{2,1,0:T(2,128)S(1)} %broadcast_in_dim.50), channel_id=1, replica_groups=mesh['y'=4,'x'=4,'z'=8,'mp'=2] {'x','z'}, dimensions={0} | all-to-all | bytes 262144 | tf_op jit(solution)/shard_map/all_to_all | solution.py:22
  133.4 2.6 %shard_map.90 = (bf16[512,1024]{1,0:T(8,128)(2,1)S(1)}, f32[1,512]{1,0:T(1,128)S(1)}) custom-call(s32[2]{0:T(128)S(1)} %pad_add_fusion.meta.refs_0_, f32[512,1024]{1,0:T(8,128)S(1)} %get-tuple-element.34.refs_1_, f32[32,2,512]{2,1,0:T(2,128)S(1)} %all_to_all.26.refs_2_, f32[512,128]{1,0:T(8,128)S(1)} %get-tuple-element.33.refs_4_.refs_3_), custom_call_target="tpu_custom_call" | custom-call | tf_op jit(solution)/shard_map/pallas_call | solution.py:50
  136.1 2.0 collective-permute-start.6
  138.1 4.7 %shard_map.91 = (bf16[512,1024]{1,0:T(8,128)(2,1)S(1)}, f32[1024,1024]{1,0:T(8,128)S(1)}) custom-call(s32[2]{0:T(128)S(1)} %pad_add_fusion.meta.refs_0_, bf16[512,1024]{1,0:T(8,128)(2,1)S(1)} %get-tuple-element.37.grad_ref, bf16[1024,1024]{1,0:T(8,128)(2,1)S(1)} %copy-done.3, bf16[32,2,16,1152]{3,2,1,0:T(8,128)(2,1)S(1)} %bitcast.26), custom_call_target="tpu_custom_call" | custom-call | flops 2147483648 | tf_op jit(solution)/shard_map/pallas_call | solution.py:50
  142.8 2.0 copy-done.4
  144.8 6.5 %shard_map.92 = (bf16[32,2,16,1024]{3,2,1,0:T(8,128)(2,1)S(1)}, bf16[1024,1024]{1,0:T(8,128)(2,1)S(1)}) custom-call(s32[2]{0:T(128)S(1)} %pad_add_fusion.meta.refs_0_, bf16[512,1024]{1,0:T(8,128)(2,1)S(1)} %collective-permute-done.6.grad_ref, bf16[1024,1024]{1,0:T(8,128)(2,1)S(1)} %copy-done.3, bf16[32,2,16,1152]{3,2,1,0:T(8,128)(2,1)S(1)} %bitcast.27, ...), custom_call_target="tpu_custom_call" | custom-call | flops 2147483648 | tf_op jit(solution)/shard_map/pallas_call | solution.py:50
  155.6 28.7 %all_to_all.27 = bf16[4,256,1024]{2,1,0:T(8,128)(2,1)S(1)} all-to-all(bf16[4,256,1024]{2,1,0:T(8,128)(2,1)S(1)} %bitcast.28), channel_id=1, replica_groups=mesh['y'=4,'x'=4,'z'=8,'mp'=2] {'x'}, dimensions={0} | all-to-all | bytes 4194304 | tf_op jit(solution)/shard_map/all_to_all | solution.py:22
  185.4 3.5 %all-to-all-start.4 = ((bf16[8,32,1024]{2,1,0:T(8,128)(2,1)}), bf16[8,32,1024]{2,1,0:T(8,128)(2,1)S(1)}, u32[]{:S(2)}, u32[]{:S(2)}) async-start(bf16[8,32,1024]{2,1,0:T(8,128)(2,1)} %bitcast.13), calls=%async_computation.4 | async-start | bytes 1048576 | tf_op jit(solution)/shard_map/all_to_all | solution.py:22
  190.7 15.7 %all-to-all-done.4 = bf16[8,32,1024]{2,1,0:T(8,128)(2,1)S(1)} async-done(((bf16[8,32,1024]{2,1,0:T(8,128)(2,1)}), bf16[8,32,1024]{2,1,0:T(8,128)(2,1)S(1)}, u32[]{:S(2)}, u32[]{:S(2)}) %all-to-all-start.4) | async-done | bytes 524320 | tf_op jit(solution)/shard_map/all_to_all | solution.py:22
  209.2 3.4 %copy-done.1 = bf16[4096,1024]{1,0:T(8,128)(2,1)S(1)} copy-done((bf16[4096,1024]{1,0:T(8,128)(2,1)S(1)}, bf16[4096,1024]{1,0:T(8,128)(2,1)}, u32[]{:S(2)}) %copy-start.1) | copy-done | bytes 8388632
  213.7 7.1 %shard_map.93 = (bf16[32,2048]{1,0:T(8,128)(2,1)}, bf16[256,2048]{1,0:T(8,128)(2,1)}) custom-call(s32[2]{0:T(128)S(1)} %pad_add_fusion.meta.refs_0_, f32[32,1024]{1,0:T(8,128)S(1)} %maximum_select_fusion.qg_ref, f32[32,1024]{1,0:T(8,128)S(1)} %collective-permute-done.7.qgo_ref, f32[32,1024]{1,0:T(8,128)S(1)} %get-tuple-element.41.qu_ref, ...), custom_call_target="tpu_custom_call" | custom-call | flops 2415919104 | tf_op jit(solution)/shard_map/pallas_call | solution.py:50
  (81 shorter events, 21.7 us)
Async XLA Ops:
  7.2 82.7 %all-gather.2.cloned.1.call-start = ((), (), s32[]{:S(2)}) async-start(), calls=%async_computation.6 | async-start | bytes 2621440 | tf_op jit(solution)/shard_map/all_gather | solution.py:478
  7.2 19.2 %collective-permute-start.1 = (s32[32]{0:T(128)}, s32[32]{0:T(128)S(1)}, u32[]{:S(2)}, u32[]{:S(2)}) collective-permute-start(s32[32]{0:T(128)} %param.9), channel_id=1, source_target_pairs={{0,64},{64,128},{128,192},{192,0},{1,65},{65,129},{129,193},{193,1... | collective-permute-start | bytes 392 | tf_op jit(solution)/shard_map/ppermute | solution.py:18
  9.4 17.1 %collective-permute-start.2 = (s32[32]{0:T(128)}, s32[32]{0:T(128)S(1)}, u32[]{:S(2)}, u32[]{:S(2)}) collective-permute-start(s32[32]{0:T(128)} %param.9), channel_id=1, source_target_pairs={{0,128},{64,192},{128,0},{192,64},{1,129},{65,193},{129,1},{193,65... | collective-permute-start | bytes 392 | tf_op jit(solution)/shard_map/ppermute | solution.py:18
  12.0 14.5 %collective-permute-start.3 = (s32[32]{0:T(128)}, s32[32]{0:T(128)S(1)}, u32[]{:S(2)}, u32[]{:S(2)}) collective-permute-start(s32[32]{0:T(128)} %param.9), channel_id=1, source_target_pairs={{0,192},{64,0},{128,64},{192,128},{1,193},{65,1},{129,65},{193,129... | collective-permute-start | bytes 392 | tf_op jit(solution)/shard_map/ppermute | solution.py:18
  13.2 3.4 %copy-start = (bf16[4096,1024]{1,0:T(8,128)(2,1)S(1)}, bf16[4096,1024]{1,0:T(8,128)(2,1)}, u32[]{:S(2)}) copy-start(bf16[4096,1024]{1,0:T(8,128)(2,1)} %w_ref.3) | copy-start | bytes 25165828
  19.1 6.8 %copy-start.16 = (s32[32]{0:T(128)S(1)}, s32[32]{0:T(128)}, u32[]{:S(2)}) copy-start(s32[32]{0:T(128)} %param.9) | copy-start | bytes 388
  19.1 6.9 %copy-start.15 = (s32[32,8]{0,1:T(8,128)S(1)}, s32[32,8]{0,1:T(8,128)}, u32[]{:S(2)}) copy-start(s32[32,8]{0,1:T(8,128)} %param.10) | copy-start | bytes 3076
  19.1 7.0 %copy-start.17 = (f32[32]{0:T(128)S(1)}, f32[32]{0:T(128)}, u32[]{:S(2)}) copy-start(f32[32]{0:T(128)} %param.11) | copy-start | bytes 388
  24.3 2.5 %collective-permute-start = (f32[1,384]{1,0:T(1,128)S(1)}, f32[1,384]{1,0:T(1,128)S(1)}, u32[]{:S(2)}, u32[]{:S(2)}) collective-permute-start(f32[1,384]{1,0:T(1,128)S(1)} %get-tuple-element.28.own_ref), channel_id=1, source_target_pairs={{0,1},{1,0},{2,3},{3,2},{4,5},{5,4},{6,7},{7,6},{8,9},{9,8},{10,11... | collective-permute-start | bytes 4616 | tf_op jit(solution)/shard_map/ppermute | solution.py:18
  58.1 31.7 %all-to-all-start.1 = ((bf16[4,256,1152]{2,1,0:T(8,128)(2,1)}), bf16[4,256,1152]{2,1,0:T(8,128)(2,1)S(1)}, u32[]{:S(2)}, u32[]{:S(2)}) async-start(bf16[4,256,1152]{2,1,0:T(8,128)(2,1)} %broadcast_in_dim.49), calls=%async_computation.1 | async-start | bytes 4718592 | tf_op jit(solution)/shard_map/all_to_all | solution.py:22
  62.1 144.4 %reduce-scatter.2.cloned.1.call-start = ((), (), s32[]{:S(2)}) async-start(), calls=%async_computation.7 | async-start | bytes 2621440 | tf_op jit(solution)/shard_map/reduce_scatter | solution.py:497
  62.1 146.2 %collective-permute-start.11 = (bf16[4096,1024]{1,0:T(8,128)(2,1)}, bf16[4096,1024]{1,0:T(8,128)(2,1)}, u32[]{:S(2)}, u32[]{:S(2)}) collective-permute-start(bf16[4096,1024]{1,0:T(8,128)(2,1)} %w_ref.3), channel_id=1, source_target_pairs={{0,1},{1,0},{2,3},{3,2},{4,5},{5,4},{6,7},{7,6},{8,9},{9,8},{10,11... | collective-permute-start | bytes 25165832 | tf_op jit(solution)/shard_map/ppermute | solution.py:18
  94.1 24.3 %collective-permute-start.4 = (f32[512,1024]{1,0:T(8,128)S(1)}, f32[512,1024]{1,0:T(8,128)S(1)}, u32[]{:S(2)}, u32[]{:S(2)}) collective-permute-start(f32[512,1024]{1,0:T(8,128)S(1)} %shard_map.88), channel_id=1, source_target_pairs={{0,1},{1,0},{2,3},{3,2},{4,5},{5,4},{6,7},{7,6},{8,9},{9,8},{10,11... | collective-permute-start | bytes 6291464 | tf_op jit(solution)/shard_map/ppermute | solution.py:18
  121.0 17.1 %copy-start.3 = (bf16[1024,1024]{1,0:T(8,128)(2,1)S(1)}, bf16[1024,1024]{1,0:T(8,128)(2,1)}, u32[]{:S(2)}) copy-start(bf16[1024,1024]{1,0:T(8,128)(2,1)} %all-gather.2.cloned.1.call-done.refs_2_.p_ref) | copy-start | bytes 6291460
  136.1 8.7 %collective-permute-start.6 = (bf16[512,1024]{1,0:T(8,128)(2,1)S(1)}, bf16[512,1024]{1,0:T(8,128)(2,1)S(1)}, u32[]{:S(2)}, u32[]{:S(2)}) collective-permute-start(bf16[512,1024]{1,0:T(8,128)(2,1)S(1)} %get-tuple-element.37.grad_ref), channel_id=1, source_target_pairs={{0,1},{1,0},{2,3},{3,2},{4,5},{5,4},{6,7},{7,6},{8,9},{9,8},{10,11... | collective-permute-start | bytes 3145736 | tf_op jit(solution)/shard_map/ppermute | solution.py:18
  184.3 25.0 %copy-start.12 = (f32[256,128]{1,0:T(8,128)S(1)}, f32[256,128]{1,0:T(8,128)}, u32[]{:S(2)}) copy-start(f32[256,128]{1,0:T(8,128)} %copy-done.11) | copy-start | bytes 393220
  184.3 25.0 %copy-start.14 = (f32[32,128]{1,0:T(8,128)S(1)}, f32[32,128]{1,0:T(8,128)}, u32[]{:S(2)}) copy-start(f32[32,128]{1,0:T(8,128)} %copy-done.13) | copy-start | bytes 49156
  185.4 21.0 %all-to-all-start.4 = ((bf16[8,32,1024]{2,1,0:T(8,128)(2,1)}), bf16[8,32,1024]{2,1,0:T(8,128)(2,1)S(1)}, u32[]{:S(2)}, u32[]{:S(2)}) async-start(bf16[8,32,1024]{2,1,0:T(8,128)(2,1)} %bitcast.13), calls=%async_computation.4 | async-start | bytes 1048576 | tf_op jit(solution)/shard_map/all_to_all | solution.py:22
  188.9 19.4 %collective-permute-start.10 = (f32[256,1024]{1,0:T(8,128)S(1)}, f32[256,1024]{1,0:T(8,128)S(1)}, u32[]{:S(2)}, u32[]{:S(2)}) collective-permute-start(f32[256,1024]{1,0:T(8,128)S(1)} %get-tuple-element.44.pu_ref), channel_id=1, source_target_pairs={{0,1},{1,0},{2,3},{3,2},{4,5},{5,4},{6,7},{7,6},{8,9},{9,8},{10,11... | collective-permute-start | bytes 3145736 | tf_op jit(solution)/shard_map/ppermute | solution.py:18
  190.1 18.1 %collective-permute-start.8 = (f32[32,1024]{1,0:T(8,128)S(1)}, f32[32,1024]{1,0:T(8,128)S(1)}, u32[]{:S(2)}, u32[]{:S(2)}) collective-permute-start(f32[32,1024]{1,0:T(8,128)S(1)} %get-tuple-element.41.qu_ref), channel_id=1, source_target_pairs={{0,1},{1,0},{2,3},{3,2},{4,5},{5,4},{6,7},{7,6},{8,9},{9,8},{10,11... | collective-permute-start | bytes 393224 | tf_op jit(solution)/shard_map/ppermute | solution.py:18
  190.3 17.3 %collective-permute-start.5 = (f32[16]{0:T(128)S(1)}, f32[16]{0:T(128)S(1)}, u32[]{:S(2)}, u32[]{:S(2)}) collective-permute-start(f32[16]{0:T(128)S(1)} %dynamic-slice_bitcast_fusion), channel_id=1, source_target_pairs={{0,1},{1,0},{2,3},{3,2},{4,5},{5,4},{6,7},{7,6},{8,9},{9,8},{10,11... | collective-permute-start | bytes 200 | tf_op jit(solution)/shard_map/ppermute | solution.py:18
  206.5 2.7 %collective-permute-start.9 = (bf16[256,1024]{1,0:T(8,128)(2,1)}, bf16[256,1024]{1,0:T(8,128)(2,1)S(1)}, u32[]{:S(2)}, u32[]{:S(2)}) collective-permute-start(bf16[256,1024]{1,0:T(8,128)(2,1)} %reduce-scatter.2.cloned.1.call-done.pg_ref), channel_id=1, source_target_pairs={{0,1},{1,0},{2,3},{3,2},{4,5},{5,4},{6,7},{7,6},{8,9},{9,8},{10,11... | collective-permute-start | bytes 1572872 | tf_op jit(solution)/shard_map/ppermute | solution.py:18
  207.6 1.6 collective-permute-start.7
  209.2 3.4 %copy-start.1 = (bf16[4096,1024]{1,0:T(8,128)(2,1)S(1)}, bf16[4096,1024]{1,0:T(8,128)(2,1)}, u32[]{:S(2)}) copy-start(bf16[4096,1024]{1,0:T(8,128)(2,1)} %w_ref.3) | copy-start | bytes 25165828
  (10 other events, 12.8 us)
Sparse Core Ops, SparseCore 0:
  29.9 33.3 all-gather.1
  154.2 24.7 reduce-scatter.1

commit v2 on v1

v2 whole, which is shorter than its diff:
```python
import jax
import jax.numpy as jnp
from jax import lax
from jax.experimental import pallas as pl
from jax.experimental.pallas import tpu as pltpu
from jax.sharding import Mesh, PartitionSpec as P

sharpness = 1.0 / 0.02
bf16 = jnp.bfloat16
f32 = jnp.float32
AUX = 128
TILE = 256
INDEX = 16
MIB = 1024 * 1024
SHAPES = {128: (4, 4, 8), 16: (4, 4, 1), 8: (2, 2, 2)}


def shifted(value, axis, shift):
    n = lax.axis_size(axis)
    return lax.ppermute(value, axis, [(i, (i + shift) % n) for i in range(n)])


def exchanged(parts, axis):
    return lax.all_to_all(parts, axis, split_axis=0, concat_axis=0, tiled=True)


def to_all(value, axis):
    n = lax.axis_size(axis)
    return exchanged(jnp.broadcast_to(value[None], (n,) + value.shape), axis)


def gather_ring(value, axis):
    n = lax.axis_size(axis)
    if n == 2:
        return [value, shifted(value, axis, 1)]
    cut = value.shape[0] // 2
    before, after = shifted(value, axis, 1), shifted(value, axis, -1)
    far = [shifted(before[:cut], axis, 1), shifted(after[cut:], axis, -1)]
    return [value, before] + far + [after]


def return_ring(parts, axis):
    n = lax.axis_size(axis)
    if n == 2:
        return parts[0].astype(f32) + shifted(parts[1], axis, 1).astype(f32)
    cut = parts.shape[1] // 2
    up = shifted(parts[2, :cut], axis, 1).astype(f32)
    down = shifted(parts[2, cut:], axis, -1).astype(f32)
    ahead = jnp.concatenate([(parts[3, :cut].astype(f32) + up).astype(bf16), parts[3, cut:]])
    behind = jnp.concatenate([parts[1, :cut], (parts[1, cut:].astype(f32) + down).astype(bf16)])
    total = parts[0].astype(f32) + shifted(ahead, axis, 1).astype(f32)
    return total + shifted(behind, axis, -1).astype(f32)


def split_three(value):
    high = lax.reduce_precision(value, 8, 7)
    rest = value - high
    middle = lax.reduce_precision(rest, 8, 7)
    return high, middle, rest - middle


def contract(a, b, dims):
    return lax.dot_general(a, b, (dims, ((), ())), preferred_element_type=f32)


def whole(*shape):
    return pl.BlockSpec(shape, lambda j, meta: (0,) * len(shape))


def struct(shape, dtype=f32):
    return jax.ShapeDtypeStruct(shape, dtype)


def call(body, meta, steps, in_specs, out_specs, out_shape, args, scratch=(), flops=0, vmem=24):
    return pl.pallas_call(
        body,
        grid_spec=pltpu.PrefetchScalarGridSpec(
            num_scalar_prefetch=1,
            grid=(steps,),
            in_specs=in_specs,
            out_specs=out_specs,
            scratch_shapes=list(scratch),
        ),
        out_shape=out_shape,
        compiler_params=pltpu.CompilerParams(
            dimension_semantics=("arbitrary",), vmem_limit_bytes=vmem * MIB
        ),
        cost_estimate=pl.CostEstimate(flops=flops, bytes_accessed=0, transcendentals=0),
    )(meta, *args)


def row_of_lane_sums(block):
    return jnp.sum(block.T, axis=0, keepdims=True)


def lanes_to_rows(row):
    return jnp.broadcast_to(row, (128, row.shape[1])).T


def project_body(meta, q_ref, p_ref, w_ref, qo_ref, po_ref, square_ref, x_ref, acc_ref):
    step = pl.program_id(0)
    n_q = q_ref.shape[0]

    @pl.when(step == 0)
    def _():
        x_ref[:n_q] = q_ref[...]
        x_ref[n_q:] = p_ref[...]
        acc_ref[...] = jnp.zeros_like(acc_ref)

    proj = contract(x_ref[...], w_ref[...], ((1,), (0,)))
    qo_ref[...] = proj[:n_q]
    po_ref[...] = proj[n_q:]
    square = proj * proj
    acc_ref[...] += square[:, :128] + square[:, 128:]

    @pl.when(step == pl.num_programs(0) - 1)
    def _():
        padded = jnp.concatenate([acc_ref[:n_q], jnp.zeros((128 - n_q, 128), f32)], axis=0)
        square_ref[:, :128] = row_of_lane_sums(padded)
        square_ref[:, 128:] = row_of_lane_sums(acc_ref[n_q:])


def project(meta, queries, passages, weight):
    n_q, n_p, (depth, width) = queries.shape[0], passages.shape[0], weight.shape
    column = lambda rows: pl.BlockSpec((rows, TILE), lambda j, meta: (0, j))
    return call(
        project_body,
        meta,
        width // TILE,
        [whole(n_q, depth), whole(n_p, depth), column(depth)],
        [column(n_q), column(n_p), whole(1, 128 + n_p)],
        [struct((n_q, width)), struct((n_p, width)), struct((1, 128 + n_p))],
        (queries, passages, weight),
        [pltpu.VMEM((n_q + n_p, depth), bf16), pltpu.VMEM((n_q + n_p, 128), f32)],
        2 * (n_q + n_p) * depth * width,
        60,
    )


def normalize_body(
    meta, q_ref, p_ref, own_ref, got_ref, aux_ref, message_ref, qu_ref, pu_ref, pe_ref, qi_ref, pi_ref
):
    n_q, width = q_ref.shape
    inv = lanes_to_rows(lax.rsqrt(own_ref[...] + got_ref[...] + 1e-06))
    q_inv, p_inv = inv[:n_q], inv[128:]
    qi_ref[...] = q_inv
    pi_ref[...] = p_inv
    q_unit = q_ref[...] * q_inv[:, :1]
    p_unit = p_ref[...] * p_inv[:, :1]
    qu_ref[...] = q_unit
    pu_ref[...] = p_unit
    pe_ref[...] = p_unit.astype(bf16)
    half = n_q // 2
    first = meta[0] == 0

    def store(columns, value):
        top, bottom = value[:half], value[half:]
        message_ref[:half, columns] = jnp.where(first, top, bottom).astype(bf16)
        message_ref[half:, columns] = jnp.where(first, bottom, top).astype(bf16)

    store(slice(0, width), q_unit)
    store(slice(width, width + AUX), aux_ref[...])


def normalize(meta, q_proj, p_proj, square, square_got, aux):
    (n_q, width), n_p = q_proj.shape, p_proj.shape[0]
    shapes = [
        struct((n_q, width + AUX), bf16),
        struct((n_q, width)),
        struct((n_p, width)),
        struct((n_p, width), bf16),
        struct((n_q, 128)),
        struct((n_p, 128)),
    ]
    args = (q_proj, p_proj, square, square_got, aux)
    return call(
        normalize_body,
        meta,
        1,
        [whole(*a.shape) for a in args],
        [whole(*s.shape) for s in shapes],
        shapes,
        args,
    )


def flat(block):
    return block.reshape(-1, block.shape[-1])


def rem(value, n):
    return lax.rem(value, jnp.int32(n))


def owner_of(meta, step, n_y, slots):
    return (rem(meta[3] - step + n_y, n_y) * slots + meta[1]).astype(f32)


def chunks(rows, size=32):
    return [slice(at, at + size) for at in range(0, rows, size)]


def row_index(rows, columns, start=0):
    return (lax.broadcasted_iota(jnp.int32, (rows, columns), 0) + start).astype(f32)


def score_sent_body(meta, q_ref, p_ref, score_ref):
    width = p_ref.shape[1]
    score_ref[...] = contract(p_ref[...], flat(q_ref[:, 0, :, :width]), ((1,), (1,)))


def score_sent(meta, q_all, p_all, n_y):
    slots, _, half, full = q_all.shape
    passages, width = p_all.shape
    rows, block = slots * half, passages // n_y
    return call(
        score_sent_body,
        meta,
        n_y,
        [
            pl.BlockSpec((slots, 1, half, full), lambda j, meta: (0, 1, 0, 0)),
            pl.BlockSpec((block, width), lambda j, meta: (j, 0)),
        ],
        pl.BlockSpec((block, rows), lambda j, meta: (j, 0)),
        struct((passages, rows)),
        (q_all, p_all),
        flops=2 * rows * passages * width,
    )


def score_kept_body(
    n_y, per_query, named, meta, q_ref, p_ref, score_ref, weight_ref, info_ref, count_ref
):
    step = pl.program_id(0)
    slots, _, half, full = q_ref.shape
    block, width = p_ref.shape
    rows = slots * half

    @pl.when(step == 0)
    def _():
        own = flat(q_ref[:, 0, :, width:]).astype(f32).T
        other = flat(q_ref[:, 1, :, width:]).astype(f32).T
        info_ref[...] = own
        turn = meta[3] - lax.broadcasted_iota(jnp.int32, (8, 1), 0)
        turn = jnp.where(turn < 0, turn + n_y, turn)
        owners = (turn * slots + meta[1]).astype(f32)
        row = row_index(block, rows)
        count = jnp.zeros((block, 8), f32)
        for info in (own, other):
            for k in [0] + list(range(per_query, named)):
                owned = (info[k : k + 1] == owners).astype(f32).astype(bf16)
                placed = (info[INDEX + k : INDEX + k + 1] == row).astype(f32).astype(bf16)
                count = count + contract(placed, owned, ((1,), (1,)))
        count_ref[...] = count

    score_ref[...] = contract(p_ref[...], flat(q_ref[:, 0, :, :width]), ((1,), (1,)))
    owner = owner_of(meta, step, n_y, slots)
    place = jnp.where(info_ref[:INDEX] == owner, info_ref[INDEX : 2 * INDEX], -1.0)
    line = lax.broadcasted_iota(jnp.int32, (1, 8), 1)
    count = jnp.sum(jnp.where(line == step, count_ref[...], 0.0), axis=1, keepdims=True)
    for at in chunks(block):
        row = row_index(at.stop - at.start, rows, at.start)
        weight = jnp.broadcast_to(count[at], row.shape)
        for k in range(1, per_query):
            weight = weight + (place[k : k + 1] == row).astype(f32)
        weight_ref[at] = weight


def score_kept(meta, q_all, p_all, n_y, per_query, named):
    slots, _, half, full = q_all.shape
    passages, width = p_all.shape
    rows, block = slots * half, passages // n_y
    out = pl.BlockSpec((block, rows), lambda j, meta: (j, 0))

    def body(*refs):
        score_kept_body(n_y, per_query, named, *refs)

    return call(
        body,
        meta,
        n_y,
        [
            whole(slots, 2, half, full),
            pl.BlockSpec((block, width), lambda j, meta: (j, 0)),
        ],
        [out, out, whole(AUX, rows)],
        [struct((passages, rows)), struct((passages, rows)), struct((AUX, rows))],
        (q_all, p_all),
        [pltpu.VMEM((block, 8), f32)],
        4 * rows * passages * width,
    )


def positive_place(meta, step, n_y, slots, info_ref):
    owner = owner_of(meta, step, n_y, slots)
    return jnp.where(info_ref[0:1] == owner, info_ref[INDEX : INDEX + 1], -1.0)


def turned_slots(meta, n_x, rows):
    size = rows // n_x
    for s in range(n_x):
        start = pl.multiple_of(rem(meta[2] - s + n_x, n_x) * size, size)
        yield slice(s * size, (s + 1) * size), pl.ds(start, size)


def weigh_body(n_y, n_x, slots, meta, kept_ref, got_ref, weight_ref, info_ref, e_ref, sum_ref, acc_ref):
    step = pl.program_id(0)
    block, rows = kept_ref.shape

    @pl.when(step == 0)
    def _():
        acc_ref[...] = jnp.zeros_like(acc_ref)

    place = positive_place(meta, step, n_y, slots, info_ref)
    for at in chunks(block):
        score = (kept_ref[at] + got_ref[at]) * sharpness
        weighted = weight_ref[at] * jnp.exp(score)
        e_ref[at] = weighted
        own = jnp.where(place == row_index(at.stop - at.start, rows, at.start), score, 0.0)
        acc_ref[0] += jnp.sum(weighted.reshape(-1, 8, rows), axis=0)
        acc_ref[1] += jnp.sum(own.reshape(-1, 8, rows), axis=0)

    @pl.when(step == pl.num_programs(0) - 1)
    def _():
        for i in range(2):
            total = jnp.sum(acc_ref[i], axis=0, keepdims=True)
            for here, there in turned_slots(meta, n_x, rows):
                sum_ref[i : i + 1, there] = total[:, here]


def weigh(meta, kept, got, weight, info, n_y, n_x, slots):
    passages, rows = kept.shape
    block = pl.BlockSpec((passages // n_y, rows), lambda j, meta: (j, 0))

    def body(*refs):
        weigh_body(n_y, n_x, slots, *refs)

    return call(
        body,
        meta,
        n_y,
        [block, block, block, whole(AUX, rows)],
        [block, whole(2, rows)],
        [struct((passages, rows)), struct((2, rows))],
        (kept, got, weight, info),
        [pltpu.VMEM((2, 8, rows), f32)],
    )


def slope_body(n_y, n_x, slots, meta, e_ref, sums_ref, info_ref, grad_ref, loss_ref, scale_ref, inv_ref):
    step = pl.program_id(0)
    block, rows = e_ref.shape

    @pl.when(step == 0)
    def _():
        loss_ref[...] = jnp.sum(sums_ref[...], axis=0)
        for here, there in turned_slots(meta, n_x, rows):
            inv_ref[:, here] = loss_ref[0:1, there]
        for here, there in turned_slots(meta, n_x, rows):
            scale_ref[:, here] = loss_ref[1:2, there]
        total = inv_ref[...]
        loss_ref[0:1] = jnp.log(total) - scale_ref[...]
        inv_ref[...] = 1.0 / total
        base = 2 * INDEX
        slope = (info_ref[base : base + 1] + info_ref[base + 1 : base + 2]) + info_ref[base + 2 : base + 3]
        scale_ref[...] = slope * sharpness

    place = positive_place(meta, step, n_y, slots, info_ref)
    inv, scale = inv_ref[...], scale_ref[...]
    for at in chunks(block):
        match = (place == row_index(at.stop - at.start, rows, at.start)).astype(f32)
        grad_ref[at] = (scale * (e_ref[at] * inv - match)).astype(bf16)


def slopes(meta, e, sums, info, n_y, n_x, slots):
    passages, rows = e.shape
    block = pl.BlockSpec((passages // n_y, rows), lambda j, meta: (j, 0))

    def body(*refs):
        slope_body(n_y, n_x, slots, *refs)

    return call(
        body,
        meta,
        n_y,
        [block, whole(*sums.shape), whole(AUX, rows)],
        [block, whole(2, rows)],
        [struct((passages, rows), bf16), struct((2, rows))],
        (e, sums, info),
        [pltpu.VMEM((1, rows), f32), pltpu.VMEM((1, rows), f32)],
    )


def query_part_body(meta, grad_ref, p_ref, out_ref, turned_ref):
    @pl.when(pl.program_id(0) == 0)
    def _():
        turned_ref[...] = grad_ref[...].T

    out_ref[...] = contract(turned_ref[...], p_ref[...], ((1,), (0,))).astype(bf16)


def query_part(meta, grad, p_all):
    passages, rows = grad.shape
    width = p_all.shape[1]
    column = lambda r: pl.BlockSpec((r, TILE), lambda j, meta: (0, j))
    return call(
        query_part_body,
        meta,
        width // TILE,
        [whole(passages, rows), column(passages)],
        column(rows),
        struct((rows, width), bf16),
        (grad, p_all),
        [pltpu.VMEM((rows, passages), bf16)],
        2 * rows * passages * width,
    )


def query_rest_body(meta, grad_ref, p_ref, first_ref, out_ref, turned_ref):
    @pl.when(pl.program_id(0) == 0)
    def _():
        turned_ref[...] = grad_ref[...].T

    slots, _, half, tile = out_ref.shape
    out_ref[:, 0] = first_ref[...].reshape(slots, half, tile)
    rest = contract(turned_ref[...], p_ref[...], ((1,), (0,))).astype(bf16)
    out_ref[:, 1] = rest.reshape(slots, half, tile)


def query_rest(meta, grad, p_all, first, slots):
    passages, rows = grad.shape
    width = p_all.shape[1]
    half = rows // slots
    column = lambda r: pl.BlockSpec((r, TILE), lambda j, meta: (0, j))
    return call(
        query_rest_body,
        meta,
        width // TILE,
        [whole(passages, rows), column(passages), column(rows)],
        pl.BlockSpec((slots, 2, half, TILE), lambda j, meta: (0, 0, 0, j)),
        struct((slots, 2, half, width), bf16),
        (grad, p_all, first),
        [pltpu.VMEM((rows, passages), bf16)],
        2 * rows * passages * width,
    )


def passage_part_body(meta, grad_ref, other_ref, q_ref, out_ref):
    total = contract(grad_ref[...], flat(q_ref[:, 0]), ((1,), (0,)))
    total = total + contract(other_ref[...], flat(q_ref[:, 1]), ((1,), (0,)))
    out_ref[...] = total.astype(bf16)


def passage_part(meta, grad, other, q_all, width):
    passages, rows = grad.shape
    slots, _, half, _ = q_all.shape
    return call(
        passage_part_body,
        meta,
        width // TILE,
        [
            whole(passages, rows),
            whole(passages, rows),
            pl.BlockSpec((slots, 2, half, TILE), lambda j, meta: (0, 0, 0, j)),
        ],
        pl.BlockSpec((passages, TILE), lambda j, meta: (0, j)),
        struct((passages, width), bf16),
        (grad, other, q_all),
        flops=4 * rows * passages * width,
    )


def finish_body(
    meta, qg_ref, qgo_ref, qu_ref, quo_ref, qi_ref, pg_ref, pgo_ref, pu_ref, puo_ref, pi_ref,
    w_ref, wo_ref, q_out, p_out, dir_ref
):
    n_q, width = qg_ref.shape

    @pl.when(pl.program_id(0) == 0)
    def _():
        def tangent(at, grad_ref, grad_other, unit_ref, unit_other, inv_ref):
            grad, other = grad_ref[...].astype(f32), grad_other[...].astype(f32)
            unit, beyond = unit_ref[...], unit_other[...]
            radial = jnp.sum(unit * grad + beyond * other, axis=1, keepdims=True)
            inv = inv_ref[:, :1]
            dir_ref[at, :width] = (inv * (grad - unit * radial)).astype(bf16)
            dir_ref[at, width:] = (inv * (other - beyond * radial)).astype(bf16)

        tangent(slice(0, n_q), qg_ref, qgo_ref, qu_ref, quo_ref, qi_ref)
        tangent(slice(n_q, dir_ref.shape[0]), pg_ref, pgo_ref, pu_ref, puo_ref, pi_ref)

    state = contract(dir_ref[:, :width], w_ref[...], ((1,), (1,)))
    state = (state + contract(dir_ref[:, width:], wo_ref[...], ((1,), (1,)))).astype(bf16)
    q_out[...] = state[:n_q]
    p_out[...] = state[n_q:]


def finish(meta, rows_in, weight, weight_got):
    depth, width = weight.shape
    n_q, n_p = rows_in[0].shape[0], rows_in[5].shape[0]
    tile = min(512, depth // 2)
    steps = depth // 2 // tile
    rows = pl.BlockSpec((tile, width), lambda j, meta: (meta[0] * steps + j, 0))
    column = lambda r: pl.BlockSpec((r, tile), lambda j, meta: (0, j))
    return call(
        finish_body,
        meta,
        steps,
        [whole(*a.shape) for a in rows_in] + [rows, rows],
        [column(n_q), column(n_p)],
        [struct((n_q, depth // 2), bf16), struct((n_p, depth // 2), bf16)],
        (*rows_in, weight, weight_got),
        [pltpu.VMEM((n_q + n_p, 2 * width), bf16)],
        2 * (n_q + n_p) * depth * width,
        60,
    )


def per_device(query_states, passage_states, head_weight, positives, negatives, slope):
    n_y, n_x, n_z = (lax.axis_size(a) for a in ("y", "x", "z"))
    y, x, z, core = (lax.axis_index(a) for a in ("y", "x", "z", "mp"))
    q_rows, p_rows = query_states.shape[0], passage_states.shape[0]
    width = head_weight.shape[1]
    half = q_rows // 2
    slots = n_x * n_z
    column = x * n_z + z
    meta = jnp.stack([core, column, x, y]).astype(jnp.int32)

    def own_first(rows):
        return jnp.where(core == 0, rows, jnp.roll(rows, half, axis=0))

    q_proj, p_proj, square = project(meta, query_states, passage_states, head_weight)
    square_got = shifted(square, "mp", 1)
    started = lax.optimization_barrier((positives, square))[0]
    line_positives = [shifted(started, "y", s) for s in range(1, n_y)]
    ids = jnp.concatenate(
        [positives[:, None], negatives] + [other[:, None] for other in line_positives], axis=1
    )
    named = ids.shape[1]
    per_query = 1 + negatives.shape[1]
    padded = ((0, 0), (0, INDEX - named))
    aux = jnp.concatenate(
        [jnp.pad((ids // p_rows).astype(f32), padded), jnp.pad((ids % p_rows).astype(f32), padded)]
        + [part[:, None] for part in split_three(slope)],
        axis=1,
    )
    aux = jnp.pad(aux, ((0, 0), (0, AUX - aux.shape[1])))
    message, q_unit, p_unit, p_embed, q_inv, p_inv = normalize(
        meta, q_proj, p_proj, square, square_got, aux
    )
    p_all = jnp.concatenate(gather_ring(p_embed, "y"), axis=0)
    weight_got = shifted(lax.optimization_barrier((head_weight, square_got))[0], "mp", 1)
    q_unit_got, p_unit_got = shifted(q_unit, "mp", 1), shifted(p_unit, "mp", 1)

    q_z = to_all(message, "z").reshape(n_z * q_rows, width + AUX)
    q_all = jnp.concatenate(gather_ring(q_z, "x"), axis=0)
    q_all = q_all.reshape(slots, 2, half, width + AUX)

    sent = score_sent(meta, q_all, p_all, n_y)
    got = shifted(sent, "mp", 1)
    kept, weight, info = score_kept(meta, q_all, p_all, n_y, per_query, named)
    e, sums = weigh(meta, kept, got, weight, info, n_y, n_x, slots)
    sums = to_all(sums, ("x", "z")).reshape((slots,) + sums.shape)
    grad, loss = slopes(meta, e, sums, info, n_y, n_x, slots)
    grad_got = shifted(grad, "mp", 1)
    own_loss = lax.dynamic_slice_in_dim(loss[0], z * half, half, 0)
    losses = own_first(jnp.concatenate([own_loss, shifted(own_loss, "mp", 1)]))

    q_part = query_part(meta, grad, p_all)
    q_part = query_rest(meta, grad_got, p_all, q_part, slots)
    p_part = passage_part(meta, grad, grad_got, q_all, width)
    q_part = return_ring(q_part.reshape(n_x, n_z * q_rows, width), "x").astype(bf16)
    p_grad = return_ring(p_part.reshape(n_y, p_rows, width), "y").astype(bf16)
    back = exchanged(q_part.reshape(n_z, q_rows, width), "z")
    q_grad = own_first(sum(back[s].astype(f32) for s in range(n_z)))

    q_grad_got, p_grad_got = shifted(q_grad, "mp", 1), shifted(p_grad, "mp", 1)
    query_grads, passage_grads = finish(
        meta,
        (q_grad, q_grad_got, q_unit, q_unit_got, q_inv, p_grad, p_grad_got, p_unit, p_unit_got, p_inv),
        head_weight,
        weight_got,
    )
    return losses, query_grads, passage_grads


def solution(mesh):
    n_dp, n_core = mesh.devices.shape
    shape = SHAPES[n_dp] + (n_core,)
    grid = Mesh(mesh.devices.reshape(shape), ("y", "x", "z", "mp"))
    dp = ("y", "x", "z")
    placed = (P(dp, None), P(dp, None), P(None, "mp"), P(dp), P(dp, None), P(dp))
    return jax.shard_map(
        per_device,
        mesh=grid,
        in_specs=placed,
        out_specs=(P(dp), P(dp, "mp"), P(dp, "mp")),
        check_vma=False,
    )
```

time: 228 us -> 178 us (0.78)
  blocking collectives: 67.7 us -> 19.1 us
  starting transfers between devices: 23.8 us -> 51.7 us
  Pallas kernels: 54.8 us -> 37.9 us
  between operations: 14.2 us -> 1.06 us
  local copies, waits for them, and re-layouts: 22.2 us -> 10.1 us
  other arithmetic: 2 us -> 9.94 us
  waiting for transfers between devices: 42.9 us -> 47 us
    all_to_all x3 -> x1, blocking collectives: 67.7 us -> 19.1 us  [exchanged(): return lax.all_to_all(parts, axis, split_axis=0, concat_axis=0, tiled=True)]
    ppermute x12 -> x28, waiting for transfers between devices: 0.96 us -> 46.4 us  [shifted(): return lax.ppermute(value, axis, [(i, (i + shift) % n) for i in range(n)])]
    all_to_all x2, waiting for transfers between devices: 41.9 us -> 0.69 us  [exchanged(): return lax.all_to_all(parts, axis, split_axis=0, concat_axis=0, tiled=True)]
    ppermute x12 -> x28, starting transfers between devices: 16.2 us -> 39.4 us  [shifted(): return lax.ppermute(value, axis, [(i, (i + shift) % n) for i in range(n)])]
    pallas_call x9 -> x10, Pallas kernels: 54.8 us -> 37.9 us  [call(): pl.pallas_call(body, grid_spec=pltpu.PrefetchScalarGridSpec(num_scalar_pr...]
    unnamed x37 -> x39, local copies, waits for them, and re-layouts: 19.6 us -> 5.72 us
    all_to_all x2, starting transfers between devices: 7.51 us -> 12.3 us  [exchanged(): return lax.all_to_all(parts, axis, split_axis=0, concat_axis=0, tiled=True)]
    convert_element_type x0 -> x4, other arithmetic: none -> 3.74 us  [the longest x1 2.27 us: per_device(): p_grad = return_ring(p_part.reshape(n_y, p_rows, width), 'y').astype(bf16)]
  transfers between devices with their start and end apart: 16 -> 30, of which waited for: 3 -> 10; matrix products, arithmetic and copies ran while one was open for 2% -> 8% of each run, Pallas kernels for 20% -> 11%
where the time goes in v2:
time: 178 us; the launch traced here: 177 us
  starting transfers between devices  51.7 us (29%)
  waiting for transfers between devices  47 us (26%)
  Pallas kernels  37.9 us (21%)
  blocking collectives  19.1 us (11%)
  local copies, waits for them, and re-layouts  10.1 us (6%)
  other arithmetic  9.94 us (6%)
    ppermute x28, waiting for transfers between devices, shifted(): return lax.ppermute(value, axis, [(i, (i + shift) % n) for i in range(n)])  46.4 us
    ppermute x28, starting transfers between devices, shifted(): return lax.ppermute(value, axis, [(i, (i + shift) % n) for i in range(n)])  39.4 us
    pallas_call x10, Pallas kernels, call(): pl.pallas_call(body, grid_spec=pltpu.PrefetchScalarGridSpec(num_scalar_pr...  37.9 us
    all_to_all x1, blocking collectives, exchanged(): return lax.all_to_all(parts, axis, split_axis=0, concat_axis=0, tiled=True)  19.1 us
    all_to_all x2, starting transfers between devices, exchanged(): return lax.all_to_all(parts, axis, split_axis=0, concat_axis=0, tiled=True)  12.3 us
    unnamed x39, local copies, waits for them, and re-layouts  5.72 us
  transfers between devices with their start and end apart: 30, of which 10 were waited for; matrix products, arithmetic and copies ran while one was open for 8% of the time, Pallas kernels for 11%

profile of v2, /device:TPU:1, one launch (start us, length us, event | category | flops | bytes accessed | tf_op | source)
XLA Modules:
  0.0 176.9 jit_solution(11908862337040555659)
XLA Ops:
  1.3 8.3 %shard_map.85 = (f32[32,1024]{1,0:T(8,128)}, f32[256,1024]{1,0:T(8,128)}, f32[1,384]{1,0:T(1,128)}) custom-call(s32[4]{0:T(128)} %pad_add_fusion.meta.refs_0_, bf16[32,4096]{1,0:T(8,128)(2,1)} %q_ref.1, bf16[256,4096]{1,0:T(8,128)(2,1)} %p_ref.1, bf16[4096,1024]{1,0:T(8,128)(2,1)} %w_ref.3), custom_call_target="tpu_custom_call" | custom-call | flops 2415919104 | tf_op jit(solution)/shard_map/pallas_call | solution.py:75
  11.8 2.6 %collective-permute-start.2 = (s32[32]{0:T(128)S(1)}, s32[32]{0:T(128)S(1)}, u32[]{:S(2)}, u32[]{:S(2)}) collective-permute-start(s32[32]{0:T(128)S(1)} %copy-done.13), channel_id=1, source_target_pairs={{0,128},{64,192},{128,0},{192,64},{1,129},{65,193},{129,1},{193,65... | collective-permute-start | bytes 392 | tf_op jit(solution)/shard_map/ppermute | solution.py:20
  22.6 8.2 %all-to-all-start = ((bf16[8,32,1152]{2,1,0:T(8,128)(2,1)}), bf16[8,32,1152]{2,1,0:T(8,128)(2,1)S(1)}, u32[]{:S(2)}, u32[]{:S(2)}) async-start(bf16[8,32,1152]{2,1,0:T(8,128)(2,1)} %broadcast_in_dim.40), calls=%async_computation | async-start | bytes 1179648 | tf_op jit(solution)/shard_map/all_to_all | solution.py:24
  33.5 10.2 %collective-permute-done.8 = bf16[256,1024]{1,0:T(8,128)(2,1)S(1)} collective-permute-done((bf16[256,1024]{1,0:T(8,128)(2,1)S(1)}, bf16[256,1024]{1,0:T(8,128)(2,1)S(1)}, u32[]{:S(2)}, u32[]{:S(2)}) %collective-permute-start.8) | collective-permute-done | bytes 524320 | tf_op jit(solution)/shard_map/ppermute | solution.py:20
  45.1 2.7 %collective-permute-start.11 = (bf16[128,1024]{1,0:T(8,128)(2,1)}, bf16[128,1024]{1,0:T(8,128)(2,1)}, u32[]{:S(2)}, u32[]{:S(2)}) collective-permute-start(bf16[128,1024]{1,0:T(8,128)(2,1)} %slice.129), channel_id=1, source_target_pairs={{0,192},{64,0},{128,64},{192,128},{1,193},{65,1},{129,65},{193,129... | collective-permute-start | bytes 786440 | tf_op jit(solution)/shard_map/ppermute | solution.py:20
  49.7 3.0 %collective-permute-start.27 = (bf16[4096,1024]{1,0:T(8,128)(2,1)}, bf16[4096,1024]{1,0:T(8,128)(2,1)}, u32[]{:S(2)}, u32[]{:S(2)}) collective-permute-start(bf16[4096,1024]{1,0:T(8,128)(2,1)} %w_ref.3), channel_id=1, source_target_pairs={{0,1},{1,0},{2,3},{3,2},{4,5},{5,4},{6,7},{7,6},{8,9},{9,8},{10,11... | collective-permute-start | bytes 25165832 | tf_op jit(solution)/shard_map/ppermute | solution.py:20
  56.3 5.6 %collective-permute-done.4 = bf16[256,1152]{1,0:T(8,128)(2,1)S(1)} collective-permute-done((bf16[256,1152]{1,0:T(8,128)(2,1)S(1)}, bf16[256,1152]{1,0:T(8,128)(2,1)S(1)}, u32[]{:S(2)}, u32[]{:S(2)}) %collective-permute-start.4) | collective-permute-done | bytes 589856 | tf_op jit(solution)/shard_map/ppermute | solution.py:20
  62.1 5.7 %collective-permute-done.6 = bf16[256,1152]{1,0:T(8,128)(2,1)S(1)} collective-permute-done((bf16[256,1152]{1,0:T(8,128)(2,1)S(1)}, bf16[256,1152]{1,0:T(8,128)(2,1)S(1)}, u32[]{:S(2)}, u32[]{:S(2)}) %collective-permute-start.6) | collective-permute-done | bytes 589856 | tf_op jit(solution)/shard_map/ppermute | solution.py:20
  67.8 2.8 %collective-permute-start.7 = (bf16[128,1152]{1,0:T(8,128)(2,1)S(1)}, bf16[128,1152]{1,0:T(8,128)(2,1)S(1)}, u32[]{:S(2)}, u32[]{:S(2)}) collective-permute-start(bf16[128,1152]{1,0:T(8,128)(2,1)S(1)} %slice.127), channel_id=1, source_target_pairs={{0,48},{16,0},{32,16},{48,32},{1,49},{17,1},{33,17},{49,33},{2,50}... | collective-permute-start | bytes 884744 | tf_op jit(solution)/shard_map/ppermute | solution.py:20
  70.7 5.4 %collective-permute-done.7 = bf16[128,1152]{1,0:T(8,128)(2,1)S(1)} collective-permute-done((bf16[128,1152]{1,0:T(8,128)(2,1)S(1)}, bf16[128,1152]{1,0:T(8,128)(2,1)S(1)}, u32[]{:S(2)}, u32[]{:S(2)}) %collective-permute-start.7) | collective-permute-done | bytes 294944 | tf_op jit(solution)/shard_map/ppermute | solution.py:20
  76.2 2.6 %shard_map.88 = f32[1024,512]{1,0:T(8,128)S(1)} custom-call(s32[4]{0:T(128)S(1)} %copy-done.5, bf16[32,2,16,1152]{3,2,1,0:T(8,128)(2,1)S(1)} %bitcast.68, bf16[1024,1024]{1,0:T(8,128)(2,1)S(1)} %constant_dynamic-update-slice_fusion.5.refs_2_.p_ref), custom_call_target="tpu_custom_call" | custom-call | flops 1073741824 | tf_op jit(solution)/shard_map/pallas_call | solution.py:75
  80.7 4.5 %shard_map.87 = (f32[1024,512]{1,0:T(8,128)S(1)}, f32[1024,512]{1,0:T(8,128)S(1)}, f32[128,512]{1,0:T(8,128)S(1)}) custom-call(s32[4]{0:T(128)S(1)} %copy-done.5, bf16[32,2,16,1152]{3,2,1,0:T(8,128)(2,1)S(1)} %bitcast.69, bf16[1024,1024]{1,0:T(8,128)(2,1)S(1)} %constant_dynamic-update-slice_fusion.5.refs_2_.p_ref), custom_call_target="tpu_custom_call" | custom-call | flops 2147483648 | tf_op jit(solution)/shard_map/pallas_call | solution.py:75
  86.6 19.1 %all_to_all.15.refs_2_ = f32[32,2,512]{2,1,0:T(2,128)S(1)} all-to-all(f32[32,2,512]{2,1,0:T(2,128)S(1)} %broadcast_in_dim.41), channel_id=1, replica_groups=mesh['y'=4,'x'=4,'z'=8,'mp'=2] {'x','z'}, dimensions={0} | all-to-all | bytes 262144 | tf_op jit(solution)/shard_map/all_to_all | solution.py:24
  109.0 3.1 %shard_map.91.first_ref = bf16[512,1024]{1,0:T(8,128)(2,1)S(1)} custom-call(s32[4]{0:T(128)S(1)} %copy-done.5, bf16[1024,512]{1,0:T(8,128)(2,1)S(1)} %get-tuple-element.35.grad_ref, bf16[1024,1024]{1,0:T(8,128)(2,1)S(1)} %constant_dynamic-update-slice_fusion.5.refs_2_.p_ref), custom_call_target="tpu_custom_call" | custom-call | flops 1073741824 | tf_op jit(solution)/shard_map/pallas_call | solution.py:75
  112.0 3.4 %shard_map.92 = bf16[32,2,16,1024]{3,2,1,0:T(8,128)(2,1)S(1)} custom-call(s32[4]{0:T(128)S(1)} %copy-done.5, bf16[1024,512]{1,0:T(8,128)(2,1)S(1)} %collective-permute-done.14.grad_ref.other_ref, bf16[1024,1024]{1,0:T(8,128)(2,1)S(1)} %constant_dynamic-update-slice_fusion.5.refs_2_.p_ref, bf16[512,1024]{1,0:T(8,128)(2,1)S(1)} %shard_map.91.first_ref), custom_call_target="tpu_custom_call" | custom-call | flops 1073741824 | tf_op jit(solution)/shard_map/pallas_call | solution.py:75
  118.3 3.8 %shard_map.93 = bf16[1024,1024]{1,0:T(8,128)(2,1)S(1)} custom-call(s32[4]{0:T(128)S(1)} %copy-done.5, bf16[1024,512]{1,0:T(8,128)(2,1)S(1)} %get-tuple-element.35.grad_ref, bf16[1024,512]{1,0:T(8,128)(2,1)S(1)} %collective-permute-done.14.grad_ref.other_ref, bf16[32,2,16,1152]{3,2,1,0:T(8,128)(2,1)S(1)} %bitcast.70), custom_call_target="tpu_custom_call" | custom-call | flops 2147483648 | tf_op jit(solution)/shard_map/pallas_call | solution.py:75
  122.9 2.7 %collective-permute-start.23 = (bf16[128,1024]{1,0:T(8,128)(2,1)S(1)}, bf16[128,1024]{1,0:T(8,128)(2,1)S(1)}, u32[]{:S(2)}, u32[]{:S(2)}) collective-permute-start(bf16[128,1024]{1,0:T(8,128)(2,1)S(1)} %get-tuple-element.46), channel_id=1, source_target_pairs={{0,192},{64,0},{128,64},{192,128},{1,193},{65,1},{129,65},{193,129... | collective-permute-start | bytes 786440 | tf_op jit(solution)/shard_map/ppermute | solution.py:20
  126.0 2.7 %collective-permute-start.18 = (bf16[256,1024]{1,0:T(8,128)(2,1)S(1)}, bf16[256,1024]{1,0:T(8,128)(2,1)S(1)}, u32[]{:S(2)}, u32[]{:S(2)}) collective-permute-start(bf16[256,1024]{1,0:T(8,128)(2,1)S(1)} %pad_maximum_fusion.1), channel_id=1, source_target_pairs={{0,48},{16,0},{32,16},{48,32},{1,49},{17,1},{33,17},{49,33},{2,50}... | collective-permute-start | bytes 1572872 | tf_op jit(solution)/shard_map/ppermute | solution.py:20
  128.8 2.6 %collective-permute-done.21 = bf16[128,1024]{1,0:T(8,128)(2,1)S(1)} collective-permute-done((bf16[128,1024]{1,0:T(8,128)(2,1)S(1)}, bf16[128,1024]{1,0:T(8,128)(2,1)S(1)}, u32[]{:S(2)}, u32[]{:S(2)}) %collective-permute-start.21) | collective-permute-done | bytes 262176 | tf_op jit(solution)/shard_map/ppermute | solution.py:20
  132.4 7.1 %collective-permute-done.16 = bf16[256,1024]{1,0:T(8,128)(2,1)S(1)} collective-permute-done((bf16[256,1024]{1,0:T(8,128)(2,1)S(1)}, bf16[256,1024]{1,0:T(8,128)(2,1)S(1)}, u32[]{:S(2)}, u32[]{:S(2)}) %collective-permute-start.16) | collective-permute-done | bytes 524320 | tf_op jit(solution)/shard_map/ppermute | solution.py:20
  140.6 4.1 %all-to-all-start.2 = ((bf16[8,32,1024]{2,1,0:T(8,128)(2,1)}), bf16[8,32,1024]{2,1,0:T(8,128)(2,1)}, u32[]{:S(2)}, u32[]{:S(2)}) async-start(bf16[8,32,1024]{2,1,0:T(8,128)(2,1)} %bitcast.76), calls=%async_computation.2 | async-start | bytes 1048576 | tf_op jit(solution)/shard_map/all_to_all | solution.py:24
  149.4 8.9 %collective-permute-done.24 = bf16[256,1024]{1,0:T(8,128)(2,1)} collective-permute-done((bf16[256,1024]{1,0:T(8,128)(2,1)}, bf16[256,1024]{1,0:T(8,128)(2,1)}, u32[]{:S(2)}, u32[]{:S(2)}) %collective-permute-start.24) | collective-permute-done | bytes 524320 | tf_op jit(solution)/shard_map/ppermute | solution.py:20
  160.6 2.9 %collective-permute-start.25 = (bf16[256,1024]{1,0:T(8,128)(2,1)}, bf16[256,1024]{1,0:T(8,128)(2,1)S(1)}, u32[]{:S(2)}, u32[]{:S(2)}) collective-permute-start(bf16[256,1024]{1,0:T(8,128)(2,1)} %add_convert_fusion.pg_ref), channel_id=1, source_target_pairs={{0,1},{1,0},{2,3},{3,2},{4,5},{5,4},{6,7},{7,6},{8,9},{9,8},{10,11... | collective-permute-start | bytes 1572872 | tf_op jit(solution)/shard_map/ppermute | solution.py:20
  167.9 9.0 %shard_map.94 = (bf16[32,2048]{1,0:T(8,128)(2,1)}, bf16[256,2048]{1,0:T(8,128)(2,1)}) custom-call(s32[4]{0:T(128)} %pad_add_fusion.meta.refs_0_, f32[32,1024]{1,0:T(8,128)} %copy-done.8, f32[32,1024]{1,0:T(8,128)} %copy-done.11, f32[32,1024]{1,0:T(8,128)} %copy-done.2, f32[32,1024]{1,0:T(8,128)} %copy-done.10, f32[32,128]{1,0:T(8,128)} %copy-done.6, ...), custom_call_target="tpu_custom_call" | custom-call | flops 2415919104 | tf_op jit(solution)/shard_map/pallas_call | solution.py:75
  (126 shorter events, 44.9 us)
Async XLA Ops:
  9.6 7.8 %collective-permute-start.1 = (s32[32]{0:T(128)S(1)}, s32[32]{0:T(128)S(1)}, u32[]{:S(2)}, u32[]{:S(2)}) collective-permute-start(s32[32]{0:T(128)S(1)} %copy-done.13), channel_id=1, source_target_pairs={{0,64},{64,128},{128,192},{192,0},{1,65},{65,129},{129,193},{193,1... | collective-permute-start | bytes 392 | tf_op jit(solution)/shard_map/ppermute | solution.py:20
  22.6 25.8 %all-to-all-start = ((bf16[8,32,1152]{2,1,0:T(8,128)(2,1)}), bf16[8,32,1152]{2,1,0:T(8,128)(2,1)S(1)}, u32[]{:S(2)}, u32[]{:S(2)}) async-start(bf16[8,32,1152]{2,1,0:T(8,128)(2,1)} %broadcast_in_dim.40), calls=%async_computation | async-start | bytes 1179648 | tf_op jit(solution)/shard_map/all_to_all | solution.py:24
  30.8 12.8 %collective-permute-start.8 = (bf16[256,1024]{1,0:T(8,128)(2,1)S(1)}, bf16[256,1024]{1,0:T(8,128)(2,1)S(1)}, u32[]{:S(2)}, u32[]{:S(2)}) collective-permute-start(bf16[256,1024]{1,0:T(8,128)(2,1)S(1)} %get-tuple-element.28), channel_id=1, source_target_pairs={{0,64},{64,128},{128,192},{192,0},{1,65},{65,129},{129,193},{193,1... | collective-permute-start | bytes 1572872 | tf_op jit(solution)/shard_map/ppermute | solution.py:20
  31.2 13.2 %collective-permute-start.10 = (bf16[256,1024]{1,0:T(8,128)(2,1)S(1)}, bf16[256,1024]{1,0:T(8,128)(2,1)S(1)}, u32[]{:S(2)}, u32[]{:S(2)}) collective-permute-start(bf16[256,1024]{1,0:T(8,128)(2,1)S(1)} %get-tuple-element.28), channel_id=1, source_target_pairs={{0,192},{64,0},{128,64},{192,128},{1,193},{65,1},{129,65},{193,129... | collective-permute-start | bytes 1572872 | tf_op jit(solution)/shard_map/ppermute | solution.py:20
  44.4 9.9 %collective-permute-start.9 = (bf16[128,1024]{1,0:T(8,128)(2,1)}, bf16[128,1024]{1,0:T(8,128)(2,1)}, u32[]{:S(2)}, u32[]{:S(2)}) collective-permute-start(bf16[128,1024]{1,0:T(8,128)(2,1)} %slice.128), channel_id=1, source_target_pairs={{0,64},{64,128},{128,192},{192,0},{1,65},{65,129},{129,193},{193,1... | collective-permute-start | bytes 786440 | tf_op jit(solution)/shard_map/ppermute | solution.py:20
  45.1 10.1 %collective-permute-start.11 = (bf16[128,1024]{1,0:T(8,128)(2,1)}, bf16[128,1024]{1,0:T(8,128)(2,1)}, u32[]{:S(2)}, u32[]{:S(2)}) collective-permute-start(bf16[128,1024]{1,0:T(8,128)(2,1)} %slice.129), channel_id=1, source_target_pairs={{0,192},{64,0},{128,64},{192,128},{1,193},{65,1},{129,65},{193,129... | collective-permute-start | bytes 786440 | tf_op jit(solution)/shard_map/ppermute | solution.py:20
  48.5 13.4 %collective-permute-start.4 = (bf16[256,1152]{1,0:T(8,128)(2,1)S(1)}, bf16[256,1152]{1,0:T(8,128)(2,1)S(1)}, u32[]{:S(2)}, u32[]{:S(2)}) collective-permute-start(bf16[256,1152]{1,0:T(8,128)(2,1)S(1)} %bitcast.73), channel_id=1, source_target_pairs={{0,16},{16,32},{32,48},{48,0},{1,17},{17,33},{33,49},{49,1},{2,18}... | collective-permute-start | bytes 1769480 | tf_op jit(solution)/shard_map/ppermute | solution.py:20
  49.7 117.5 %collective-permute-start.27 = (bf16[4096,1024]{1,0:T(8,128)(2,1)}, bf16[4096,1024]{1,0:T(8,128)(2,1)}, u32[]{:S(2)}, u32[]{:S(2)}) collective-permute-start(bf16[4096,1024]{1,0:T(8,128)(2,1)} %w_ref.3), channel_id=1, source_target_pairs={{0,1},{1,0},{2,3},{3,2},{4,5},{5,4},{6,7},{7,6},{8,9},{9,8},{10,11... | collective-permute-start | bytes 25165832 | tf_op jit(solution)/shard_map/ppermute | solution.py:20
  52.8 15.0 %collective-permute-start.6 = (bf16[256,1152]{1,0:T(8,128)(2,1)S(1)}, bf16[256,1152]{1,0:T(8,128)(2,1)S(1)}, u32[]{:S(2)}, u32[]{:S(2)}) collective-permute-start(bf16[256,1152]{1,0:T(8,128)(2,1)S(1)} %bitcast.74), channel_id=1, source_target_pairs={{0,48},{16,0},{32,16},{48,32},{1,49},{17,1},{33,17},{49,33},{2,50}... | collective-permute-start | bytes 1769480 | tf_op jit(solution)/shard_map/ppermute | solution.py:20
  61.9 8.7 %collective-permute-start.5 = (bf16[128,1152]{1,0:T(8,128)(2,1)S(1)}, bf16[128,1152]{1,0:T(8,128)(2,1)S(1)}, u32[]{:S(2)}, u32[]{:S(2)}) collective-permute-start(bf16[128,1152]{1,0:T(8,128)(2,1)S(1)} %slice.126), channel_id=1, source_target_pairs={{0,16},{16,32},{32,48},{48,0},{1,17},{17,33},{33,49},{49,1},{2,18}... | collective-permute-start | bytes 884744 | tf_op jit(solution)/shard_map/ppermute | solution.py:20
  67.8 8.3 %collective-permute-start.7 = (bf16[128,1152]{1,0:T(8,128)(2,1)S(1)}, bf16[128,1152]{1,0:T(8,128)(2,1)S(1)}, u32[]{:S(2)}, u32[]{:S(2)}) collective-permute-start(bf16[128,1152]{1,0:T(8,128)(2,1)S(1)} %slice.127), channel_id=1, source_target_pairs={{0,48},{16,0},{32,16},{48,32},{1,49},{17,1},{33,17},{49,33},{2,50}... | collective-permute-start | bytes 884744 | tf_op jit(solution)/shard_map/ppermute | solution.py:20
  78.8 6.4 %collective-permute-start.12 = (f32[1024,512]{1,0:T(8,128)S(1)}, f32[1024,512]{1,0:T(8,128)S(1)}, u32[]{:S(2)}, u32[]{:S(2)}) collective-permute-start(f32[1024,512]{1,0:T(8,128)S(1)} %shard_map.88), channel_id=1, source_target_pairs={{0,1},{1,0},{2,3},{3,2},{4,5},{5,4},{6,7},{7,6},{8,9},{9,8},{10,11... | collective-permute-start | bytes 6291464 | tf_op jit(solution)/shard_map/ppermute | solution.py:20
  115.6 10.1 %collective-permute-start.15 = (bf16[128,1024]{1,0:T(8,128)(2,1)S(1)}, bf16[128,1024]{1,0:T(8,128)(2,1)S(1)}, u32[]{:S(2)}, u32[]{:S(2)}) collective-permute-start(bf16[128,1024]{1,0:T(8,128)(2,1)S(1)} %get-tuple-element.51), channel_id=1, source_target_pairs={{0,16},{16,32},{32,48},{48,0},{1,17},{17,33},{33,49},{49,1},{2,18}... | collective-permute-start | bytes 786440 | tf_op jit(solution)/shard_map/ppermute | solution.py:20
  116.0 9.7 %collective-permute-start.17 = (bf16[128,1024]{1,0:T(8,128)(2,1)S(1)}, bf16[128,1024]{1,0:T(8,128)(2,1)S(1)}, u32[]{:S(2)}, u32[]{:S(2)}) collective-permute-start(bf16[128,1024]{1,0:T(8,128)(2,1)S(1)} %get-tuple-element.52), channel_id=1, source_target_pairs={{0,48},{16,0},{32,16},{48,32},{1,49},{17,1},{33,17},{49,33},{2,50}... | collective-permute-start | bytes 786440 | tf_op jit(solution)/shard_map/ppermute | solution.py:20
  122.9 8.5 %collective-permute-start.21 = (bf16[128,1024]{1,0:T(8,128)(2,1)S(1)}, bf16[128,1024]{1,0:T(8,128)(2,1)S(1)}, u32[]{:S(2)}, u32[]{:S(2)}) collective-permute-start(bf16[128,1024]{1,0:T(8,128)(2,1)S(1)} %get-tuple-element.45), channel_id=1, source_target_pairs={{0,64},{64,128},{128,192},{192,0},{1,65},{65,129},{129,193},{193,1... | collective-permute-start | bytes 786440 | tf_op jit(solution)/shard_map/ppermute | solution.py:20
  122.9 8.5 %collective-permute-start.23 = (bf16[128,1024]{1,0:T(8,128)(2,1)S(1)}, bf16[128,1024]{1,0:T(8,128)(2,1)S(1)}, u32[]{:S(2)}, u32[]{:S(2)}) collective-permute-start(bf16[128,1024]{1,0:T(8,128)(2,1)S(1)} %get-tuple-element.46), channel_id=1, source_target_pairs={{0,192},{64,0},{128,64},{192,128},{1,193},{65,1},{129,65},{193,129... | collective-permute-start | bytes 786440 | tf_op jit(solution)/shard_map/ppermute | solution.py:20
  125.9 13.7 %collective-permute-start.16 = (bf16[256,1024]{1,0:T(8,128)(2,1)S(1)}, bf16[256,1024]{1,0:T(8,128)(2,1)S(1)}, u32[]{:S(2)}, u32[]{:S(2)}) collective-permute-start(bf16[256,1024]{1,0:T(8,128)(2,1)S(1)} %pad_maximum_fusion), channel_id=1, source_target_pairs={{0,16},{16,32},{32,48},{48,0},{1,17},{17,33},{33,49},{49,1},{2,18}... | collective-permute-start | bytes 1572872 | tf_op jit(solution)/shard_map/ppermute | solution.py:20
  126.0 13.5 %collective-permute-start.18 = (bf16[256,1024]{1,0:T(8,128)(2,1)S(1)}, bf16[256,1024]{1,0:T(8,128)(2,1)S(1)}, u32[]{:S(2)}, u32[]{:S(2)}) collective-permute-start(bf16[256,1024]{1,0:T(8,128)(2,1)S(1)} %pad_maximum_fusion.1), channel_id=1, source_target_pairs={{0,48},{16,0},{32,16},{48,32},{1,49},{17,1},{33,17},{49,33},{2,50}... | collective-permute-start | bytes 1572872 | tf_op jit(solution)/shard_map/ppermute | solution.py:20
  132.4 16.6 %collective-permute-start.22 = (bf16[256,1024]{1,0:T(8,128)(2,1)}, bf16[256,1024]{1,0:T(8,128)(2,1)}, u32[]{:S(2)}, u32[]{:S(2)}) collective-permute-start(bf16[256,1024]{1,0:T(8,128)(2,1)} %pad_maximum_fusion.2), channel_id=1, source_target_pairs={{0,64},{64,128},{128,192},{192,0},{1,65},{65,129},{129,193},{193,1... | collective-permute-start | bytes 1572872 | tf_op jit(solution)/shard_map/ppermute | solution.py:20
  140.6 22.9 %all-to-all-start.2 = ((bf16[8,32,1024]{2,1,0:T(8,128)(2,1)}), bf16[8,32,1024]{2,1,0:T(8,128)(2,1)}, u32[]{:S(2)}, u32[]{:S(2)}) async-start(bf16[8,32,1024]{2,1,0:T(8,128)(2,1)} %bitcast.76), calls=%async_computation.2 | async-start | bytes 1048576 | tf_op jit(solution)/shard_map/all_to_all | solution.py:24
  146.6 11.8 %collective-permute-start.24 = (bf16[256,1024]{1,0:T(8,128)(2,1)}, bf16[256,1024]{1,0:T(8,128)(2,1)}, u32[]{:S(2)}, u32[]{:S(2)}) collective-permute-start(bf16[256,1024]{1,0:T(8,128)(2,1)} %pad_maximum_fusion.3), channel_id=1, source_target_pairs={{0,192},{64,0},{128,64},{192,128},{1,193},{65,1},{129,65},{193,129... | collective-permute-start | bytes 1572872 | tf_op jit(solution)/shard_map/ppermute | solution.py:20
  146.8 19.7 %collective-permute-start.26 = (f32[256,1024]{1,0:T(8,128)S(1)}, f32[256,1024]{1,0:T(8,128)}, u32[]{:S(2)}, u32[]{:S(2)}) collective-permute-start(f32[256,1024]{1,0:T(8,128)S(1)} %get-tuple-element.38.pu_ref), channel_id=1, source_target_pairs={{0,1},{1,0},{2,3},{3,2},{4,5},{5,4},{6,7},{7,6},{8,9},{9,8},{10,11... | collective-permute-start | bytes 3145736 | tf_op jit(solution)/shard_map/ppermute | solution.py:20
  148.8 17.7 %collective-permute-start.20 = (f32[32,1024]{1,0:T(8,128)S(1)}, f32[32,1024]{1,0:T(8,128)S(1)}, u32[]{:S(2)}, u32[]{:S(2)}) collective-permute-start(f32[32,1024]{1,0:T(8,128)S(1)} %get-tuple-element.36.qu_ref), channel_id=1, source_target_pairs={{0,1},{1,0},{2,3},{3,2},{4,5},{5,4},{6,7},{7,6},{8,9},{9,8},{10,11... | collective-permute-start | bytes 393224 | tf_op jit(solution)/shard_map/ppermute | solution.py:20
  149.0 16.8 %collective-permute-start.13 = (f32[16]{0:T(128)S(1)}, f32[16]{0:T(128)S(1)}, u32[]{:S(2)}, u32[]{:S(2)}) collective-permute-start(f32[16]{0:T(128)S(1)} %dynamic-slice_bitcast_fusion), channel_id=1, source_target_pairs={{0,1},{1,0},{2,3},{3,2},{4,5},{5,4},{6,7},{7,6},{8,9},{9,8},{10,11... | collective-permute-start | bytes 200 | tf_op jit(solution)/shard_map/ppermute | solution.py:20
  (21 other events, 401.7 us)

commit v3 on v0

v3 whole, which is shorter than its diff:
```python
import jax
import jax.numpy as jnp
from jax import lax
from jax.experimental import pallas as pl
from jax.experimental.pallas import tpu as pltpu
from jax.sharding import Mesh, PartitionSpec as P

sharpness = 1.0 / 0.02
bf16 = jnp.bfloat16
f32 = jnp.float32
AUX = 128
TILE = 256
CHUNK = 512
INDEX = 16
MIB = 1024 * 1024
SHAPES = {128: (4, 4, 8), 32: (4, 4, 2), 8: (2, 2, 2)}


def shifted(value, axis, shift):
    n = lax.axis_size(axis)
    return lax.ppermute(value, axis, [(i, (i + shift) % n) for i in range(n)])


def exchanged(parts, axis):
    return lax.all_to_all(parts, axis, split_axis=0, concat_axis=0, tiled=True)


def to_all(value, axis):
    n = lax.axis_size(axis)
    return exchanged(jnp.broadcast_to(value[None], (n,) + value.shape), axis)


def after(value, *others):
    return lax.optimization_barrier((value, *others))[0]


def ring_near(value, axis):
    shifts = (1, -1) if lax.axis_size(axis) > 2 else (1,)
    return [shifted(value, axis, shift) for shift in shifts]


def ring_far(value, near, axis):
    if len(near) == 1:
        return [value] + near
    cut = value.shape[0] // 2
    before, behind = near
    return [value, before, shifted(before[:cut], axis, 1), shifted(behind[cut:], axis, -1), behind]


def return_first(pieces, axis, gate=None):
    if len(pieces) == 2:
        return [pieces[1]]
    up, down = shifted(pieces[2], axis, 1), shifted(pieces[3], axis, -1)
    if gate is not None:
        up = after(up, gate)
    return join(pieces[4], up, pieces[1], down)


def return_second(pieces, leaving, axis):
    coming = [shifted(value, axis, shift) for shift, value in zip((1, -1), leaving)]
    return total([pieces[0]] + coming, bf16)


def split_three(value):
    high = lax.reduce_precision(value, 8, 7)
    rest = value - high
    middle = lax.reduce_precision(rest, 8, 7)
    return high, middle, rest - middle


def contract(a, b, dims):
    return lax.dot_general(a, b, (dims, ((), ())), preferred_element_type=f32)


def struct(shape, dtype=f32):
    return jax.ShapeDtypeStruct(shape, dtype)


def call(body, args, outs, scratch=(), flops=0, hbm=(), free=(), vmem=8, loose=False):
    specs, operands = [], []
    for i, arg in enumerate(args):
        if i == 0:
            specs.append(pl.BlockSpec(memory_space=pltpu.SMEM))
        elif i in hbm:
            specs.append(pl.BlockSpec(memory_space=pl.ANY))
            arg = pltpu.with_memory_space_constraint(arg, pltpu.HBM)
        else:
            specs.append(pl.BlockSpec(memory_space=pltpu.VMEM))
            arg = arg if loose else pltpu.with_memory_space_constraint(arg, pltpu.VMEM)
        operands.append(arg)
    kept = [s if loose or i in free else pltpu.VMEM(s.shape, s.dtype) for i, s in enumerate(outs)]
    return pl.pallas_call(
        body,
        in_specs=specs,
        out_specs=[pl.BlockSpec(memory_space=pltpu.VMEM)] * len(outs),
        out_shape=kept,
        scratch_shapes=list(scratch),
        compiler_params=pltpu.CompilerParams(vmem_limit_bytes=vmem * 1024 * 1024),
        cost_estimate=pl.CostEstimate(flops=flops, bytes_accessed=0, transcendentals=0),
    )(*operands)


def row_of_lane_sums(block):
    return jnp.sum(block.T, axis=0, keepdims=True)


def lanes_to_rows(row):
    return jnp.broadcast_to(row, (128, row.shape[1])).T


def rem(value, n):
    return lax.rem(value, jnp.int32(n))


def spans(rows, size):
    return [slice(at, min(at + size, rows)) for at in range(0, rows, size)]


def pieces_at(pieces):
    at = 0
    for piece in pieces:
        yield slice(at, at + piece.shape[0]), piece
        at += piece.shape[0]


def row_index(rows, columns, start=0):
    return (lax.broadcasted_iota(jnp.int32, (rows, columns), 0) + start).astype(f32)


def total_body(meta, *refs):
    value = refs[0][...].astype(f32)
    for ref in refs[1:-1]:
        value = value + ref[...].astype(f32)
    refs[-1][...] = value.astype(refs[-1].dtype)


def total(parts, dtype):
    meta = jnp.zeros((1,), jnp.int32)
    return call(total_body, [meta] + list(parts), [struct(parts[0].shape, dtype)], loose=True)[0]


def total_slots_body(size, meta, ref, loss_ref, out_ref):
    value = ref[0].astype(f32)
    for s in range(1, ref.shape[0]):
        value = value + ref[s].astype(f32)
    n = value.shape[0]
    out_ref[:n] = value
    own = loss_ref[0:1, :size]
    own = pltpu.roll(own, rem(size - meta[4], size), 1)
    out_ref[n:] = jnp.zeros((8, value.shape[1]), f32)
    out_ref[n : n + 1, :size] = own


def total_slots(meta, stacked, loss, size):
    def body(*refs):
        total_slots_body(size, *refs)

    shape = (stacked.shape[1] + 8, stacked.shape[2])
    return call(body, [meta, stacked, loss], [struct(shape)], loose=True)[0]


def join_body(meta, ahead_ref, up_ref, behind_ref, down_ref, ahead_out, behind_out):
    cut = up_ref.shape[0]
    ahead_out[:cut] = (ahead_ref[:cut].astype(f32) + up_ref[...].astype(f32)).astype(bf16)
    ahead_out[cut:] = ahead_ref[cut:]
    behind_out[:cut] = behind_ref[:cut]
    behind_out[cut:] = (behind_ref[cut:].astype(f32) + down_ref[...].astype(f32)).astype(bf16)


def join(ahead, up, behind, down):
    meta = jnp.zeros((1,), jnp.int32)
    shape = struct(ahead.shape, bf16)
    return call(join_body, [meta, ahead, up, behind, down], [shape, shape], loose=True)


def project_body(
    meta, q_ref, p_ref, w_ref, qo_ref, po_ref, square_ref, x_ref, acc_ref, head_ref, sems
):
    n_q = q_ref.shape[0]
    depth, width = w_ref.shape
    chunk = min(CHUNK, depth)
    loads = [
        pltpu.make_async_copy(q_ref, x_ref.at[pl.ds(0, n_q)], sems.at[0]),
        pltpu.make_async_copy(p_ref, x_ref.at[pl.ds(n_q, p_ref.shape[0])], sems.at[1]),
    ]
    blocks = []
    for at in spans(depth, chunk):
        rows = pl.ds(at.start, chunk)
        blocks.append(pltpu.make_async_copy(w_ref.at[rows], head_ref.at[rows], sems.at[2 + len(blocks)]))
    for load in loads:
        load.start()
    for block in blocks:
        block.start()
    for load in loads:
        load.wait()
    for i, at in enumerate(spans(depth, chunk)):
        blocks[i].wait()
        part = contract(x_ref[:, at], head_ref[at], ((1,), (0,)))
        acc_ref[...] = part if i == 0 else acc_ref[...] + part
    qo_ref[...] = acc_ref[:n_q]
    po_ref[...] = acc_ref[n_q:]
    square = jnp.zeros((acc_ref.shape[0], 128), f32)
    for at in range(0, width, 128):
        block = acc_ref[:, at : at + 128]
        square = square + block * block
    padded = jnp.concatenate([square[:n_q], jnp.zeros((128 - n_q, 128), f32)], axis=0)
    square_ref[:, :128] = row_of_lane_sums(padded)
    square_ref[:, 128:] = row_of_lane_sums(square[n_q:])


def project(meta, queries, passages, weight):
    n_q, n_p, (depth, width) = queries.shape[0], passages.shape[0], weight.shape
    copies = 2 + depth // min(CHUNK, depth)
    return call(
        project_body,
        [meta, queries, passages, weight],
        [struct((n_q, width)), struct((n_p, width)), struct((1, 128 + n_p))],
        [
            pltpu.VMEM((n_q + n_p, depth), bf16),
            pltpu.VMEM((n_q + n_p, width), f32),
            pltpu.VMEM((depth, width), bf16),
            pltpu.SemaphoreType.DMA((copies,)),
        ],
        2 * (n_q + n_p) * depth * width,
        hbm=(1, 2, 3),
        vmem=18,
    )


def normalize_body(
    meta, q_ref, p_ref, own_ref, got_ref, aux_ref, message_ref, unit_ref, embed_ref, inv_ref
):
    n_q, width = q_ref.shape
    inv = lanes_to_rows(lax.rsqrt(own_ref[...] + got_ref[...] + 1e-06))
    inv_ref[:n_q] = inv[:n_q]
    inv_ref[n_q:] = inv[128:]
    q_unit = q_ref[...] * inv[:n_q, :1]
    p_unit = p_ref[...] * inv[128:, :1]
    unit_ref[:n_q] = q_unit
    unit_ref[n_q:] = p_unit
    embed_ref[...] = p_unit.astype(bf16)
    half = n_q // 2
    first = meta[0] == 0

    def store(columns, value):
        top, bottom = value[:half], value[half:]
        message_ref[:half, columns] = jnp.where(first, top, bottom).astype(bf16)
        message_ref[half:, columns] = jnp.where(first, bottom, top).astype(bf16)

    store(slice(0, width), q_unit)
    store(slice(width, width + AUX), aux_ref[...])


def normalize(meta, q_proj, p_proj, square, square_got, aux):
    (n_q, width), n_p = q_proj.shape, p_proj.shape[0]
    return call(
        normalize_body,
        [meta, q_proj, p_proj, square, square_got, aux],
        [
            struct((n_q, width + AUX), bf16),
            struct((n_q + n_p, width)),
            struct((n_p, width), bf16),
            struct((n_q + n_p, 128)),
        ],
    )


def owner_of(meta, line, n_y, slots):
    return (rem(meta[3] - line + n_y, n_y) * slots + meta[1]).astype(f32)


def score_sent_body(n_pieces, meta, *refs):
    q_refs, p_refs = refs[:n_pieces[0]], refs[n_pieces[0] : sum(n_pieces)]
    score_ref, own_ref, other_ref, all_ref, aux_ref, aux_other_ref = refs[sum(n_pieces) :]
    width = own_ref.shape[1]
    at = 0
    for ref in q_refs:
        value = ref[...].reshape(-1, 2, 16, ref.shape[1])
        rows = value.shape[0] * 16
        for i, (to_ref, aux) in enumerate(((own_ref, aux_ref), (other_ref, aux_other_ref))):
            side = value[:, i].reshape(rows, -1)
            to_ref[at : at + rows] = side[:, :width]
            aux[at : at + rows] = side[:, width:].astype(f32)
        at += rows
    for at, ref in pieces_at(p_refs):
        all_ref[at] = ref[...]
        score_ref[at] = contract(ref[...], other_ref[...], ((1,), (1,)))


def score_sent(meta, q_pieces, p_pieces):
    width = p_pieces[0].shape[1]
    passages = sum(p.shape[0] for p in p_pieces)
    rows = sum(q.shape[0] for q in q_pieces) // 2

    def body(*refs):
        score_sent_body((len(q_pieces), len(p_pieces)), *refs)

    return call(
        body,
        [meta] + q_pieces + p_pieces,
        [
            struct((passages, rows)),
            struct((rows, width), bf16),
            struct((rows, width), bf16),
            struct((passages, width), bf16),
            struct((rows, AUX)),
            struct((rows, AUX)),
        ],
        flops=2 * rows * passages * width,
    )


def count_body(slots, meta, aux_ref, other_ref, info_ref, count_ref):
    block = count_ref.shape[1]
    info_ref[...] = aux_ref[...].T
    owners = (lax.broadcasted_iota(jnp.int32, (8, 1), 0) * slots + meta[1]).astype(f32)
    count = jnp.zeros(count_ref.shape, f32)
    for info in (info_ref[...], other_ref[...].T):
        owned = (info[0:1] == owners).astype(f32).astype(bf16)
        placed = info[INDEX : INDEX + 1] == row_index(block, info.shape[1])
        count = count + contract(owned, placed.astype(f32).astype(bf16), ((1,), (1,)))
    count_ref[...] = count


def count_positives(meta, aux, aux_other, block, slots):
    def body(*refs):
        count_body(slots, *refs)

    return call(
        body, [meta, aux, aux_other], [struct((AUX, aux.shape[0])), struct((8, block))]
    )


def score_kept_body(n_y, slots, per_query, meta, q_ref, p_ref, info_ref, score_ref, weight_ref):
    passages, rows = score_ref.shape
    block = passages // n_y
    for line in range(n_y):
        owner = owner_of(meta, line, n_y, slots)
        place = jnp.where(info_ref[:INDEX] == owner, info_ref[INDEX : 2 * INDEX], -1.0)
        at = slice(line * block, (line + 1) * block)
        score_ref[at] = contract(p_ref[at], q_ref[...], ((1,), (1,)))
        for span in spans(block, 32):
            row = row_index(span.stop - span.start, rows, span.start)
            weight = (place[1:2] == row).astype(f32)
            for k in range(2, per_query):
                weight = weight + (place[k : k + 1] == row).astype(f32)
            weight_ref[line * block + span.start : line * block + span.stop] = weight


def score_kept(meta, q_own, p_all, info, n_y, slots, per_query):
    passages, rows = p_all.shape[0], q_own.shape[0]

    def body(*refs):
        score_kept_body(n_y, slots, per_query, *refs)

    return call(
        body,
        [meta, q_own, p_all, info],
        [struct((passages, rows)), struct((passages, rows))],
        flops=4 * rows * passages * p_all.shape[1],
    )


def positive_place(meta, line, n_y, slots, info_ref):
    owner = owner_of(meta, line, n_y, slots)
    return jnp.where(info_ref[0:1] == owner, info_ref[INDEX : INDEX + 1], -1.0)


def turned_slots(meta, n_x, rows):
    size = rows // n_x
    for s in range(n_x):
        start = pl.multiple_of(rem(meta[2] - s + n_x, n_x) * size, size)
        yield slice(s * size, (s + 1) * size), pl.ds(start, size)


def weigh_body(
    n_y, n_x, slots, meta, kept_ref, got_ref, weight_ref, info_ref, *rest_refs
):
    counts_ref, (e_ref, sum_ref) = rest_refs[:-2], rest_refs[-2:]
    passages, rows = kept_ref.shape
    block = passages // n_y
    counts = counts_ref[0][...]
    for ref in counts_ref[1:]:
        counts = counts + ref[...]
    rest = jnp.zeros((128 - counts.shape[0], block), f32)
    counts = jnp.concatenate([counts, rest], axis=0).T
    lane = lax.broadcasted_iota(jnp.int32, (1, 128), 1)
    sums = [jnp.zeros((8, rows), f32), jnp.zeros((8, rows), f32)]
    for line in range(n_y):
        mine = lane == rem(meta[3] - line + n_y, n_y)
        count = jnp.sum(jnp.where(mine, counts, 0.0), axis=1, keepdims=True)
        place = positive_place(meta, line, n_y, slots, info_ref)
        for span in spans(block, 32):
            at = slice(line * block + span.start, line * block + span.stop)
            score = (kept_ref[at] + got_ref[at]) * sharpness
            weighted = (weight_ref[at] + count[span]) * jnp.exp(score)
            e_ref[at] = weighted
            own = jnp.where(place == row_index(span.stop - span.start, rows, span.start), score, 0.0)
            sums[0] = sums[0] + jnp.sum(weighted.reshape(-1, 8, rows), axis=0)
            sums[1] = sums[1] + jnp.sum(own.reshape(-1, 8, rows), axis=0)
    for i in range(2):
        row = jnp.sum(sums[i], axis=0, keepdims=True)
        for here, there in turned_slots(meta, n_x, rows):
            sum_ref[i : i + 1, there] = row[:, here]


def weigh(meta, kept, got, weight, info, counts, n_y, n_x, slots):
    passages, rows = kept.shape

    def body(*refs):
        weigh_body(n_y, n_x, slots, *refs)

    return call(
        body,
        [meta, kept, got, weight, info, *counts],
        [struct((passages, rows)), struct((2, rows))],
    )


def slope_body(n_y, n_x, slots, meta, e_ref, sums_ref, info_ref, grad_ref, loss_ref, scale_ref, inv_ref):
    passages, rows = e_ref.shape
    block = passages // n_y
    loss_ref[...] = jnp.sum(sums_ref[...], axis=0)
    for here, there in turned_slots(meta, n_x, rows):
        inv_ref[:, here] = loss_ref[0:1, there]
    for here, there in turned_slots(meta, n_x, rows):
        scale_ref[:, here] = loss_ref[1:2, there]
    sums = inv_ref[...]
    loss_ref[0:1] = jnp.log(sums) - scale_ref[...]
    inv = 1.0 / sums
    base = 2 * INDEX
    scale = (info_ref[base : base + 1] + info_ref[base + 1 : base + 2]) + info_ref[base + 2 : base + 3]
    scale = scale * sharpness
    for line in range(n_y):
        place = positive_place(meta, line, n_y, slots, info_ref)
        for span in spans(block, 32):
            at = slice(line * block + span.start, line * block + span.stop)
            match = (place == row_index(span.stop - span.start, rows, span.start)).astype(f32)
            grad_ref[at] = (scale * (e_ref[at] * inv - match)).astype(bf16)


def slopes(meta, e, sums, info, n_y, n_x, slots):
    passages, rows = e.shape

    def body(*refs):
        slope_body(n_y, n_x, slots, *refs)

    return call(
        body,
        [meta, e, sums, info],
        [struct((passages, rows), bf16), struct((2, rows))],
        [pltpu.VMEM((1, rows), f32), pltpu.VMEM((1, rows), f32)],
    )


def query_part_body(meta, grad_ref, p_ref, out_ref, turned_ref):
    turned_ref[...] = grad_ref[...].T
    for at in spans(p_ref.shape[1], TILE):
        out_ref[:, at] = contract(turned_ref[...], p_ref[:, at], ((1,), (0,))).astype(bf16)


def query_part(meta, grad, p_all):
    (passages, rows), width = grad.shape, p_all.shape[1]
    return call(
        query_part_body,
        [meta, grad, p_all],
        [struct((rows, width), bf16)],
        [pltpu.VMEM((rows, passages), bf16)],
        2 * rows * passages * width,
    )[0]


def query_rest_body(meta, grad_ref, p_ref, first_ref, *refs):
    out_refs, turned_ref = refs[:-1], refs[-1]
    turned_ref[...] = grad_ref[...].T
    for span in spans(p_ref.shape[1], TILE):
        rest = contract(turned_ref[...], p_ref[:, span], ((1,), (0,))).astype(bf16)
        at = 0
        for ref in out_refs:
            rows = ref.shape[0] * 16
            for i, value in enumerate((first_ref[at : at + rows, span], rest[at : at + rows])):
                ref[:, i, :, span] = value.reshape(-1, 16, value.shape[1])
            at += rows


def query_rest(meta, grad, p_all, first, shapes):
    (passages, rows), width = grad.shape, p_all.shape[1]
    return call(
        query_rest_body,
        [meta, grad, p_all, first],
        [struct((n // 32, 2, 16, width), bf16) for n in shapes],
        [pltpu.VMEM((rows, passages), bf16)],
        2 * rows * passages * width,
    )


def passage_part_body(meta, grad_ref, other_ref, own_ref, q_ref, *out_refs):
    for at, ref in pieces_at(out_refs):
        value = contract(grad_ref[at], own_ref[...], ((1,), (0,)))
        value = value + contract(other_ref[at], q_ref[...], ((1,), (0,)))
        ref[...] = value.astype(bf16)


def passage_part(meta, grad, other, q_own, q_other, shapes):
    (passages, rows), width = grad.shape, q_own.shape[1]
    return call(
        passage_part_body,
        [meta, grad, other, q_own, q_other],
        [struct((n, width), bf16) for n in shapes],
        flops=4 * rows * passages * width,
    )


def tangent(grad, other, unit, beyond, inv):
    radial = jnp.sum(unit * grad + beyond * other, axis=1, keepdims=True)
    return (inv * (grad - unit * radial)).astype(bf16), (inv * (other - beyond * radial)).astype(bf16)


def finish_body(
    meta, qg_ref, qgo_ref, pg_ref, pgo_ref, unit_ref, beyond_ref, inv_ref, w_hbm, wo_hbm,
    q_out, p_out, loss_out, here_ref, there_ref, w_ref, wo_ref, sems
):
    half = w_ref.shape[0]
    blocks = spans(half, CHUNK)
    loads = []
    for i, at in enumerate(blocks):
        size, to = at.stop - at.start, pl.ds(at.start, at.stop - at.start)
        rows = pl.ds(pl.multiple_of(meta[0] * half + at.start, size), size)
        loads.append(pltpu.make_async_copy(w_hbm.at[rows], w_ref.at[to], sems.at[2 * i]))
        loads.append(pltpu.make_async_copy(wo_hbm.at[rows], wo_ref.at[to], sems.at[2 * i + 1]))
    for load in loads:
        load.start()
    n_q = q_out.shape[0]
    part = n_q // 2
    first = meta[0] == 0
    turn = lambda rows: jnp.concatenate([rows[part:], rows[:part]], axis=0)
    grad, other = qg_ref[:n_q], qgo_ref[:n_q]
    grad, other = jnp.where(first, grad, turn(grad)), jnp.where(first, turn(other), other)
    here_ref[:n_q], there_ref[:n_q] = tangent(
        grad, other, unit_ref[:n_q], beyond_ref[:n_q], inv_ref[:n_q, :1]
    )
    own, got = qg_ref[n_q : n_q + 1, :128], qgo_ref[n_q : n_q + 1, :128]
    low, high = jnp.where(first, own, got), jnp.where(first, got, own)
    lane = lax.broadcasted_iota(jnp.int32, (1, 128), 1)
    loss_out[...] = jnp.where(lane < part, low, pltpu.roll(high, part, 1))
    for at in spans(pg_ref.shape[0], 64):
        to = slice(n_q + at.start, n_q + at.stop)
        here_ref[to], there_ref[to] = tangent(
            pg_ref[at].astype(f32), pgo_ref[at].astype(f32), unit_ref[to], beyond_ref[to], inv_ref[to, :1]
        )
    for i, at in enumerate(blocks):
        loads[2 * i].wait()
        loads[2 * i + 1].wait()
        state = contract(here_ref[...], w_ref[at], ((1,), (1,)))
        state = (state + contract(there_ref[...], wo_ref[at], ((1,), (1,)))).astype(bf16)
        q_out[:, at] = state[:n_q]
        p_out[:, at] = state[n_q:]


def finish(meta, rows_in, weight, weight_got):
    depth, width = weight.shape
    n, n_p, out_width = rows_in[4].shape[0], rows_in[2].shape[0], depth // 2
    copies = 2 * len(spans(out_width, CHUNK))
    return call(
        finish_body,
        [meta, *rows_in, weight, weight_got],
        [struct((n - n_p, out_width), bf16), struct((n_p, out_width), bf16), struct((1, 128))],
        [
            pltpu.VMEM((n, width), bf16),
            pltpu.VMEM((n, width), bf16),
            pltpu.VMEM((out_width, width), bf16),
            pltpu.VMEM((out_width, width), bf16),
            pltpu.SemaphoreType.DMA((copies,)),
        ],
        4 * n * out_width * width,
        hbm=(8, 9),
        free=(0, 1, 2),
        vmem=20,
    )


def per_device(query_states, passage_states, head_weight, positives, negatives, slope):
    n_y, n_x, n_z = (lax.axis_size(a) for a in ("y", "x", "z"))
    y, x, z, core = (lax.axis_index(a) for a in ("y", "x", "z", "mp"))
    q_rows, p_rows = query_states.shape[0], passage_states.shape[0]
    width = head_weight.shape[1]
    half = q_rows // 2
    slots = n_x * n_z
    column = x * n_z + z
    meta = jnp.stack([core, column, x, y, z * half]).astype(jnp.int32)

    q_proj, p_proj, square = project(meta, query_states, passage_states, head_weight)
    square_got = shifted(square, "mp", 1)
    ids = jnp.concatenate([positives[:, None], negatives], axis=1)
    per_query = ids.shape[1]
    padded = ((0, 0), (0, INDEX - per_query))
    aux = jnp.concatenate(
        [jnp.pad((ids // p_rows).astype(f32), padded), jnp.pad((ids % p_rows).astype(f32), padded)]
        + [part[:, None] for part in split_three(slope)],
        axis=1,
    )
    aux = jnp.pad(aux, ((0, 0), (0, AUX - aux.shape[1])))
    message, unit, p_embed, inv = normalize(
        meta, q_proj, p_proj, square, square_got, aux
    )
    unit_got = shifted(unit, "mp", 1)
    weight_got = shifted(after(head_weight, unit), "mp", 1)
    p_near = ring_near(p_embed, "y")
    q_z = to_all(message, "z").reshape(n_z * q_rows, width + AUX)
    q_z = after(q_z, unit_got, weight_got, *p_near)
    q_near = ring_near(q_z, "x")
    q_pieces = ring_far(q_z, q_near, "x")
    p_pieces = ring_far(p_embed, [after(piece, *q_near) for piece in p_near], "y")
    q_shapes, p_shapes = ([piece.shape[0] for piece in pieces] for pieces in (q_pieces, p_pieces))
    sent, q_own, q_other, p_all, aux, aux_other = score_sent(meta, q_pieces, p_pieces)
    got = shifted(sent, "mp", 1)
    info, count = count_positives(meta, aux, aux_other, p_rows, slots)
    counts = [count] + [shifted(count, "y", s) for s in range(1, n_y)]
    kept, named = score_kept(meta, q_own, p_all, info, n_y, slots, per_query)
    e, sums = weigh(meta, kept, got, named, info, counts, n_y, n_x, slots)
    sums = to_all(sums, ("x", "z")).reshape((slots,) + sums.shape)
    grad, loss = slopes(meta, e, sums, info, n_y, n_x, slots)
    grad_got = shifted(grad, "mp", 1)
    q_part = query_part(meta, grad, p_all)
    grad_got = after(grad_got, q_part)
    p_parts = passage_part(meta, grad, grad_got, q_own, q_other, p_shapes)
    q_parts = query_rest(meta, grad_got, p_all, q_part, q_shapes)
    p_leaving = return_first(p_parts, "y", q_parts[0])
    q_leaving = return_first([part.reshape(-1, width) for part in q_parts], "x")
    p_grad = return_second(p_parts, p_leaving, "y")
    p_grad_got = shifted(p_grad, "mp", 1)
    q_part = return_second([part.reshape(-1, width) for part in q_parts], q_leaving, "x")
    q_part = after(q_part, p_grad_got)
    back = exchanged(q_part.reshape(n_z, q_rows, width), "z")
    q_grad = total_slots(meta, back, loss, n_z * half)
    q_grad_got = shifted(q_grad, "mp", 1)
    query_grads, passage_grads, losses = finish(
        meta, (q_grad, q_grad_got, p_grad, p_grad_got, unit, unit_got, inv), head_weight, weight_got
    )
    return losses[0, :q_rows], query_grads, passage_grads


def solution(mesh):
    n_dp, n_core = mesh.devices.shape
    shape = SHAPES[n_dp] + (n_core,)
    grid = Mesh(mesh.devices.reshape(shape), ("y", "x", "z", "mp"))
    dp = ("y", "x", "z")
    placed = (P(dp, None), P(dp, None), P(None, "mp"), P(dp), P(dp, None), P(dp))
    return jax.shard_map(
        per_device,
        mesh=grid,
        in_specs=placed,
        out_specs=(P(dp), P(dp, "mp"), P(dp, "mp")),
        check_vma=False,
    )
```

time: 246 us -> 167 us (0.68)
  matrix products: 46.8 us -> 0 us
  blocking collectives: 64.7 us -> 28.7 us
  Pallas kernels: 0 us -> 30.4 us
  local copies, waits for them, and re-layouts: 29.8 us -> 4.54 us
  starting transfers between devices: 25.2 us -> 49.1 us
  other arithmetic: 16.8 us -> 0.1 us
  between operations: 14.4 us -> 0.87 us
  waiting for transfers between devices: 47.1 us -> 53 us
    ppermute x9 -> x26, waiting for transfers between devices: 0.86 us -> 50.5 us  [shifted(): return lax.ppermute(value, axis, [(i, (i + shift) % n) for i in range(n)])]
    dot_general x12 -> x0, matrix products: 46.8 us -> none  [contract(): return lax.dot_general(a, b, (dims, ((), ())), preferred_element_type=f32)]
    all_to_all x3 -> x1, waiting for transfers between devices: 46.2 us -> 2.56 us  [exchanged(): return lax.all_to_all(parts, axis, split_axis=0, concat_axis=0, tiled=True)]
    pallas_call x0 -> x16, Pallas kernels: none -> 30.4 us  [call(): pl.pallas_call(body, in_specs=specs, out_specs=[pl.BlockSpec(memory_space...]
    ppermute x9 -> x26, starting transfers between devices: 12.6 us -> 42.6 us  [shifted(): return lax.ppermute(value, axis, [(i, (i + shift) % n) for i in range(n)])]
    all_to_all x2, blocking collectives: 57.7 us -> 28.7 us  [exchanged(): return lax.all_to_all(parts, axis, split_axis=0, concat_axis=0, tiled=True)]
    unnamed x32 -> x15, local copies, waits for them, and re-layouts: 14.8 us -> 1.57 us
    reduce_sum x6 -> x0, other arithmetic: 7.81 us -> none  [the longest x1 2.92 us: per_device(): q_part = jnp.sum(exchanged(q_part, 'x').astype(f32), axis=0).astype(bf16)]
  transfers between devices with their start and end apart: 14 -> 27, of which waited for: 4 -> 14; matrix products, arithmetic and copies ran while one was open for 28% -> 2% of each run, Pallas kernels for 0% -> 5%
where the time goes in v3:
time: 167 us
  waiting for transfers between devices  53 us (32%)
  starting transfers between devices  49.1 us (29%)
  Pallas kernels  30.4 us (18%)
  blocking collectives  28.7 us (17%)
  local copies, waits for them, and re-layouts  4.54 us (3%)
    ppermute x26, waiting for transfers between devices, shifted(): return lax.ppermute(value, axis, [(i, (i + shift) % n) for i in range(n)])  50.5 us
    ppermute x26, starting transfers between devices, shifted(): return lax.ppermute(value, axis, [(i, (i + shift) % n) for i in range(n)])  42.6 us
    pallas_call x16, Pallas kernels, call(): pl.pallas_call(body, in_specs=specs, out_specs=[pl.BlockSpec(memory_space...  30.4 us
    all_to_all x2, blocking collectives, exchanged(): return lax.all_to_all(parts, axis, split_axis=0, concat_axis=0, tiled=True)  28.7 us
    all_to_all x1, starting transfers between devices, exchanged(): return lax.all_to_all(parts, axis, split_axis=0, concat_axis=0, tiled=True)  6.45 us
  transfers between devices with their start and end apart: 27, of which 14 were waited for; matrix products, arithmetic and copies ran while one was open for 2% of the time, Pallas kernels for 5%

profile of v3, /device:TPU:1, one launch (start us, length us, event | category | flops | bytes accessed | tf_op | source)
XLA Modules:
  0.0 166.8 jit_solution(16521879772101416316)
XLA Ops:
  0.7 5.6 %shard_map.85 = (f32[32,1024]{1,0:T(8,128)S(1)}, f32[256,1024]{1,0:T(8,128)S(1)}, f32[1,384]{1,0:T(1,128)S(1)}) custom-call(s32[5]{0:T(128)S(1)} %stack.23.meta.refs_0_, bf16[32,4096]{1,0:T(8,128)(2,1)} %q_ref.1, bf16[256,4096]{1,0:T(8,128)(2,1)} %p_ref.1, bf16[4096,1024]{1,0:T(8,128)(2,1)} %w_hbm.1), custom_call_target="tpu_custom_call" | custom-call | flops 2415919104 | tf_op jit(solution)/shard_map/pallas_call | solution.py:92
  6.4 3.3 %collective-permute-start = (f32[1,384]{1,0:T(1,128)S(1)}, f32[1,384]{1,0:T(1,128)S(1)}, u32[]{:S(2)}, u32[]{:S(2)}) collective-permute-start(f32[1,384]{1,0:T(1,128)S(1)} %get-tuple-element.50.own_ref), channel_id=1, source_target_pairs={{0,1},{1,0},{2,3},{3,2},{4,5},{5,4},{6,7},{7,6},{8,9},{9,8},{10,11... | collective-permute-start | bytes 4616 | tf_op jit(solution)/shard_map/ppermute | solution.py:21
  14.2 6.5 %all-to-all-start = ((bf16[8,32,1152]{2,1,0:T(8,128)(2,1)}), bf16[8,32,1152]{2,1,0:T(8,128)(2,1)S(1)}, u32[]{:S(2)}, u32[]{:S(2)}) async-start(bf16[8,32,1152]{2,1,0:T(8,128)(2,1)} %broadcast_in_dim.28), calls=%async_computation | async-start | bytes 1179648 | tf_op jit(solution)/shard_map/all_to_all | solution.py:25
  20.7 2.7 %collective-permute-start.4 = (bf16[256,1024]{1,0:T(8,128)(2,1)}, bf16[256,1024]{1,0:T(8,128)(2,1)S(1)}, u32[]{:S(2)}, u32[]{:S(2)}) collective-permute-start(bf16[256,1024]{1,0:T(8,128)(2,1)} %copy-done), channel_id=1, source_target_pairs={{0,192},{64,0},{128,64},{192,128},{1,193},{65,1},{129,65},{193,129... | collective-permute-start | bytes 1572872 | tf_op jit(solution)/shard_map/ppermute | solution.py:21
  23.4 11.0 %collective-permute-done.4.refs_10_ = bf16[256,1024]{1,0:T(8,128)(2,1)S(1)} collective-permute-done((bf16[256,1024]{1,0:T(8,128)(2,1)}, bf16[256,1024]{1,0:T(8,128)(2,1)S(1)}, u32[]{:S(2)}, u32[]{:S(2)}) %collective-permute-start.4) | collective-permute-done | bytes 524320 | tf_op jit(solution)/shard_map/ppermute | solution.py:21
  34.4 3.1 %collective-permute-done.3.refs_7_ = bf16[256,1024]{1,0:T(8,128)(2,1)} collective-permute-done((bf16[256,1024]{1,0:T(8,128)(2,1)}, bf16[256,1024]{1,0:T(8,128)(2,1)}, u32[]{:S(2)}, u32[]{:S(2)}) %collective-permute-start.3) | collective-permute-done | bytes 524320 | tf_op jit(solution)/shard_map/ppermute | solution.py:21
  42.6 12.2 %collective-permute-done.7.refs_5_ = bf16[256,1152]{1,0:T(8,128)(2,1)S(1)} collective-permute-done((bf16[256,1152]{1,0:T(8,128)(2,1)S(1)}, bf16[256,1152]{1,0:T(8,128)(2,1)S(1)}, u32[]{:S(2)}, u32[]{:S(2)}) %collective-permute-start.7) | collective-permute-done | bytes 589856 | tf_op jit(solution)/shard_map/ppermute | solution.py:21
  54.8 3.5 %collective-permute-start.8 = (bf16[128,1152]{1,0:T(8,128)(2,1)S(1)}, bf16[128,1152]{1,0:T(8,128)(2,1)S(1)}, u32[]{:S(2)}, u32[]{:S(2)}) collective-permute-start(bf16[128,1152]{1,0:T(8,128)(2,1)S(1)} %slice.21), channel_id=1, source_target_pairs={{0,48},{16,0},{32,16},{48,32},{1,49},{17,1},{33,17},{49,33},{2,50}... | collective-permute-start | bytes 884744 | tf_op jit(solution)/shard_map/ppermute | solution.py:21
  59.4 2.8 %collective-permute-start.10 = (bf16[128,1024]{1,0:T(8,128)(2,1)S(1)}, bf16[128,1024]{1,0:T(8,128)(2,1)S(1)}, u32[]{:S(2)}, u32[]{:S(2)}) collective-permute-start(bf16[128,1024]{1,0:T(8,128)(2,1)S(1)} %slice.18), channel_id=1, source_target_pairs={{0,192},{64,0},{128,64},{192,128},{1,193},{65,1},{129,65},{193,129... | collective-permute-start | bytes 786440 | tf_op jit(solution)/shard_map/ppermute | solution.py:21
  62.2 4.0 %collective-permute-done.10.refs_9_ = bf16[128,1024]{1,0:T(8,128)(2,1)S(1)} collective-permute-done((bf16[128,1024]{1,0:T(8,128)(2,1)S(1)}, bf16[128,1024]{1,0:T(8,128)(2,1)S(1)}, u32[]{:S(2)}, u32[]{:S(2)}) %collective-permute-start.10) | collective-permute-done | bytes 262176 | tf_op jit(solution)/shard_map/ppermute | solution.py:21
  66.2 3.1 %collective-permute-done.9.refs_8_ = bf16[128,1024]{1,0:T(8,128)(2,1)S(1)} collective-permute-done((bf16[128,1024]{1,0:T(8,128)(2,1)S(1)}, bf16[128,1024]{1,0:T(8,128)(2,1)S(1)}, u32[]{:S(2)}, u32[]{:S(2)}) %collective-permute-start.9) | collective-permute-done | bytes 262176 | tf_op jit(solution)/shard_map/ppermute | solution.py:21
  69.4 2.9 %shard_map.87 = (f32[1024,512]{1,0:T(8,128)S(1)}, bf16[512,1024]{1,0:T(8,128)(2,1)S(1)}, bf16[512,1024]{1,0:T(8,128)(2,1)S(1)}, bf16[1024,1024]{1,0:T(8,128)(2,1...) custom-call(s32[5]{0:T(128)S(1)} %stack.23.meta.refs_0_, bf16[256,1152]{1,0:T(8,128)(2,1)S(1)} %bitcast.23, ...), custom_call_target="tpu_custom_call" | custom-call | flops 1073741824 | tf_op jit(solution)/shard_map/pallas_call | solution.py:92
  72.3 3.1 %collective-permute-start.11 = (f32[1024,512]{1,0:T(8,128)S(1)}, f32[1024,512]{1,0:T(8,128)S(1)}, u32[]{:S(2)}, u32[]{:S(2)}) collective-permute-start(f32[1024,512]{1,0:T(8,128)S(1)} %get-tuple-element.64), channel_id=1, source_target_pairs={{0,1},{1,0},{2,3},{3,2},{4,5},{5,4},{6,7},{7,6},{8,9},{9,8},{10,11... | collective-permute-start | bytes 6291464 | tf_op jit(solution)/shard_map/ppermute | solution.py:21
  77.8 3.2 %shard_map.89 = (f32[1024,512]{1,0:T(8,128)S(1)}, f32[1024,512]{1,0:T(8,128)S(1)}) custom-call(s32[5]{0:T(128)S(1)} %stack.23.meta.refs_0_, bf16[512,1024]{1,0:T(8,128)(2,1)S(1)} %get-tuple-element.58.refs_1_.own_ref, bf16[1024,1024]{1,0:T(8,128)(2,1)S(1)} %get-tuple-element.59.refs_2_.p_ref, f32[128,512]{1,0:T(8,128)S(1)} %get-tuple-element.62.refs_3_.refs_4_), custom_call_target="tpu_custom_call" | custom-call | flops 2147483648 | tf_op jit(solution)/shard_map/pallas_call | solution.py:92
  82.9 13.3 %all_to_all.15.refs_2_ = f32[32,2,512]{2,1,0:T(2,128)S(1)} all-to-all(f32[32,2,512]{2,1,0:T(2,128)S(1)} %broadcast_in_dim.29), channel_id=1, replica_groups=mesh['y'=4,'x'=4,'z'=8,'mp'=2] {'x','z'}, dimensions={0} | all-to-all | bytes 262144 | tf_op jit(solution)/shard_map/all_to_all | solution.py:25
  97.2 3.3 %collective-permute-start.15 = (bf16[1024,512]{1,0:T(8,128)(2,1)S(1)}, bf16[1024,512]{1,0:T(8,128)(2,1)S(1)}, u32[]{:S(2)}, u32[]{:S(2)}) collective-permute-start(bf16[1024,512]{1,0:T(8,128)(2,1)S(1)} %get-tuple-element.69.grad_ref), channel_id=1, source_target_pairs={{0,1},{1,0},{2,3},{3,2},{4,5},{5,4},{6,7},{7,6},{8,9},{9,8},{10,11... | collective-permute-start | bytes 3145736 | tf_op jit(solution)/shard_map/ppermute | solution.py:21
  102.8 2.9 %shard_map.96 = (bf16[256,1024]{1,0:T(8,128)(2,1)S(1)}, bf16[256,1024]{1,0:T(8,128)(2,1)S(1)}, bf16[128,1024]{1,0:T(8,128)(2,1)S(1)}, bf16[128,1024]{1,0:T(8,128)(2,1)S(1)}, bf16[256,1024]{1,0:T(8,128)(2,1)S(1)}) custom-call(s32[5]{0:T(128)S(1)} %stack.23.meta.refs_0_, bf16[1024,512]{1,0:T(8,128)(2,1)S(1)} %get-tuple-element.69.grad_ref, ...), custom_call_target="tpu_custom_call" | custom-call | flops 2147483648 | tf_op jit(solution)/shard_map/pallas_call | solution.py:92
  110.4 4.2 %collective-permute-done.20.up_ref = bf16[128,1024]{1,0:T(8,128)(2,1)S(1)} collective-permute-done((bf16[128,1024]{1,0:T(8,128)(2,1)S(1)}, bf16[128,1024]{1,0:T(8,128)(2,1)S(1)}, u32[]{:S(2)}, u32[]{:S(2)}) %collective-permute-start.20) | collective-permute-done | bytes 262176 | tf_op jit(solution)/shard_map/ppermute | solution.py:21
  120.1 4.6 %collective-permute-done.16.up_ref = bf16[128,1024]{1,0:T(8,128)(2,1)S(1)} collective-permute-done((bf16[128,1024]{1,0:T(8,128)(2,1)S(1)}, bf16[128,1024]{1,0:T(8,128)(2,1)S(1)}, u32[]{:S(2)}, u32[]{:S(2)}) %collective-permute-start.16) | collective-permute-done | bytes 262176 | tf_op jit(solution)/shard_map/ppermute | solution.py:21
  128.4 2.7 %collective-permute-start.24 = (bf16[256,1024]{1,0:T(8,128)(2,1)S(1)}, bf16[256,1024]{1,0:T(8,128)(2,1)S(1)}, u32[]{:S(2)}, u32[]{:S(2)}) collective-permute-start(bf16[256,1024]{1,0:T(8,128)(2,1)S(1)} %shard_map.98.pg_ref), channel_id=1, source_target_pairs={{0,1},{1,0},{2,3},{3,2},{4,5},{5,4},{6,7},{7,6},{8,9},{9,8},{10,11... | collective-permute-start | bytes 1572872 | tf_op jit(solution)/shard_map/ppermute | solution.py:21
  131.1 5.7 %collective-permute-done.18.refs_1_ = bf16[256,1024]{1,0:T(8,128)(2,1)S(1)} collective-permute-done((bf16[256,1024]{1,0:T(8,128)(2,1)S(1)}, bf16[256,1024]{1,0:T(8,128)(2,1)S(1)}, u32[]{:S(2)}, u32[]{:S(2)}) %collective-permute-start.18) | collective-permute-done | bytes 524320 | tf_op jit(solution)/shard_map/ppermute | solution.py:21
  137.0 15.4 %all_to_all.16.refs_1_ = bf16[8,32,1024]{2,1,0:T(8,128)(2,1)S(1)} all-to-all(bf16[8,32,1024]{2,1,0:T(8,128)(2,1)S(1)} %bitcast.24), channel_id=1, replica_groups=mesh['y'=4,'x'=4,'z'=8,'mp'=2] {'z'}, dimensions={0} | all-to-all | bytes 1048576 | tf_op jit(solution)/shard_map/all_to_all | solution.py:25
  153.1 5.5 %collective-permute-start.25 = (f32[40,1024]{1,0:T(8,128)S(1)}, f32[40,1024]{1,0:T(8,128)S(1)}, u32[]{:S(2)}, u32[]{:S(2)}) collective-permute-start(f32[40,1024]{1,0:T(8,128)S(1)} %shard_map.99.qg_ref), channel_id=1, source_target_pairs={{0,1},{1,0},{2,3},{3,2},{4,5},{5,4},{6,7},{7,6},{8,9},{9,8},{10,11... | collective-permute-start | bytes 491528 | tf_op jit(solution)/shard_map/ppermute | solution.py:21
  159.6 6.6 %shard_map.100 = (bf16[32,2048]{1,0:T(8,128)(2,1)}, bf16[256,2048]{1,0:T(8,128)(2,1)}, f32[1,128]{1,0:T(1,128)S(1)}) custom-call(s32[5]{0:T(128)S(1)} %stack.23.meta.refs_0_, f32[40,1024]{1,0:T(8,128)S(1)} %shard_map.99.qg_ref, f32[40,1024]{1,0:T(8,128)S(1)} %collective-permute-done.25.qgo_ref, bf16[256,1024]{1,0:T(8,128)(2,1)S(1)} %shard_map.98.pg_ref, ...), custom_call_target="tpu_custom_call" | custom-call | flops 2415919104 | tf_op jit(solution)/shard_map/pallas_call | solution.py:92
  (81 shorter events, 34.6 us)
Async XLA Ops:
  12.8 27.2 %collective-permute-start.2 = (bf16[4096,1024]{1,0:T(8,128)(2,1)}, bf16[4096,1024]{1,0:T(8,128)(2,1)}, u32[]{:S(2)}, u32[]{:S(2)}) collective-permute-start(bf16[4096,1024]{1,0:T(8,128)(2,1)} %w_hbm.1), channel_id=1, source_target_pairs={{0,1},{1,0},{2,3},{3,2},{4,5},{5,4},{6,7},{7,6},{8,9},{9,8},{10,11... | collective-permute-start | bytes 25165832 | tf_op jit(solution)/shard_map/ppermute | solution.py:21
  13.2 26.9 %collective-permute-start.1 = (f32[288,1024]{1,0:T(8,128)S(1)}, f32[288,1024]{1,0:T(8,128)S(1)}, u32[]{:S(2)}, u32[]{:S(2)}) collective-permute-start(f32[288,1024]{1,0:T(8,128)S(1)} %get-tuple-element.52.unit_ref), channel_id=1, source_target_pairs={{0,1},{1,0},{2,3},{3,2},{4,5},{5,4},{6,7},{7,6},{8,9},{9,8},{10,11... | collective-permute-start | bytes 3538952 | tf_op jit(solution)/shard_map/ppermute | solution.py:21
  14.2 25.8 %all-to-all-start = ((bf16[8,32,1152]{2,1,0:T(8,128)(2,1)}), bf16[8,32,1152]{2,1,0:T(8,128)(2,1)S(1)}, u32[]{:S(2)}, u32[]{:S(2)}) async-start(bf16[8,32,1152]{2,1,0:T(8,128)(2,1)} %broadcast_in_dim.28), calls=%async_computation | async-start | bytes 1179648 | tf_op jit(solution)/shard_map/all_to_all | solution.py:25
  20.7 13.7 %collective-permute-start.4 = (bf16[256,1024]{1,0:T(8,128)(2,1)}, bf16[256,1024]{1,0:T(8,128)(2,1)S(1)}, u32[]{:S(2)}, u32[]{:S(2)}) collective-permute-start(bf16[256,1024]{1,0:T(8,128)(2,1)} %copy-done), channel_id=1, source_target_pairs={{0,192},{64,0},{128,64},{192,128},{1,193},{65,1},{129,65},{193,129... | collective-permute-start | bytes 1572872 | tf_op jit(solution)/shard_map/ppermute | solution.py:21
  23.4 14.1 %collective-permute-start.3 = (bf16[256,1024]{1,0:T(8,128)(2,1)}, bf16[256,1024]{1,0:T(8,128)(2,1)}, u32[]{:S(2)}, u32[]{:S(2)}) collective-permute-start(bf16[256,1024]{1,0:T(8,128)(2,1)} %copy-done), channel_id=1, source_target_pairs={{0,64},{64,128},{128,192},{192,0},{1,65},{65,129},{129,193},{193,1... | collective-permute-start | bytes 1572872 | tf_op jit(solution)/shard_map/ppermute | solution.py:21
  40.0 14.8 %collective-permute-start.7 = (bf16[256,1152]{1,0:T(8,128)(2,1)S(1)}, bf16[256,1152]{1,0:T(8,128)(2,1)S(1)}, u32[]{:S(2)}, u32[]{:S(2)}) collective-permute-start(bf16[256,1152]{1,0:T(8,128)(2,1)S(1)} %bitcast.21), channel_id=1, source_target_pairs={{0,48},{16,0},{32,16},{48,32},{1,49},{17,1},{33,17},{49,33},{2,50}... | collective-permute-start | bytes 1769480 | tf_op jit(solution)/shard_map/ppermute | solution.py:21
  42.6 15.7 %collective-permute-start.5 = (bf16[256,1152]{1,0:T(8,128)(2,1)S(1)}, bf16[256,1152]{1,0:T(8,128)(2,1)S(1)}, u32[]{:S(2)}, u32[]{:S(2)}) collective-permute-start(bf16[256,1152]{1,0:T(8,128)(2,1)S(1)} %bitcast.22), channel_id=1, source_target_pairs={{0,16},{16,32},{32,48},{48,0},{1,17},{17,33},{33,49},{49,1},{2,18}... | collective-permute-start | bytes 1769480 | tf_op jit(solution)/shard_map/ppermute | solution.py:21
  54.8 14.5 %collective-permute-start.8 = (bf16[128,1152]{1,0:T(8,128)(2,1)S(1)}, bf16[128,1152]{1,0:T(8,128)(2,1)S(1)}, u32[]{:S(2)}, u32[]{:S(2)}) collective-permute-start(bf16[128,1152]{1,0:T(8,128)(2,1)S(1)} %slice.21), channel_id=1, source_target_pairs={{0,48},{16,0},{32,16},{48,32},{1,49},{17,1},{33,17},{49,33},{2,50}... | collective-permute-start | bytes 884744 | tf_op jit(solution)/shard_map/ppermute | solution.py:21
  58.3 11.0 %collective-permute-start.6 = (bf16[128,1152]{1,0:T(8,128)(2,1)S(1)}, bf16[128,1152]{1,0:T(8,128)(2,1)S(1)}, u32[]{:S(2)}, u32[]{:S(2)}) collective-permute-start(bf16[128,1152]{1,0:T(8,128)(2,1)S(1)} %slice.20), channel_id=1, source_target_pairs={{0,16},{16,32},{32,48},{48,0},{1,17},{17,33},{33,49},{49,1},{2,18}... | collective-permute-start | bytes 884744 | tf_op jit(solution)/shard_map/ppermute | solution.py:21
  59.4 6.8 %collective-permute-start.10 = (bf16[128,1024]{1,0:T(8,128)(2,1)S(1)}, bf16[128,1024]{1,0:T(8,128)(2,1)S(1)}, u32[]{:S(2)}, u32[]{:S(2)}) collective-permute-start(bf16[128,1024]{1,0:T(8,128)(2,1)S(1)} %slice.18), channel_id=1, source_target_pairs={{0,192},{64,0},{128,64},{192,128},{1,193},{65,1},{129,65},{193,129... | collective-permute-start | bytes 786440 | tf_op jit(solution)/shard_map/ppermute | solution.py:21
  62.2 7.1 %collective-permute-start.9 = (bf16[128,1024]{1,0:T(8,128)(2,1)S(1)}, bf16[128,1024]{1,0:T(8,128)(2,1)S(1)}, u32[]{:S(2)}, u32[]{:S(2)}) collective-permute-start(bf16[128,1024]{1,0:T(8,128)(2,1)S(1)} %slice.17), channel_id=1, source_target_pairs={{0,64},{64,128},{128,192},{192,0},{1,65},{65,129},{129,193},{193,1... | collective-permute-start | bytes 786440 | tf_op jit(solution)/shard_map/ppermute | solution.py:21
  72.3 9.1 %collective-permute-start.11 = (f32[1024,512]{1,0:T(8,128)S(1)}, f32[1024,512]{1,0:T(8,128)S(1)}, u32[]{:S(2)}, u32[]{:S(2)}) collective-permute-start(f32[1024,512]{1,0:T(8,128)S(1)} %get-tuple-element.64), channel_id=1, source_target_pairs={{0,1},{1,0},{2,3},{3,2},{4,5},{5,4},{6,7},{7,6},{8,9},{9,8},{10,11... | collective-permute-start | bytes 6291464 | tf_op jit(solution)/shard_map/ppermute | solution.py:21
  76.2 4.8 %collective-permute-start.14 = (f32[8,256]{1,0:T(8,128)S(1)}, f32[8,256]{1,0:T(8,128)S(1)}, u32[]{:S(2)}, u32[]{:S(2)}) collective-permute-start(f32[8,256]{1,0:T(8,128)S(1)} %get-tuple-element.66.refs_5_), channel_id=1, source_target_pairs={{0,192},{64,0},{128,64},{192,128},{1,193},{65,1},{129,65},{193,129... | collective-permute-start | bytes 24584 | tf_op jit(solution)/shard_map/ppermute | solution.py:21
  97.2 5.6 %collective-permute-start.15 = (bf16[1024,512]{1,0:T(8,128)(2,1)S(1)}, bf16[1024,512]{1,0:T(8,128)(2,1)S(1)}, u32[]{:S(2)}, u32[]{:S(2)}) collective-permute-start(bf16[1024,512]{1,0:T(8,128)(2,1)S(1)} %get-tuple-element.69.grad_ref), channel_id=1, source_target_pairs={{0,1},{1,0},{2,3},{3,2},{4,5},{5,4},{6,7},{7,6},{8,9},{9,8},{10,11... | collective-permute-start | bytes 3145736 | tf_op jit(solution)/shard_map/ppermute | solution.py:21
  105.7 8.8 %collective-permute-start.20 = (bf16[128,1024]{1,0:T(8,128)(2,1)S(1)}, bf16[128,1024]{1,0:T(8,128)(2,1)S(1)}, u32[]{:S(2)}, u32[]{:S(2)}) collective-permute-start(bf16[128,1024]{1,0:T(8,128)(2,1)S(1)} %get-tuple-element.81), channel_id=1, source_target_pairs={{0,64},{64,128},{128,192},{192,0},{1,65},{65,129},{129,193},{193,1... | collective-permute-start | bytes 786440 | tf_op jit(solution)/shard_map/ppermute | solution.py:21
  105.8 8.7 %collective-permute-start.21 = (bf16[128,1024]{1,0:T(8,128)(2,1)S(1)}, bf16[128,1024]{1,0:T(8,128)(2,1)S(1)}, u32[]{:S(2)}, u32[]{:S(2)}) collective-permute-start(bf16[128,1024]{1,0:T(8,128)(2,1)S(1)} %get-tuple-element.84), channel_id=1, source_target_pairs={{0,192},{64,0},{128,64},{192,128},{1,193},{65,1},{129,65},{193,129... | collective-permute-start | bytes 786440 | tf_op jit(solution)/shard_map/ppermute | solution.py:21
  114.7 13.5 %collective-permute-start.22 = (bf16[256,1024]{1,0:T(8,128)(2,1)S(1)}, bf16[256,1024]{1,0:T(8,128)(2,1)S(1)}, u32[]{:S(2)}, u32[]{:S(2)}) collective-permute-start(bf16[256,1024]{1,0:T(8,128)(2,1)S(1)} %get-tuple-element.85), channel_id=1, source_target_pairs={{0,64},{64,128},{128,192},{192,0},{1,65},{65,129},{129,193},{193,1... | collective-permute-start | bytes 1572872 | tf_op jit(solution)/shard_map/ppermute | solution.py:21
  115.1 13.0 %collective-permute-start.23 = (bf16[256,1024]{1,0:T(8,128)(2,1)S(1)}, bf16[256,1024]{1,0:T(8,128)(2,1)S(1)}, u32[]{:S(2)}, u32[]{:S(2)}) collective-permute-start(bf16[256,1024]{1,0:T(8,128)(2,1)S(1)} %get-tuple-element.86), channel_id=1, source_target_pairs={{0,192},{64,0},{128,64},{192,128},{1,193},{65,1},{129,65},{193,129... | collective-permute-start | bytes 1572872 | tf_op jit(solution)/shard_map/ppermute | solution.py:21
  117.4 7.2 %collective-permute-start.16 = (bf16[128,1024]{1,0:T(8,128)(2,1)S(1)}, bf16[128,1024]{1,0:T(8,128)(2,1)S(1)}, u32[]{:S(2)}, u32[]{:S(2)}) collective-permute-start(bf16[128,1024]{1,0:T(8,128)(2,1)S(1)} %bitcast.29), channel_id=1, source_target_pairs={{0,16},{16,32},{32,48},{48,0},{1,17},{17,33},{33,49},{49,1},{2,18}... | collective-permute-start | bytes 786440 | tf_op jit(solution)/shard_map/ppermute | solution.py:21
  117.8 6.9 %collective-permute-start.17 = (bf16[128,1024]{1,0:T(8,128)(2,1)S(1)}, bf16[128,1024]{1,0:T(8,128)(2,1)S(1)}, u32[]{:S(2)}, u32[]{:S(2)}) collective-permute-start(bf16[128,1024]{1,0:T(8,128)(2,1)S(1)} %bitcast.28), channel_id=1, source_target_pairs={{0,48},{16,0},{32,16},{48,32},{1,49},{17,1},{33,17},{49,33},{2,50}... | collective-permute-start | bytes 786440 | tf_op jit(solution)/shard_map/ppermute | solution.py:21
  124.8 12.0 %collective-permute-start.18 = (bf16[256,1024]{1,0:T(8,128)(2,1)S(1)}, bf16[256,1024]{1,0:T(8,128)(2,1)S(1)}, u32[]{:S(2)}, u32[]{:S(2)}) collective-permute-start(bf16[256,1024]{1,0:T(8,128)(2,1)S(1)} %get-tuple-element.76), channel_id=1, source_target_pairs={{0,16},{16,32},{32,48},{48,0},{1,17},{17,33},{33,49},{49,1},{2,18}... | collective-permute-start | bytes 1572872 | tf_op jit(solution)/shard_map/ppermute | solution.py:21
  124.9 11.9 %collective-permute-start.19 = (bf16[256,1024]{1,0:T(8,128)(2,1)S(1)}, bf16[256,1024]{1,0:T(8,128)(2,1)S(1)}, u32[]{:S(2)}, u32[]{:S(2)}) collective-permute-start(bf16[256,1024]{1,0:T(8,128)(2,1)S(1)} %get-tuple-element.77), channel_id=1, source_target_pairs={{0,48},{16,0},{32,16},{48,32},{1,49},{17,1},{33,17},{49,33},{2,50}... | collective-permute-start | bytes 1572872 | tf_op jit(solution)/shard_map/ppermute | solution.py:21
  128.4 8.7 %collective-permute-start.24 = (bf16[256,1024]{1,0:T(8,128)(2,1)S(1)}, bf16[256,1024]{1,0:T(8,128)(2,1)S(1)}, u32[]{:S(2)}, u32[]{:S(2)}) collective-permute-start(bf16[256,1024]{1,0:T(8,128)(2,1)S(1)} %shard_map.98.pg_ref), channel_id=1, source_target_pairs={{0,1},{1,0},{2,3},{3,2},{4,5},{5,4},{6,7},{7,6},{8,9},{9,8},{10,11... | collective-permute-start | bytes 1572872 | tf_op jit(solution)/shard_map/ppermute | solution.py:21
  153.1 6.5 %collective-permute-start.25 = (f32[40,1024]{1,0:T(8,128)S(1)}, f32[40,1024]{1,0:T(8,128)S(1)}, u32[]{:S(2)}, u32[]{:S(2)}) collective-permute-start(f32[40,1024]{1,0:T(8,128)S(1)} %shard_map.99.qg_ref), channel_id=1, source_target_pairs={{0,1},{1,0},{2,3},{3,2},{4,5},{5,4},{6,7},{7,6},{8,9},{9,8},{10,11... | collective-permute-start | bytes 491528 | tf_op jit(solution)/shard_map/ppermute | solution.py:21
  (10 other events, 102.5 us)

commit v4 on v3

--- a/solution.py
+++ b/solution.py
@@ -47,18 +47,18 @@
     return [value, before, shifted(before[:cut], axis, 1), shifted(behind[cut:], axis, -1), behind]
 
 
-def return_first(pieces, axis, gate=None):
+def return_far(pieces, axis):
     if len(pieces) == 2:
         return [pieces[1]]
-    up, down = shifted(pieces[2], axis, 1), shifted(pieces[3], axis, -1)
-    if gate is not None:
-        up = after(up, gate)
-    return join(pieces[4], up, pieces[1], down)
-
-
-def return_second(pieces, leaving, axis):
-    coming = [shifted(value, axis, shift) for shift, value in zip((1, -1), leaving)]
-    return total([pieces[0]] + coming, bf16)
+    return [shifted(pieces[2], axis, 1), shifted(pieces[3], axis, -1)]
+
+
+def near_coming(leaving, axis):
+    return [shifted(value, axis, shift) for shift, value in zip((1, -1), leaving)]
+
+
+def return_near(pieces, leaving, axis):
+    return total([pieces[0]] + near_coming(leaving, axis), bf16)
 
 
 def split_three(value):
@@ -167,10 +167,12 @@
     behind_out[cut:] = (behind_ref[cut:].astype(f32) + down_ref[...].astype(f32)).astype(bf16)
 
 
-def join(ahead, up, behind, down):
+def join(pieces, far):
+    if len(pieces) == 2:
+        return far
     meta = jnp.zeros((1,), jnp.int32)
-    shape = struct(ahead.shape, bf16)
-    return call(join_body, [meta, ahead, up, behind, down], [shape, shape], loose=True)
+    shape = struct(pieces[1].shape, bf16)
+    return call(join_body, [meta, pieces[4], far[0], pieces[1], far[1]], [shape, shape], loose=True)
 
 
 def project_body(
@@ -244,20 +246,22 @@
 
     def store(columns, value):
         top, bottom = value[:half], value[half:]
-        message_ref[:half, columns] = jnp.where(first, top, bottom).astype(bf16)
-        message_ref[half:, columns] = jnp.where(first, bottom, top).astype(bf16)
+        upper, lower = jnp.where(first, top, bottom), jnp.where(first, bottom, top)
+        for s in range(message_ref.shape[0]):
+            message_ref[s, :half, columns] = upper.astype(bf16)
+            message_ref[s, half:, columns] = lower.astype(bf16)
 
     store(slice(0, width), q_unit)
     store(slice(width, width + AUX), aux_ref[...])
 
 
-def normalize(meta, q_proj, p_proj, square, square_got, aux):
+def normalize(meta, q_proj, p_proj, square, square_got, aux, copies):
     (n_q, width), n_p = q_proj.shape, p_proj.shape[0]
     return call(
         normalize_body,
         [meta, q_proj, p_proj, square, square_got, aux],
         [
-            struct((n_q, width + AUX), bf16),
+            struct((copies, n_q, width + AUX), bf16),
             struct((n_q + n_p, width)),
             struct((n_p, width), bf16),
             struct((n_q + n_p, 128)),
@@ -511,25 +515,44 @@
     )
 
 
+def head_rows_body(meta, w_ref, wo_ref, keep_ref, got_ref, sems):
+    half = keep_ref.shape[0]
+    copies = []
+    for at in spans(half, CHUNK):
+        rows = pl.ds(pl.multiple_of(meta[0] * half + at.start, CHUNK), at.stop - at.start)
+        to = pl.ds(at.start, at.stop - at.start)
+        for from_ref, to_ref in ((w_ref, keep_ref), (wo_ref, got_ref)):
+            sem = sems.at[len(copies)]
+            copies.append(pltpu.make_async_copy(from_ref.at[rows], to_ref.at[to], sem))
+    for copy in copies:
+        copy.start()
+    for copy in copies:
+        copy.wait()
+
+
+def head_rows(meta, weight, weight_got):
+    depth, width = weight.shape
+    shape = struct((depth // 2, width), bf16)
+    count = 2 * len(spans(depth // 2, CHUNK))
+    return call(
+        head_rows_body,
+        [meta, weight, weight_got],
+        [shape, shape],
+        [pltpu.SemaphoreType.DMA((count,))],
+        hbm=(1, 2),
+        vmem=4,
+    )
+
+
 def tangent(grad, other, unit, beyond, inv):
     radial = jnp.sum(unit * grad + beyond * other, axis=1, keepdims=True)
     return (inv * (grad - unit * radial)).astype(bf16), (inv * (other - beyond * radial)).astype(bf16)
 
 
 def finish_body(
-    meta, qg_ref, qgo_ref, pg_ref, pgo_ref, unit_ref, beyond_ref, inv_ref, w_hbm, wo_hbm,
-    q_out, p_out, loss_out, here_ref, there_ref, w_ref, wo_ref, sems
+    meta, qg_ref, qgo_ref, pg_ref, pgo_ref, unit_ref, beyond_ref, inv_ref, w_ref, wo_ref,
+    q_out, p_out, loss_out, here_ref, there_ref
 ):
-    half = w_ref.shape[0]
-    blocks = spans(half, CHUNK)
-    loads = []
-    for i, at in enumerate(blocks):
-        size, to = at.stop - at.start, pl.ds(at.start, at.stop - at.start)
-        rows = pl.ds(pl.multiple_of(meta[0] * half + at.start, size), size)
-        loads.append(pltpu.make_async_copy(w_hbm.at[rows], w_ref.at[to], sems.at[2 * i]))
-        loads.append(pltpu.make_async_copy(wo_hbm.at[rows], wo_ref.at[to], sems.at[2 * i + 1]))
-    for load in loads:
-        load.start()
     n_q = q_out.shape[0]
     part = n_q // 2
     first = meta[0] == 0
@@ -548,9 +571,7 @@
         here_ref[to], there_ref[to] = tangent(
             pg_ref[at].astype(f32), pgo_ref[at].astype(f32), unit_ref[to], beyond_ref[to], inv_ref[to, :1]
         )
-    for i, at in enumerate(blocks):
-        loads[2 * i].wait()
-        loads[2 * i + 1].wait()
+    for at in spans(w_ref.shape[0], CHUNK):
         state = contract(here_ref[...], w_ref[at], ((1,), (1,)))
         state = (state + contract(there_ref[...], wo_ref[at], ((1,), (1,)))).astype(bf16)
         q_out[:, at] = state[:n_q]
@@ -558,9 +579,8 @@
 
 
 def finish(meta, rows_in, weight, weight_got):
-    depth, width = weight.shape
-    n, n_p, out_width = rows_in[4].shape[0], rows_in[2].shape[0], depth // 2
-    copies = 2 * len(spans(out_width, CHUNK))
+    out_width, width = weight.shape
+    n, n_p = rows_in[4].shape[0], rows_in[2].shape[0]
     return call(
         finish_body,
         [meta, *rows_in, weight, weight_got],
@@ -568,14 +588,9 @@
         [
             pltpu.VMEM((n, width), bf16),
             pltpu.VMEM((n, width), bf16),
-            pltpu.VMEM((out_width, width), bf16),
-            pltpu.VMEM((out_width, width), bf16),
-            pltpu.SemaphoreType.DMA((copies,)),
         ],
         4 * n * out_width * width,
-        hbm=(8, 9),
         free=(0, 1, 2),
-        vmem=20,
     )
 
 
@@ -601,12 +616,12 @@
     )
     aux = jnp.pad(aux, ((0, 0), (0, AUX - aux.shape[1])))
     message, unit, p_embed, inv = normalize(
-        meta, q_proj, p_proj, square, square_got, aux
+        meta, q_proj, p_proj, square, square_got, aux, n_z
     )
     unit_got = shifted(unit, "mp", 1)
     weight_got = shifted(after(head_weight, unit), "mp", 1)
     p_near = ring_near(p_embed, "y")
-    q_z = to_all(message, "z").reshape(n_z * q_rows, width + AUX)
+    q_z = exchanged(message, "z").reshape(n_z * q_rows, width + AUX)
     q_z = after(q_z, unit_got, weight_got, *p_near)
     q_near = ring_near(q_z, "x")
     q_pieces = ring_far(q_z, q_near, "x")
@@ -625,17 +640,21 @@
     grad_got = after(grad_got, q_part)
     p_parts = passage_part(meta, grad, grad_got, q_own, q_other, p_shapes)
     q_parts = query_rest(meta, grad_got, p_all, q_part, q_shapes)
-    p_leaving = return_first(p_parts, "y", q_parts[0])
-    q_leaving = return_first([part.reshape(-1, width) for part in q_parts], "x")
-    p_grad = return_second(p_parts, p_leaving, "y")
+    q_parts = [part.reshape(-1, width) for part in q_parts]
+    p_far, q_far = return_far(p_parts, "y"), return_far(q_parts, "x")
+    q_leaving = join(q_parts, q_far)
+    p_leaving = join(p_parts, [after(p_far[0], *q_leaving)] + p_far[1:])
+    p_coming = near_coming(p_leaving, "y")
+    q_part = return_near(q_parts, q_leaving, "x")
+    weight, weight_got = head_rows(after(meta, *q_leaving), head_weight, weight_got)
+    q_part = after(q_part, *p_coming, weight, weight_got)
+    back = exchanged(q_part.reshape(n_z, q_rows, width), "z")
+    p_grad = total([after(p_parts[0], back)] + p_coming, bf16)
     p_grad_got = shifted(p_grad, "mp", 1)
-    q_part = return_second([part.reshape(-1, width) for part in q_parts], q_leaving, "x")
-    q_part = after(q_part, p_grad_got)
-    back = exchanged(q_part.reshape(n_z, q_rows, width), "z")
     q_grad = total_slots(meta, back, loss, n_z * half)
     q_grad_got = shifted(q_grad, "mp", 1)
     query_grads, passage_grads, losses = finish(
-        meta, (q_grad, q_grad_got, p_grad, p_grad_got, unit, unit_got, inv), head_weight, weight_got
+        meta, (q_grad, q_grad_got, p_grad, p_grad_got, unit, unit_got, inv), weight, weight_got
     )
     return losses[0, :q_rows], query_grads, passage_grads
 

time: 167 us -> 160 us (0.958)
  waiting for transfers between devices: 53 us -> 46.7 us
  starting transfers between devices: 49.1 us -> 45.2 us
  Pallas kernels: 30.4 us -> 33.1 us
    ppermute x26, waiting for transfers between devices: 50.5 us -> 44.1 us  [shifted(): return lax.ppermute(value, axis, [(i, (i + shift) % n) for i in range(n)])]
    ppermute x26, starting transfers between devices: 42.6 us -> 38.8 us  [shifted(): return lax.ppermute(value, axis, [(i, (i + shift) % n) for i in range(n)])]
    pallas_call x16 -> x17, Pallas kernels: 30.4 us -> 33.1 us  [call(): pl.pallas_call(body, in_specs=specs, out_specs=[pl.BlockSpec(memory_space...]
  transfers between devices with their start and end apart: 27 -> 27, of which waited for: 14 -> 14; matrix products, arithmetic and copies ran while one was open for 2% -> 1% of each run, Pallas kernels for 5% -> 9%
where the time goes in v4:
time: 160 us
  waiting for transfers between devices  46.7 us (29%)
  starting transfers between devices  45.2 us (28%)
  Pallas kernels  33.1 us (21%)
  blocking collectives  30 us (19%)
  local copies, waits for them, and re-layouts  3.68 us (2%)
    ppermute x26, waiting for transfers between devices, shifted(): return lax.ppermute(value, axis, [(i, (i + shift) % n) for i in range(n)])  44.1 us
    ppermute x26, starting transfers between devices, shifted(): return lax.ppermute(value, axis, [(i, (i + shift) % n) for i in range(n)])  38.8 us
    pallas_call x17, Pallas kernels, call(): pl.pallas_call(body, in_specs=specs, out_specs=[pl.BlockSpec(memory_space...  33.1 us
    all_to_all x2, blocking collectives, exchanged(): return lax.all_to_all(parts, axis, split_axis=0, concat_axis=0, tiled=True)  30 us
    all_to_all x1, starting transfers between devices, exchanged(): return lax.all_to_all(parts, axis, split_axis=0, concat_axis=0, tiled=True)  6.45 us
  transfers between devices with their start and end apart: 27, of which 14 were waited for; matrix products, arithmetic and copies ran while one was open for 1% of the time, Pallas kernels for 9%

profile of v4, /device:TPU:1, one launch (start us, length us, event | category | flops | bytes accessed | tf_op | source)
XLA Modules:
  0.0 159.7 jit_solution(2441078656117491252)
XLA Ops:
  0.7 5.6 %shard_map.85 = (f32[32,1024]{1,0:T(8,128)S(1)}, f32[256,1024]{1,0:T(8,128)S(1)}, f32[1,384]{1,0:T(1,128)S(1)}) custom-call(s32[5]{0:T(128)S(1)} %stack.23.meta.refs_0_, bf16[32,4096]{1,0:T(8,128)(2,1)} %q_ref.1, bf16[256,4096]{1,0:T(8,128)(2,1)} %p_ref.1, bf16[4096,1024]{1,0:T(8,128)(2,1)} %w_ref.3), custom_call_target="tpu_custom_call" | custom-call | flops 2415919104 | tf_op jit(solution)/shard_map/pallas_call | solution.py:92
  6.4 3.3 %collective-permute-start = (f32[1,384]{1,0:T(1,128)S(1)}, f32[1,384]{1,0:T(1,128)S(1)}, u32[]{:S(2)}, u32[]{:S(2)}) collective-permute-start(f32[1,384]{1,0:T(1,128)S(1)} %get-tuple-element.54.own_ref), channel_id=1, source_target_pairs={{0,1},{1,0},{2,3},{3,2},{4,5},{5,4},{6,7},{7,6},{8,9},{9,8},{10,11... | collective-permute-start | bytes 4616 | tf_op jit(solution)/shard_map/ppermute | solution.py:21
  14.1 6.5 %all-to-all-start = ((bf16[8,32,1152]{2,1,0:T(8,128)(2,1)}), bf16[8,32,1152]{2,1,0:T(8,128)(2,1)S(1)}, u32[]{:S(2)}, u32[]{:S(2)}) async-start(bf16[8,32,1152]{2,1,0:T(8,128)(2,1)} %get-tuple-element.55), calls=%async_computation | async-start | bytes 1179648 | tf_op jit(solution)/shard_map/all_to_all | solution.py:25
  20.6 2.7 %collective-permute-start.4 = (bf16[256,1024]{1,0:T(8,128)(2,1)}, bf16[256,1024]{1,0:T(8,128)(2,1)S(1)}, u32[]{:S(2)}, u32[]{:S(2)}) collective-permute-start(bf16[256,1024]{1,0:T(8,128)(2,1)} %copy-done), channel_id=1, source_target_pairs={{0,192},{64,0},{128,64},{192,128},{1,193},{65,1},{129,65},{193,129... | collective-permute-start | bytes 1572872 | tf_op jit(solution)/shard_map/ppermute | solution.py:21
  23.3 11.0 %collective-permute-done.4.refs_10_ = bf16[256,1024]{1,0:T(8,128)(2,1)S(1)} collective-permute-done((bf16[256,1024]{1,0:T(8,128)(2,1)}, bf16[256,1024]{1,0:T(8,128)(2,1)S(1)}, u32[]{:S(2)}, u32[]{:S(2)}) %collective-permute-start.4) | collective-permute-done | bytes 524320 | tf_op jit(solution)/shard_map/ppermute | solution.py:21
  34.3 3.1 %collective-permute-done.3.refs_7_ = bf16[256,1024]{1,0:T(8,128)(2,1)} collective-permute-done((bf16[256,1024]{1,0:T(8,128)(2,1)}, bf16[256,1024]{1,0:T(8,128)(2,1)}, u32[]{:S(2)}, u32[]{:S(2)}) %collective-permute-start.3) | collective-permute-done | bytes 524320 | tf_op jit(solution)/shard_map/ppermute | solution.py:21
  42.5 12.2 %collective-permute-done.7.refs_5_ = bf16[256,1152]{1,0:T(8,128)(2,1)S(1)} collective-permute-done((bf16[256,1152]{1,0:T(8,128)(2,1)S(1)}, bf16[256,1152]{1,0:T(8,128)(2,1)S(1)}, u32[]{:S(2)}, u32[]{:S(2)}) %collective-permute-start.7) | collective-permute-done | bytes 589856 | tf_op jit(solution)/shard_map/ppermute | solution.py:21
  54.7 3.5 %collective-permute-start.8 = (bf16[128,1152]{1,0:T(8,128)(2,1)S(1)}, bf16[128,1152]{1,0:T(8,128)(2,1)S(1)}, u32[]{:S(2)}, u32[]{:S(2)}) collective-permute-start(bf16[128,1152]{1,0:T(8,128)(2,1)S(1)} %slice.21), channel_id=1, source_target_pairs={{0,48},{16,0},{32,16},{48,32},{1,49},{17,1},{33,17},{49,33},{2,50}... | collective-permute-start | bytes 884744 | tf_op jit(solution)/shard_map/ppermute | solution.py:21
  59.3 2.8 %collective-permute-start.10 = (bf16[128,1024]{1,0:T(8,128)(2,1)S(1)}, bf16[128,1024]{1,0:T(8,128)(2,1)S(1)}, u32[]{:S(2)}, u32[]{:S(2)}) collective-permute-start(bf16[128,1024]{1,0:T(8,128)(2,1)S(1)} %slice.18), channel_id=1, source_target_pairs={{0,192},{64,0},{128,64},{192,128},{1,193},{65,1},{129,65},{193,129... | collective-permute-start | bytes 786440 | tf_op jit(solution)/shard_map/ppermute | solution.py:21
  62.1 4.0 %collective-permute-done.10.refs_9_ = bf16[128,1024]{1,0:T(8,128)(2,1)S(1)} collective-permute-done((bf16[128,1024]{1,0:T(8,128)(2,1)S(1)}, bf16[128,1024]{1,0:T(8,128)(2,1)S(1)}, u32[]{:S(2)}, u32[]{:S(2)}) %collective-permute-start.10) | collective-permute-done | bytes 262176 | tf_op jit(solution)/shard_map/ppermute | solution.py:21
  66.1 3.1 %collective-permute-done.9.refs_8_ = bf16[128,1024]{1,0:T(8,128)(2,1)S(1)} collective-permute-done((bf16[128,1024]{1,0:T(8,128)(2,1)S(1)}, bf16[128,1024]{1,0:T(8,128)(2,1)S(1)}, u32[]{:S(2)}, u32[]{:S(2)}) %collective-permute-start.9) | collective-permute-done | bytes 262176 | tf_op jit(solution)/shard_map/ppermute | solution.py:21
  69.3 2.9 %shard_map.87 = (f32[1024,512]{1,0:T(8,128)S(1)}, bf16[512,1024]{1,0:T(8,128)(2,1)S(1)}, bf16[512,1024]{1,0:T(8,128)(2,1)S(1)}, bf16[1024,1024]{1,0:T(8,128)(2,1...) custom-call(s32[5]{0:T(128)S(1)} %stack.23.meta.refs_0_, bf16[256,1152]{1,0:T(8,128)(2,1)S(1)} %bitcast.23, ...), custom_call_target="tpu_custom_call" | custom-call | flops 1073741824 | tf_op jit(solution)/shard_map/pallas_call | solution.py:92
  72.2 3.1 %collective-permute-start.11 = (f32[1024,512]{1,0:T(8,128)S(1)}, f32[1024,512]{1,0:T(8,128)S(1)}, u32[]{:S(2)}, u32[]{:S(2)}) collective-permute-start(f32[1024,512]{1,0:T(8,128)S(1)} %get-tuple-element.68), channel_id=1, source_target_pairs={{0,1},{1,0},{2,3},{3,2},{4,5},{5,4},{6,7},{7,6},{8,9},{9,8},{10,11... | collective-permute-start | bytes 6291464 | tf_op jit(solution)/shard_map/ppermute | solution.py:21
  77.7 3.2 %shard_map.89 = (f32[1024,512]{1,0:T(8,128)S(1)}, f32[1024,512]{1,0:T(8,128)S(1)}) custom-call(s32[5]{0:T(128)S(1)} %stack.23.meta.refs_0_, bf16[512,1024]{1,0:T(8,128)(2,1)S(1)} %get-tuple-element.62.refs_1_.own_ref, bf16[1024,1024]{1,0:T(8,128)(2,1)S(1)} %get-tuple-element.63.refs_2_.p_ref, f32[128,512]{1,0:T(8,128)S(1)} %get-tuple-element.66.refs_3_.refs_4_), custom_call_target="tpu_custom_call" | custom-call | flops 2147483648 | tf_op jit(solution)/shard_map/pallas_call | solution.py:92
  82.8 13.3 %all_to_all.15.refs_2_ = f32[32,2,512]{2,1,0:T(2,128)S(1)} all-to-all(f32[32,2,512]{2,1,0:T(2,128)S(1)} %broadcast_in_dim.22), channel_id=1, replica_groups=mesh['y'=4,'x'=4,'z'=8,'mp'=2] {'x','z'}, dimensions={0} | all-to-all | bytes 262144 | tf_op jit(solution)/shard_map/all_to_all | solution.py:25
  97.1 3.3 %collective-permute-start.15 = (bf16[1024,512]{1,0:T(8,128)(2,1)S(1)}, bf16[1024,512]{1,0:T(8,128)(2,1)S(1)}, u32[]{:S(2)}, u32[]{:S(2)}) collective-permute-start(bf16[1024,512]{1,0:T(8,128)(2,1)S(1)} %get-tuple-element.73.grad_ref), channel_id=1, source_target_pairs={{0,1},{1,0},{2,3},{3,2},{4,5},{5,4},{6,7},{7,6},{8,9},{9,8},{10,11... | collective-permute-start | bytes 3145736 | tf_op jit(solution)/shard_map/ppermute | solution.py:21
  107.4 2.9 %shard_map.96 = (bf16[256,1024]{1,0:T(8,128)(2,1)S(1)}, bf16[256,1024]{1,0:T(8,128)(2,1)S(1)}, bf16[128,1024]{1,0:T(8,128)(2,1)S(1)}, bf16[128,1024]{1,0:T(8,128)(2,1)S(1)}, bf16[256,1024]{1,0:T(8,128)(2,1)S(1)}) custom-call(s32[5]{0:T(128)S(1)} %stack.23.meta.refs_0_, bf16[1024,512]{1,0:T(8,128)(2,1)S(1)} %get-tuple-element.73.grad_ref, ...), custom_call_target="tpu_custom_call" | custom-call | flops 2147483648 | tf_op jit(solution)/shard_map/pallas_call | solution.py:92
  110.4 2.7 %collective-permute-start.21 = (bf16[128,1024]{1,0:T(8,128)(2,1)S(1)}, bf16[128,1024]{1,0:T(8,128)(2,1)S(1)}, u32[]{:S(2)}, u32[]{:S(2)}) collective-permute-start(bf16[128,1024]{1,0:T(8,128)(2,1)S(1)} %get-tuple-element.87), channel_id=1, source_target_pairs={{0,192},{64,0},{128,64},{192,128},{1,193},{65,1},{129,65},{193,129... | collective-permute-start | bytes 786440 | tf_op jit(solution)/shard_map/ppermute | solution.py:21
  113.7 2.7 %collective-permute-start.19 = (bf16[256,1024]{1,0:T(8,128)(2,1)S(1)}, bf16[256,1024]{1,0:T(8,128)(2,1)S(1)}, u32[]{:S(2)}, u32[]{:S(2)}) collective-permute-start(bf16[256,1024]{1,0:T(8,128)(2,1)S(1)} %get-tuple-element.81), channel_id=1, source_target_pairs={{0,48},{16,0},{32,16},{48,32},{1,49},{17,1},{33,17},{49,33},{2,50}... | collective-permute-start | bytes 1572872 | tf_op jit(solution)/shard_map/ppermute | solution.py:21
  121.3 4.0 %shard_map.98 = (bf16[2048,1024]{1,0:T(8,128)(2,1)S(1)}, bf16[2048,1024]{1,0:T(8,128)(2,1)S(1)}) custom-call(s32[5]{0:T(128)S(1)} %stack.23.meta.refs_0_, bf16[4096,1024]{1,0:T(8,128)(2,1)} %w_ref.3, bf16[4096,1024]{1,0:T(8,128)(2,1)} %collective-permute-done.2.wo_ref), custom_call_target="tpu_custom_call" | custom-call | tf_op jit(solution)/shard_map/pallas_call | solution.py:92
  127.3 4.1 %collective-permute-done.22.refs_1_ = bf16[256,1024]{1,0:T(8,128)(2,1)S(1)} collective-permute-done((bf16[256,1024]{1,0:T(8,128)(2,1)S(1)}, bf16[256,1024]{1,0:T(8,128)(2,1)S(1)}, u32[]{:S(2)}, u32[]{:S(2)}) %collective-permute-start.22) | collective-permute-done | bytes 524320 | tf_op jit(solution)/shard_map/ppermute | solution.py:21
  131.4 16.7 %all_to_all.16.refs_1_ = bf16[8,32,1024]{2,1,0:T(8,128)(2,1)S(1)} all-to-all(bf16[8,32,1024]{2,1,0:T(8,128)(2,1)S(1)} %bitcast.24), channel_id=1, replica_groups=mesh['y'=4,'x'=4,'z'=8,'mp'=2] {'z'}, dimensions={0} | all-to-all | bytes 1048576 | tf_op jit(solution)/shard_map/all_to_all | solution.py:25
  148.4 4.2 %collective-permute-start.25 = (bf16[256,1024]{1,0:T(8,128)(2,1)S(1)}, bf16[256,1024]{1,0:T(8,128)(2,1)S(1)}, u32[]{:S(2)}, u32[]{:S(2)}) collective-permute-start(bf16[256,1024]{1,0:T(8,128)(2,1)S(1)} %shard_map.100.pg_ref), channel_id=1, source_target_pairs={{0,1},{1,0},{2,3},{3,2},{4,5},{5,4},{6,7},{7,6},{8,9},{9,8},{10,11... | collective-permute-start | bytes 1572872 | tf_op jit(solution)/shard_map/ppermute | solution.py:21
  154.7 4.5 %shard_map.101 = (bf16[32,2048]{1,0:T(8,128)(2,1)}, bf16[256,2048]{1,0:T(8,128)(2,1)}, f32[1,128]{1,0:T(1,128)S(1)}) custom-call(s32[5]{0:T(128)S(1)} %stack.23.meta.refs_0_, f32[40,1024]{1,0:T(8,128)S(1)} %shard_map.99.qg_ref, f32[40,1024]{1,0:T(8,128)S(1)} %collective-permute-done.24.qgo_ref, bf16[256,1024]{1,0:T(8,128)(2,1)S(1)} %shard_map.100.pg_ref, ...), custom_call_target="tpu_custom_call" | custom-call | flops 2415919104 | tf_op jit(solution)/shard_map/pallas_call | solution.py:92
  (81 shorter events, 33.3 us)
Async XLA Ops:
  13.6 26.3 %collective-permute-start.2 = (bf16[4096,1024]{1,0:T(8,128)(2,1)}, bf16[4096,1024]{1,0:T(8,128)(2,1)}, u32[]{:S(2)}, u32[]{:S(2)}) collective-permute-start(bf16[4096,1024]{1,0:T(8,128)(2,1)} %w_ref.3), channel_id=1, source_target_pairs={{0,1},{1,0},{2,3},{3,2},{4,5},{5,4},{6,7},{7,6},{8,9},{9,8},{10,11... | collective-permute-start | bytes 25165832 | tf_op jit(solution)/shard_map/ppermute | solution.py:21
  13.9 26.0 %collective-permute-start.1 = (f32[288,1024]{1,0:T(8,128)S(1)}, f32[288,1024]{1,0:T(8,128)S(1)}, u32[]{:S(2)}, u32[]{:S(2)}) collective-permute-start(f32[288,1024]{1,0:T(8,128)S(1)} %get-tuple-element.56.unit_ref), channel_id=1, source_target_pairs={{0,1},{1,0},{2,3},{3,2},{4,5},{5,4},{6,7},{7,6},{8,9},{9,8},{10,11... | collective-permute-start | bytes 3538952 | tf_op jit(solution)/shard_map/ppermute | solution.py:21
  14.1 25.8 %all-to-all-start = ((bf16[8,32,1152]{2,1,0:T(8,128)(2,1)}), bf16[8,32,1152]{2,1,0:T(8,128)(2,1)S(1)}, u32[]{:S(2)}, u32[]{:S(2)}) async-start(bf16[8,32,1152]{2,1,0:T(8,128)(2,1)} %get-tuple-element.55), calls=%async_computation | async-start | bytes 1179648 | tf_op jit(solution)/shard_map/all_to_all | solution.py:25
  20.6 13.7 %collective-permute-start.4 = (bf16[256,1024]{1,0:T(8,128)(2,1)}, bf16[256,1024]{1,0:T(8,128)(2,1)S(1)}, u32[]{:S(2)}, u32[]{:S(2)}) collective-permute-start(bf16[256,1024]{1,0:T(8,128)(2,1)} %copy-done), channel_id=1, source_target_pairs={{0,192},{64,0},{128,64},{192,128},{1,193},{65,1},{129,65},{193,129... | collective-permute-start | bytes 1572872 | tf_op jit(solution)/shard_map/ppermute | solution.py:21
  23.3 14.1 %collective-permute-start.3 = (bf16[256,1024]{1,0:T(8,128)(2,1)}, bf16[256,1024]{1,0:T(8,128)(2,1)}, u32[]{:S(2)}, u32[]{:S(2)}) collective-permute-start(bf16[256,1024]{1,0:T(8,128)(2,1)} %copy-done), channel_id=1, source_target_pairs={{0,64},{64,128},{128,192},{192,0},{1,65},{65,129},{129,193},{193,1... | collective-permute-start | bytes 1572872 | tf_op jit(solution)/shard_map/ppermute | solution.py:21
  39.9 14.8 %collective-permute-start.7 = (bf16[256,1152]{1,0:T(8,128)(2,1)S(1)}, bf16[256,1152]{1,0:T(8,128)(2,1)S(1)}, u32[]{:S(2)}, u32[]{:S(2)}) collective-permute-start(bf16[256,1152]{1,0:T(8,128)(2,1)S(1)} %bitcast.21), channel_id=1, source_target_pairs={{0,48},{16,0},{32,16},{48,32},{1,49},{17,1},{33,17},{49,33},{2,50}... | collective-permute-start | bytes 1769480 | tf_op jit(solution)/shard_map/ppermute | solution.py:21
  42.5 15.7 %collective-permute-start.5 = (bf16[256,1152]{1,0:T(8,128)(2,1)S(1)}, bf16[256,1152]{1,0:T(8,128)(2,1)S(1)}, u32[]{:S(2)}, u32[]{:S(2)}) collective-permute-start(bf16[256,1152]{1,0:T(8,128)(2,1)S(1)} %bitcast.22), channel_id=1, source_target_pairs={{0,16},{16,32},{32,48},{48,0},{1,17},{17,33},{33,49},{49,1},{2,18}... | collective-permute-start | bytes 1769480 | tf_op jit(solution)/shard_map/ppermute | solution.py:21
  54.7 14.5 %collective-permute-start.8 = (bf16[128,1152]{1,0:T(8,128)(2,1)S(1)}, bf16[128,1152]{1,0:T(8,128)(2,1)S(1)}, u32[]{:S(2)}, u32[]{:S(2)}) collective-permute-start(bf16[128,1152]{1,0:T(8,128)(2,1)S(1)} %slice.21), channel_id=1, source_target_pairs={{0,48},{16,0},{32,16},{48,32},{1,49},{17,1},{33,17},{49,33},{2,50}... | collective-permute-start | bytes 884744 | tf_op jit(solution)/shard_map/ppermute | solution.py:21
  58.2 11.0 %collective-permute-start.6 = (bf16[128,1152]{1,0:T(8,128)(2,1)S(1)}, bf16[128,1152]{1,0:T(8,128)(2,1)S(1)}, u32[]{:S(2)}, u32[]{:S(2)}) collective-permute-start(bf16[128,1152]{1,0:T(8,128)(2,1)S(1)} %slice.20), channel_id=1, source_target_pairs={{0,16},{16,32},{32,48},{48,0},{1,17},{17,33},{33,49},{49,1},{2,18}... | collective-permute-start | bytes 884744 | tf_op jit(solution)/shard_map/ppermute | solution.py:21
  59.3 6.8 %collective-permute-start.10 = (bf16[128,1024]{1,0:T(8,128)(2,1)S(1)}, bf16[128,1024]{1,0:T(8,128)(2,1)S(1)}, u32[]{:S(2)}, u32[]{:S(2)}) collective-permute-start(bf16[128,1024]{1,0:T(8,128)(2,1)S(1)} %slice.18), channel_id=1, source_target_pairs={{0,192},{64,0},{128,64},{192,128},{1,193},{65,1},{129,65},{193,129... | collective-permute-start | bytes 786440 | tf_op jit(solution)/shard_map/ppermute | solution.py:21
  62.1 7.1 %collective-permute-start.9 = (bf16[128,1024]{1,0:T(8,128)(2,1)S(1)}, bf16[128,1024]{1,0:T(8,128)(2,1)S(1)}, u32[]{:S(2)}, u32[]{:S(2)}) collective-permute-start(bf16[128,1024]{1,0:T(8,128)(2,1)S(1)} %slice.17), channel_id=1, source_target_pairs={{0,64},{64,128},{128,192},{192,0},{1,65},{65,129},{129,193},{193,1... | collective-permute-start | bytes 786440 | tf_op jit(solution)/shard_map/ppermute | solution.py:21
  72.2 9.1 %collective-permute-start.11 = (f32[1024,512]{1,0:T(8,128)S(1)}, f32[1024,512]{1,0:T(8,128)S(1)}, u32[]{:S(2)}, u32[]{:S(2)}) collective-permute-start(f32[1024,512]{1,0:T(8,128)S(1)} %get-tuple-element.68), channel_id=1, source_target_pairs={{0,1},{1,0},{2,3},{3,2},{4,5},{5,4},{6,7},{7,6},{8,9},{9,8},{10,11... | collective-permute-start | bytes 6291464 | tf_op jit(solution)/shard_map/ppermute | solution.py:21
  76.1 4.8 %collective-permute-start.14 = (f32[8,256]{1,0:T(8,128)S(1)}, f32[8,256]{1,0:T(8,128)S(1)}, u32[]{:S(2)}, u32[]{:S(2)}) collective-permute-start(f32[8,256]{1,0:T(8,128)S(1)} %get-tuple-element.70.refs_5_), channel_id=1, source_target_pairs={{0,192},{64,0},{128,64},{192,128},{1,193},{65,1},{129,65},{193,129... | collective-permute-start | bytes 24584 | tf_op jit(solution)/shard_map/ppermute | solution.py:21
  76.2 4.7 %collective-permute-start.13 = (f32[8,256]{1,0:T(8,128)S(1)}, f32[8,256]{1,0:T(8,128)S(1)}, u32[]{:S(2)}, u32[]{:S(2)}) collective-permute-start(f32[8,256]{1,0:T(8,128)S(1)} %get-tuple-element.70.refs_5_), channel_id=1, source_target_pairs={{0,128},{64,192},{128,0},{192,64},{1,129},{65,193},{129,1},{193,65... | collective-permute-start | bytes 24584 | tf_op jit(solution)/shard_map/ppermute | solution.py:21
  97.1 5.6 %collective-permute-start.15 = (bf16[1024,512]{1,0:T(8,128)(2,1)S(1)}, bf16[1024,512]{1,0:T(8,128)(2,1)S(1)}, u32[]{:S(2)}, u32[]{:S(2)}) collective-permute-start(bf16[1024,512]{1,0:T(8,128)(2,1)S(1)} %get-tuple-element.73.grad_ref), channel_id=1, source_target_pairs={{0,1},{1,0},{2,3},{3,2},{4,5},{5,4},{6,7},{7,6},{8,9},{9,8},{10,11... | collective-permute-start | bytes 3145736 | tf_op jit(solution)/shard_map/ppermute | solution.py:21
  104.6 8.8 %collective-permute-start.16 = (bf16[128,1024]{1,0:T(8,128)(2,1)S(1)}, bf16[128,1024]{1,0:T(8,128)(2,1)S(1)}, u32[]{:S(2)}, u32[]{:S(2)}) collective-permute-start(bf16[128,1024]{1,0:T(8,128)(2,1)S(1)} %bitcast.29), channel_id=1, source_target_pairs={{0,16},{16,32},{32,48},{48,0},{1,17},{17,33},{33,49},{49,1},{2,18}... | collective-permute-start | bytes 786440 | tf_op jit(solution)/shard_map/ppermute | solution.py:21
  105.1 8.4 %collective-permute-start.17 = (bf16[128,1024]{1,0:T(8,128)(2,1)S(1)}, bf16[128,1024]{1,0:T(8,128)(2,1)S(1)}, u32[]{:S(2)}, u32[]{:S(2)}) collective-permute-start(bf16[128,1024]{1,0:T(8,128)(2,1)S(1)} %bitcast.28), channel_id=1, source_target_pairs={{0,48},{16,0},{32,16},{48,32},{1,49},{17,1},{33,17},{49,33},{2,50}... | collective-permute-start | bytes 786440 | tf_op jit(solution)/shard_map/ppermute | solution.py:21
  110.3 8.2 %collective-permute-start.20 = (bf16[128,1024]{1,0:T(8,128)(2,1)S(1)}, bf16[128,1024]{1,0:T(8,128)(2,1)S(1)}, u32[]{:S(2)}, u32[]{:S(2)}) collective-permute-start(bf16[128,1024]{1,0:T(8,128)(2,1)S(1)} %get-tuple-element.84), channel_id=1, source_target_pairs={{0,64},{64,128},{128,192},{192,0},{1,65},{65,129},{129,193},{193,1... | collective-permute-start | bytes 786440 | tf_op jit(solution)/shard_map/ppermute | solution.py:21
  110.4 8.1 %collective-permute-start.21 = (bf16[128,1024]{1,0:T(8,128)(2,1)S(1)}, bf16[128,1024]{1,0:T(8,128)(2,1)S(1)}, u32[]{:S(2)}, u32[]{:S(2)}) collective-permute-start(bf16[128,1024]{1,0:T(8,128)(2,1)S(1)} %get-tuple-element.87), channel_id=1, source_target_pairs={{0,192},{64,0},{128,64},{192,128},{1,193},{65,1},{129,65},{193,129... | collective-permute-start | bytes 786440 | tf_op jit(solution)/shard_map/ppermute | solution.py:21
  113.6 13.5 %collective-permute-start.18 = (bf16[256,1024]{1,0:T(8,128)(2,1)S(1)}, bf16[256,1024]{1,0:T(8,128)(2,1)S(1)}, u32[]{:S(2)}, u32[]{:S(2)}) collective-permute-start(bf16[256,1024]{1,0:T(8,128)(2,1)S(1)} %get-tuple-element.80), channel_id=1, source_target_pairs={{0,16},{16,32},{32,48},{48,0},{1,17},{17,33},{33,49},{49,1},{2,18}... | collective-permute-start | bytes 1572872 | tf_op jit(solution)/shard_map/ppermute | solution.py:21
  113.7 13.4 %collective-permute-start.19 = (bf16[256,1024]{1,0:T(8,128)(2,1)S(1)}, bf16[256,1024]{1,0:T(8,128)(2,1)S(1)}, u32[]{:S(2)}, u32[]{:S(2)}) collective-permute-start(bf16[256,1024]{1,0:T(8,128)(2,1)S(1)} %get-tuple-element.81), channel_id=1, source_target_pairs={{0,48},{16,0},{32,16},{48,32},{1,49},{17,1},{33,17},{49,33},{2,50}... | collective-permute-start | bytes 1572872 | tf_op jit(solution)/shard_map/ppermute | solution.py:21
  118.6 12.9 %collective-permute-start.22 = (bf16[256,1024]{1,0:T(8,128)(2,1)S(1)}, bf16[256,1024]{1,0:T(8,128)(2,1)S(1)}, u32[]{:S(2)}, u32[]{:S(2)}) collective-permute-start(bf16[256,1024]{1,0:T(8,128)(2,1)S(1)} %get-tuple-element.88), channel_id=1, source_target_pairs={{0,64},{64,128},{128,192},{192,0},{1,65},{65,129},{129,193},{193,1... | collective-permute-start | bytes 1572872 | tf_op jit(solution)/shard_map/ppermute | solution.py:21
  119.1 12.4 %collective-permute-start.23 = (bf16[256,1024]{1,0:T(8,128)(2,1)S(1)}, bf16[256,1024]{1,0:T(8,128)(2,1)S(1)}, u32[]{:S(2)}, u32[]{:S(2)}) collective-permute-start(bf16[256,1024]{1,0:T(8,128)(2,1)S(1)} %get-tuple-element.89), channel_id=1, source_target_pairs={{0,192},{64,0},{128,64},{192,128},{1,193},{65,1},{129,65},{193,129... | collective-permute-start | bytes 1572872 | tf_op jit(solution)/shard_map/ppermute | solution.py:21
  148.4 6.3 %collective-permute-start.25 = (bf16[256,1024]{1,0:T(8,128)(2,1)S(1)}, bf16[256,1024]{1,0:T(8,128)(2,1)S(1)}, u32[]{:S(2)}, u32[]{:S(2)}) collective-permute-start(bf16[256,1024]{1,0:T(8,128)(2,1)S(1)} %shard_map.100.pg_ref), channel_id=1, source_target_pairs={{0,1},{1,0},{2,3},{3,2},{4,5},{5,4},{6,7},{7,6},{8,9},{9,8},{10,11... | collective-permute-start | bytes 1572872 | tf_op jit(solution)/shard_map/ppermute | solution.py:21
  (10 other events, 95.4 us)

commit v5 on v4

--- a/solution.py
+++ b/solution.py
@@ -273,21 +273,24 @@
     return (rem(meta[3] - line + n_y, n_y) * slots + meta[1]).astype(f32)
 
 
+def side_rows(ref, i, width):
+    value = ref[:, :width].reshape(-1, 2, 16, width)
+    return value[:, i].reshape(value.shape[0] * 16, width)
+
+
 def score_sent_body(n_pieces, meta, *refs):
-    q_refs, p_refs = refs[:n_pieces[0]], refs[n_pieces[0] : sum(n_pieces)]
-    score_ref, own_ref, other_ref, all_ref, aux_ref, aux_other_ref = refs[sum(n_pieces) :]
-    width = own_ref.shape[1]
+    q_refs, p_refs = refs[: n_pieces[0]], refs[n_pieces[0] : sum(n_pieces)]
+    score_ref, other_ref, aux_ref, aux_other_ref = refs[sum(n_pieces) :]
+    width = other_ref.shape[1]
     at = 0
     for ref in q_refs:
-        value = ref[...].reshape(-1, 2, 16, ref.shape[1])
-        rows = value.shape[0] * 16
-        for i, (to_ref, aux) in enumerate(((own_ref, aux_ref), (other_ref, aux_other_ref))):
-            side = value[:, i].reshape(rows, -1)
-            to_ref[at : at + rows] = side[:, :width]
-            aux[at : at + rows] = side[:, width:].astype(f32)
+        rows = ref.shape[0] // 2
+        other_ref[at : at + rows] = side_rows(ref, 1, width)
+        value = ref[:, width:].reshape(-1, 2, 16, AUX)
+        for i, aux in enumerate((aux_ref, aux_other_ref)):
+            aux[at : at + rows] = value[:, i].reshape(rows, AUX).astype(f32)
         at += rows
     for at, ref in pieces_at(p_refs):
-        all_ref[at] = ref[...]
         score_ref[at] = contract(ref[...], other_ref[...], ((1,), (1,)))
 
 
@@ -305,8 +308,6 @@
         [
             struct((passages, rows)),
             struct((rows, width), bf16),
-            struct((rows, width), bf16),
-            struct((passages, width), bf16),
             struct((rows, AUX)),
             struct((rows, AUX)),
         ],
@@ -335,9 +336,18 @@
     )
 
 
-def score_kept_body(n_y, slots, per_query, meta, q_ref, p_ref, info_ref, score_ref, weight_ref):
+def score_kept_body(n_y, slots, per_query, n_pieces, meta, info_ref, *refs):
+    q_refs, p_refs = refs[: n_pieces[0]], refs[n_pieces[0] : sum(n_pieces)]
+    score_ref, weight_ref, q_ref, p_ref = refs[sum(n_pieces) :]
     passages, rows = score_ref.shape
     block = passages // n_y
+    at = 0
+    for ref in q_refs:
+        n = ref.shape[0] // 2
+        q_ref[at : at + n] = side_rows(ref, 0, q_ref.shape[1])
+        at += n
+    for at, ref in pieces_at(p_refs):
+        p_ref[at] = ref[...]
     for line in range(n_y):
         owner = owner_of(meta, line, n_y, slots)
         place = jnp.where(info_ref[:INDEX] == owner, info_ref[INDEX : 2 * INDEX], -1.0)
@@ -351,17 +361,24 @@
             weight_ref[line * block + span.start : line * block + span.stop] = weight
 
 
-def score_kept(meta, q_own, p_all, info, n_y, slots, per_query):
-    passages, rows = p_all.shape[0], q_own.shape[0]
+def score_kept(meta, info, q_pieces, p_pieces, n_y, slots, per_query):
+    width = p_pieces[0].shape[1]
+    passages = sum(p.shape[0] for p in p_pieces)
+    rows = sum(q.shape[0] for q in q_pieces) // 2
 
     def body(*refs):
-        score_kept_body(n_y, slots, per_query, *refs)
+        score_kept_body(n_y, slots, per_query, (len(q_pieces), len(p_pieces)), *refs)
 
     return call(
         body,
-        [meta, q_own, p_all, info],
-        [struct((passages, rows)), struct((passages, rows))],
-        flops=4 * rows * passages * p_all.shape[1],
+        [meta, info] + q_pieces + p_pieces,
+        [
+            struct((passages, rows)),
+            struct((passages, rows)),
+            struct((rows, width), bf16),
+            struct((passages, width), bf16),
+        ],
+        flops=4 * rows * passages * width,
     )
 
 
@@ -474,44 +491,58 @@
     )[0]
 
 
-def query_rest_body(meta, grad_ref, p_ref, first_ref, *refs):
-    out_refs, turned_ref = refs[:-1], refs[-1]
-    turned_ref[...] = grad_ref[...].T
-    for span in spans(p_ref.shape[1], TILE):
-        rest = contract(turned_ref[...], p_ref[:, span], ((1,), (0,))).astype(bf16)
-        at = 0
-        for ref in out_refs:
-            rows = ref.shape[0] * 16
-            for i, value in enumerate((first_ref[at : at + rows, span], rest[at : at + rows])):
+def ranges_of(shapes, chosen):
+    starts = [sum(shapes[:i]) for i in range(len(shapes))]
+    return [slice(starts[i], starts[i] + shapes[i]) for i in chosen]
+
+
+def query_rest_body(ranges, meta, grad_ref, p_ref, first_ref, *refs):
+    out_refs, turned_refs = refs[: len(ranges)], refs[len(ranges) :]
+    for at, ref, turned_ref in zip(ranges, out_refs, turned_refs):
+        rows = slice(at.start // 2, at.stop // 2)
+        turned_ref[...] = grad_ref[:, rows].T
+        for span in spans(p_ref.shape[1], TILE):
+            rest = contract(turned_ref[...], p_ref[:, span], ((1,), (0,))).astype(bf16)
+            for i, value in enumerate((first_ref[rows, span], rest)):
                 ref[:, i, :, span] = value.reshape(-1, 16, value.shape[1])
-            at += rows
-
-
-def query_rest(meta, grad, p_all, first, shapes):
-    (passages, rows), width = grad.shape, p_all.shape[1]
-    return call(
-        query_rest_body,
+
+
+def query_rest(meta, grad, p_all, first, shapes, chosen):
+    passages, width = p_all.shape
+    ranges = ranges_of(shapes, chosen)
+
+    def body(*refs):
+        query_rest_body(ranges, *refs)
+
+    parts = call(
+        body,
         [meta, grad, p_all, first],
-        [struct((n // 32, 2, 16, width), bf16) for n in shapes],
-        [pltpu.VMEM((rows, passages), bf16)],
-        2 * rows * passages * width,
-    )
-
-
-def passage_part_body(meta, grad_ref, other_ref, own_ref, q_ref, *out_refs):
-    for at, ref in pieces_at(out_refs):
+        [struct((shapes[i] // 32, 2, 16, width), bf16) for i in chosen],
+        [pltpu.VMEM((shapes[i] // 2, passages), bf16) for i in chosen],
+        sum(shapes[i] for i in chosen) * passages * width,
+    )
+    return [part.reshape(-1, width) for part in parts]
+
+
+def passage_part_body(ranges, meta, grad_ref, other_ref, own_ref, q_ref, *out_refs):
+    for at, ref in zip(ranges, out_refs):
         value = contract(grad_ref[at], own_ref[...], ((1,), (0,)))
         value = value + contract(other_ref[at], q_ref[...], ((1,), (0,)))
         ref[...] = value.astype(bf16)
 
 
-def passage_part(meta, grad, other, q_own, q_other, shapes):
-    (passages, rows), width = grad.shape, q_own.shape[1]
-    return call(
-        passage_part_body,
+def passage_part(meta, grad, other, q_own, q_other, shapes, chosen):
+    rows, width = q_own.shape
+    ranges = ranges_of(shapes, chosen)
+
+    def body(*refs):
+        passage_part_body(ranges, *refs)
+
+    return call(
+        body,
         [meta, grad, other, q_own, q_other],
-        [struct((n, width), bf16) for n in shapes],
-        flops=4 * rows * passages * width,
+        [struct((shapes[i], width), bf16) for i in chosen],
+        flops=4 * rows * sum(shapes[i] for i in chosen) * width,
     )
 
 
@@ -620,28 +651,41 @@
     )
     unit_got = shifted(unit, "mp", 1)
     weight_got = shifted(after(head_weight, unit), "mp", 1)
-    p_near = ring_near(p_embed, "y")
+    p_pieces = [p_embed] + [shifted(p_embed, "y", s) for s in range(1, n_y)]
     q_z = exchanged(message, "z").reshape(n_z * q_rows, width + AUX)
-    q_z = after(q_z, unit_got, weight_got, *p_near)
+    q_z = after(q_z, unit_got, weight_got)
     q_near = ring_near(q_z, "x")
     q_pieces = ring_far(q_z, q_near, "x")
-    p_pieces = ring_far(p_embed, [after(piece, *q_near) for piece in p_near], "y")
-    q_shapes, p_shapes = ([piece.shape[0] for piece in pieces] for pieces in (q_pieces, p_pieces))
-    sent, q_own, q_other, p_all, aux, aux_other = score_sent(meta, q_pieces, p_pieces)
+    q_shapes = [piece.shape[0] for piece in q_pieces]
+    p_shapes = [p_rows, p_rows, p_rows // 2, p_rows // 2, p_rows] if n_y == 4 else [p_rows, p_rows]
+    sent, q_other, aux, aux_other = score_sent(meta, q_pieces, p_pieces)
     got = shifted(sent, "mp", 1)
     info, count = count_positives(meta, aux, aux_other, p_rows, slots)
     counts = [count] + [shifted(count, "y", s) for s in range(1, n_y)]
-    kept, named = score_kept(meta, q_own, p_all, info, n_y, slots, per_query)
+    kept, named, q_own, p_all = score_kept(
+        meta, info, q_pieces, p_pieces, n_y, slots, per_query
+    )
     e, sums = weigh(meta, kept, got, named, info, counts, n_y, n_x, slots)
     sums = to_all(sums, ("x", "z")).reshape((slots,) + sums.shape)
     grad, loss = slopes(meta, e, sums, info, n_y, n_x, slots)
     grad_got = shifted(grad, "mp", 1)
     q_part = query_part(meta, grad, p_all)
     grad_got = after(grad_got, q_part)
-    p_parts = passage_part(meta, grad, grad_got, q_own, q_other, p_shapes)
-    q_parts = query_rest(meta, grad_got, p_all, q_part, q_shapes)
-    q_parts = [part.reshape(-1, width) for part in q_parts]
-    p_far, q_far = return_far(p_parts, "y"), return_far(q_parts, "x")
+    far, near = ((2, 3), (0, 1, 4)) if len(q_shapes) > 2 else ((1,), (0,))
+    q_parts, p_parts = [None] * len(q_shapes), [None] * len(p_shapes)
+
+    def fill(parts, chosen, values):
+        for i, value in zip(chosen, values):
+            parts[i] = value
+
+    fill(q_parts, far, query_rest(meta, grad_got, p_all, q_part, q_shapes, far))
+    q_far = return_far(q_parts, "x")
+    grad_next = after(grad_got, q_parts[far[0]])
+    fill(p_parts, far, passage_part(meta, grad, grad_next, q_own, q_other, p_shapes, far))
+    p_far = return_far(p_parts, "y")
+    grad_last = after(grad_got, p_parts[far[0]])
+    fill(q_parts, near, query_rest(meta, grad_last, p_all, q_part, q_shapes, near))
+    fill(p_parts, near, passage_part(meta, grad, grad_last, q_own, q_other, p_shapes, near))
     q_leaving = join(q_parts, q_far)
     p_leaving = join(p_parts, [after(p_far[0], *q_leaving)] + p_far[1:])
     p_coming = near_coming(p_leaving, "y")

time: 160 us -> 154 us (0.963)
  blocking collectives: 30 us -> 53.4 us
  waiting for transfers between devices: 46.7 us -> 25.8 us
  starting transfers between devices: 45.2 us -> 39.3 us
  local copies, waits for them, and re-layouts: 3.68 us -> 1.22 us
    all_to_all x2 -> x3, blocking collectives: 30 us -> 53.4 us  [exchanged(): return lax.all_to_all(parts, axis, split_axis=0, concat_axis=0, tiled=True)]
    ppermute x26 -> x25, waiting for transfers between devices: 44.1 us -> 25.8 us  [shifted(): return lax.ppermute(value, axis, [(i, (i + shift) % n) for i in range(n)])]
    all_to_all x1 -> x0, starting transfers between devices: 6.45 us -> none  [exchanged(): return lax.all_to_all(parts, axis, split_axis=0, concat_axis=0, tiled=True)]
    all_to_all x1 -> x0, waiting for transfers between devices: 2.56 us -> none  [exchanged(): return lax.all_to_all(parts, axis, split_axis=0, concat_axis=0, tiled=True)]
    ppermute x26 -> x25, starting transfers between devices: 38.8 us -> 39.3 us  [shifted(): return lax.ppermute(value, axis, [(i, (i + shift) % n) for i in range(n)])]
    pallas_call x17 -> x19, Pallas kernels: 33.1 us -> 33.1 us  [call(): pl.pallas_call(body, in_specs=specs, out_specs=[pl.BlockSpec(memory_space...]
  transfers between devices with their start and end apart: 27 -> 25, of which waited for: 14 -> 8; matrix products, arithmetic and copies ran while one was open for 1% -> 0% of each run, Pallas kernels for 9% -> 11%
where the time goes in v5:
time: 154 us
  blocking collectives  53.4 us (35%)
  starting transfers between devices  39.3 us (26%)
  Pallas kernels  33.1 us (21%)
  waiting for transfers between devices  25.8 us (17%)
    all_to_all x3, blocking collectives, exchanged(): return lax.all_to_all(parts, axis, split_axis=0, concat_axis=0, tiled=True)  53.4 us
    ppermute x25, starting transfers between devices, shifted(): return lax.ppermute(value, axis, [(i, (i + shift) % n) for i in range(n)])  39.3 us
    pallas_call x19, Pallas kernels, call(): pl.pallas_call(body, in_specs=specs, out_specs=[pl.BlockSpec(memory_space...  33.1 us
    ppermute x25, waiting for transfers between devices, shifted(): return lax.ppermute(value, axis, [(i, (i + shift) % n) for i in range(n)])  25.8 us
  transfers between devices with their start and end apart: 25, of which 8 were waited for; matrix products, arithmetic and copies ran while one was open for 0% of the time, Pallas kernels for 11%

profile of v5, /device:TPU:1, one launch (start us, length us, event | category | flops | bytes accessed | tf_op | source)
XLA Modules:
  0.0 153.8 jit_solution(3220328304018815785)
XLA Ops:
  0.7 5.6 %shard_map.85 = (f32[32,1024]{1,0:T(8,128)S(1)}, f32[256,1024]{1,0:T(8,128)S(1)}, f32[1,384]{1,0:T(1,128)S(1)}) custom-call(s32[5]{0:T(128)S(1)} %stack.23.meta.refs_0_, bf16[32,4096]{1,0:T(8,128)(2,1)} %q_ref.1, bf16[256,4096]{1,0:T(8,128)(2,1)} %p_ref.1, bf16[4096,1024]{1,0:T(8,128)(2,1)} %w_ref.3), custom_call_target="tpu_custom_call" | custom-call | flops 2415919104 | tf_op jit(solution)/shard_map/pallas_call | solution.py:92
  6.4 3.3 %collective-permute-start = (f32[1,384]{1,0:T(1,128)S(1)}, f32[1,384]{1,0:T(1,128)S(1)}, u32[]{:S(2)}, u32[]{:S(2)}) collective-permute-start(f32[1,384]{1,0:T(1,128)S(1)} %get-tuple-element.54.own_ref), channel_id=1, source_target_pairs={{0,1},{1,0},{2,3},{3,2},{4,5},{5,4},{6,7},{7,6},{8,9},{9,8},{10,11... | collective-permute-start | bytes 4616 | tf_op jit(solution)/shard_map/ppermute | solution.py:21
  12.0 24.7 %all_to_all.15 = bf16[8,32,1152]{2,1,0:T(8,128)(2,1)S(1)} all-to-all(bf16[8,32,1152]{2,1,0:T(8,128)(2,1)S(1)} %get-tuple-element.55), channel_id=1, replica_groups=mesh['y'=4,'x'=4,'z'=8,'mp'=2] {'z'}, dimensions={0} | all-to-all | bytes 1179648 | tf_op jit(solution)/shard_map/all_to_all | solution.py:25
  40.8 2.6 %collective-permute-start.8 = (bf16[256,1024]{1,0:T(8,128)(2,1)S(1)}, bf16[256,1024]{1,0:T(8,128)(2,1)S(1)}, u32[]{:S(2)}, u32[]{:S(2)}) collective-permute-start(bf16[256,1024]{1,0:T(8,128)(2,1)S(1)} %get-tuple-element.59.refs_6_.refs_7_), channel_id=1, source_target_pairs={{0,128},{64,192},{128,0},{192,64},{1,129},{65,193},{129,1},{193,65... | collective-permute-start | bytes 1572872 | tf_op jit(solution)/shard_map/ppermute | solution.py:21
  44.5 7.0 %collective-permute-done.3.refs_2_.refs_3_ = bf16[256,1152]{1,0:T(8,128)(2,1)S(1)} collective-permute-done((bf16[256,1152]{1,0:T(8,128)(2,1)S(1)}, bf16[256,1152]{1,0:T(8,128)(2,1)S(1)}, u32[]{:S(2)}, u32[]{:S(2)}) %collective-permute-start.3) | collective-permute-done | bytes 589856 | tf_op jit(solution)/shard_map/ppermute | solution.py:21
  51.6 2.7 %collective-permute-start.6 = (bf16[128,1152]{1,0:T(8,128)(2,1)S(1)}, bf16[128,1152]{1,0:T(8,128)(2,1)S(1)}, u32[]{:S(2)}, u32[]{:S(2)}) collective-permute-start(bf16[128,1152]{1,0:T(8,128)(2,1)S(1)} %slice.13), channel_id=1, source_target_pairs={{0,48},{16,0},{32,16},{48,32},{1,49},{17,1},{33,17},{49,33},{2,50}... | collective-permute-start | bytes 884744 | tf_op jit(solution)/shard_map/ppermute | solution.py:21
  54.3 10.3 %collective-permute-done.8.refs_8_.refs_9_ = bf16[256,1024]{1,0:T(8,128)(2,1)S(1)} collective-permute-done((bf16[256,1024]{1,0:T(8,128)(2,1)S(1)}, bf16[256,1024]{1,0:T(8,128)(2,1)S(1)}, u32[]{:S(2)}, u32[]{:S(2)}) %collective-permute-start.8) | collective-permute-done | bytes 524320 | tf_op jit(solution)/shard_map/ppermute | solution.py:21
  65.4 1.9 %shard_map.87 = (f32[1024,512]{1,0:T(8,128)S(1)}, bf16[512,1024]{1,0:T(8,128)(2,1)S(1)}, f32[512,128]{1,0:T(8,128)S(1)}, f32[512,128]{1,0:T(8,128)S(1)}) custom-call(s32[5]{0:T(128)S(1)} %stack.23.meta.refs_0_, bf16[256,1152]{1,0:T(8,128)(2,1)S(1)} %bitcast.23, bf16[256,1152]{1,0:T(8,128)(2,1)S(1)} %collective-permute-done.3.refs_2_.refs_3_, ...), custom_call_target="tpu_custom_call" | custom-call | flops 1073741824 | tf_op jit(solution)/shard_map/pallas_call | solution.py:92
  67.3 2.2 %collective-permute-start.10 = (f32[1024,512]{1,0:T(8,128)S(1)}, f32[1024,512]{1,0:T(8,128)S(1)}, u32[]{:S(2)}, u32[]{:S(2)}) collective-permute-start(f32[1024,512]{1,0:T(8,128)S(1)} %get-tuple-element.64), channel_id=1, source_target_pairs={{0,1},{1,0},{2,3},{3,2},{4,5},{5,4},{6,7},{7,6},{8,9},{9,8},{10,11... | collective-permute-start | bytes 6291464 | tf_op jit(solution)/shard_map/ppermute | solution.py:21
  71.3 2.1 %collective-permute-start.12 = (f32[8,256]{1,0:T(8,128)S(1)}, f32[8,256]{1,0:T(8,128)S(1)}, u32[]{:S(2)}, u32[]{:S(2)}) collective-permute-start(f32[8,256]{1,0:T(8,128)S(1)} %get-tuple-element.66.refs_5_), channel_id=1, source_target_pairs={{0,128},{64,192},{128,0},{192,64},{1,129},{65,193},{129,1},{193,65... | collective-permute-start | bytes 24584 | tf_op jit(solution)/shard_map/ppermute | solution.py:21
  74.8 3.3 %shard_map.89 = (f32[1024,512]{1,0:T(8,128)S(1)}, f32[1024,512]{1,0:T(8,128)S(1)}, bf16[512,1024]{1,0:T(8,128)(2,1)S(1)}, bf16[1024,1024]{1,0:T(8,128)(2,1)S(1)}) custom-call(s32[5]{0:T(128)S(1)} %stack.23.meta.refs_0_, f32[128,512]{1,0:T(8,128)S(1)} %get-tuple-element.62.refs_1_.refs_4_.refs_3_, bf16[256,1152]{1,0:T(8,128)(2,1)S(1)} %bitcast.24, ...), custom_call_target="tpu_custom_call" | custom-call | flops 2147483648 | tf_op jit(solution)/shard_map/pallas_call | solution.py:92
  79.6 12.5 %all_to_all.16.refs_2_ = f32[32,2,512]{2,1,0:T(2,128)S(1)} all-to-all(f32[32,2,512]{2,1,0:T(2,128)S(1)} %broadcast_in_dim.22), channel_id=1, replica_groups=mesh['y'=4,'x'=4,'z'=8,'mp'=2] {'x','z'}, dimensions={0} | all-to-all | bytes 262144 | tf_op jit(solution)/shard_map/all_to_all | solution.py:25
  93.1 2.3 %collective-permute-start.14 = (bf16[1024,512]{1,0:T(8,128)(2,1)S(1)}, bf16[1024,512]{1,0:T(8,128)(2,1)S(1)}, u32[]{:S(2)}, u32[]{:S(2)}) collective-permute-start(bf16[1024,512]{1,0:T(8,128)(2,1)S(1)} %get-tuple-element.69.grad_ref.refs_1_), channel_id=1, source_target_pairs={{0,1},{1,0},{2,3},{3,2},{4,5},{5,4},{6,7},{7,6},{8,9},{9,8},{10,11... | collective-permute-start | bytes 3145736 | tf_op jit(solution)/shard_map/ppermute | solution.py:21
  99.6 2.3 %collective-permute-start.16 = (bf16[128,1024]{1,0:T(8,128)(2,1)S(1)}, bf16[128,1024]{1,0:T(8,128)(2,1)S(1)}, u32[]{:S(2)}, u32[]{:S(2)}) collective-permute-start(bf16[128,1024]{1,0:T(8,128)(2,1)S(1)} %bitcast.29), channel_id=1, source_target_pairs={{0,48},{16,0},{32,16},{48,32},{1,49},{17,1},{33,17},{49,33},{2,50}... | collective-permute-start | bytes 786440 | tf_op jit(solution)/shard_map/ppermute | solution.py:21
  103.3 2.6 %collective-permute-start.20 = (bf16[128,1024]{1,0:T(8,128)(2,1)S(1)}, bf16[128,1024]{1,0:T(8,128)(2,1)S(1)}, u32[]{:S(2)}, u32[]{:S(2)}) collective-permute-start(bf16[128,1024]{1,0:T(8,128)(2,1)S(1)} %get-tuple-element.87), channel_id=1, source_target_pairs={{0,192},{64,0},{128,64},{192,128},{1,193},{65,1},{129,65},{193,129... | collective-permute-start | bytes 786440 | tf_op jit(solution)/shard_map/ppermute | solution.py:21
  107.5 2.3 %shard_map.98 = (bf16[256,1024]{1,0:T(8,128)(2,1)S(1)}, bf16[256,1024]{1,0:T(8,128)(2,1)S(1)}, bf16[256,1024]{1,0:T(8,128)(2,1)S(1)}) custom-call(s32[5]{0:T(128)S(1)} %stack.23.meta.refs_0_, bf16[1024,512]{1,0:T(8,128)(2,1)S(1)} %get-tuple-element.69.grad_ref.refs_1_, bf16[1024,512]{1,0:T(8,128)(2,1)S(1)} %collective-permute-done.14.refs_1_.refs_2_, ...), custom_call_target="tpu_custom_call" | custom-call | flops 1610612736 | tf_op jit(solution)/shard_map/pallas_call | solution.py:92
  110.1 2.7 %collective-permute-start.18 = (bf16[256,1024]{1,0:T(8,128)(2,1)S(1)}, bf16[256,1024]{1,0:T(8,128)(2,1)S(1)}, u32[]{:S(2)}, u32[]{:S(2)}) collective-permute-start(bf16[256,1024]{1,0:T(8,128)(2,1)S(1)} %get-tuple-element.83), channel_id=1, source_target_pairs={{0,48},{16,0},{32,16},{48,32},{1,49},{17,1},{33,17},{49,33},{2,50}... | collective-permute-start | bytes 1572872 | tf_op jit(solution)/shard_map/ppermute | solution.py:21
  113.0 2.7 %collective-permute-start.22 = (bf16[256,1024]{1,0:T(8,128)(2,1)S(1)}, bf16[256,1024]{1,0:T(8,128)(2,1)S(1)}, u32[]{:S(2)}, u32[]{:S(2)}) collective-permute-start(bf16[256,1024]{1,0:T(8,128)(2,1)S(1)} %get-tuple-element.89), channel_id=1, source_target_pairs={{0,192},{64,0},{128,64},{192,128},{1,193},{65,1},{129,65},{193,129... | collective-permute-start | bytes 1572872 | tf_op jit(solution)/shard_map/ppermute | solution.py:21
  115.7 4.0 %shard_map.100 = (bf16[2048,1024]{1,0:T(8,128)(2,1)S(1)}, bf16[2048,1024]{1,0:T(8,128)(2,1)S(1)}) custom-call(s32[5]{0:T(128)S(1)} %stack.23.meta.refs_0_, bf16[4096,1024]{1,0:T(8,128)(2,1)} %w_ref.3, bf16[4096,1024]{1,0:T(8,128)(2,1)} %copy-done), custom_call_target="tpu_custom_call" | custom-call | tf_op jit(solution)/shard_map/pallas_call | solution.py:92
  119.7 3.5 %collective-permute-done.17.refs_1_ = bf16[256,1024]{1,0:T(8,128)(2,1)S(1)} collective-permute-done((bf16[256,1024]{1,0:T(8,128)(2,1)S(1)}, bf16[256,1024]{1,0:T(8,128)(2,1)S(1)}, u32[]{:S(2)}, u32[]{:S(2)}) %collective-permute-start.17) | collective-permute-done | bytes 524320 | tf_op jit(solution)/shard_map/ppermute | solution.py:21
  123.5 2.1 %collective-permute-done.21.refs_1_ = bf16[256,1024]{1,0:T(8,128)(2,1)S(1)} collective-permute-done((bf16[256,1024]{1,0:T(8,128)(2,1)S(1)}, bf16[256,1024]{1,0:T(8,128)(2,1)S(1)}, u32[]{:S(2)}, u32[]{:S(2)}) %collective-permute-start.21) | collective-permute-done | bytes 524320 | tf_op jit(solution)/shard_map/ppermute | solution.py:21
  125.6 16.1 %all_to_all.17.refs_1_ = bf16[8,32,1024]{2,1,0:T(8,128)(2,1)S(1)} all-to-all(bf16[8,32,1024]{2,1,0:T(8,128)(2,1)S(1)} %bitcast.25), channel_id=1, replica_groups=mesh['y'=4,'x'=4,'z'=8,'mp'=2] {'z'}, dimensions={0} | all-to-all | bytes 1048576 | tf_op jit(solution)/shard_map/all_to_all | solution.py:25
  141.9 4.8 %collective-permute-start.24 = (bf16[256,1024]{1,0:T(8,128)(2,1)S(1)}, bf16[256,1024]{1,0:T(8,128)(2,1)S(1)}, u32[]{:S(2)}, u32[]{:S(2)}) collective-permute-start(bf16[256,1024]{1,0:T(8,128)(2,1)S(1)} %shard_map.102.pg_ref), channel_id=1, source_target_pairs={{0,1},{1,0},{2,3},{3,2},{4,5},{5,4},{6,7},{7,6},{8,9},{9,8},{10,11... | collective-permute-start | bytes 1572872 | tf_op jit(solution)/shard_map/ppermute | solution.py:21
  148.8 4.5 %shard_map.103 = (bf16[32,2048]{1,0:T(8,128)(2,1)}, bf16[256,2048]{1,0:T(8,128)(2,1)}, f32[1,128]{1,0:T(1,128)S(1)}) custom-call(s32[5]{0:T(128)S(1)} %stack.23.meta.refs_0_, f32[40,1024]{1,0:T(8,128)S(1)} %shard_map.101.qg_ref, f32[40,1024]{1,0:T(8,128)S(1)} %collective-permute-done.23.qgo_ref, bf16[256,1024]{1,0:T(8,128)(2,1)S(1)} %shard_map.102.pg_ref, ...), custom_call_target="tpu_custom_call" | custom-call | flops 2415919104 | tf_op jit(solution)/shard_map/pallas_call | solution.py:92
  (72 shorter events, 24.5 us)
Async XLA Ops:
  6.4 4.1 %collective-permute-start = (f32[1,384]{1,0:T(1,128)S(1)}, f32[1,384]{1,0:T(1,128)S(1)}, u32[]{:S(2)}, u32[]{:S(2)}) collective-permute-start(f32[1,384]{1,0:T(1,128)S(1)} %get-tuple-element.54.own_ref), channel_id=1, source_target_pairs={{0,1},{1,0},{2,3},{3,2},{4,5},{5,4},{6,7},{7,6},{8,9},{9,8},{10,11... | collective-permute-start | bytes 4616 | tf_op jit(solution)/shard_map/ppermute | solution.py:21
  11.4 25.3 %collective-permute-start.2 = (bf16[4096,1024]{1,0:T(8,128)(2,1)}, bf16[4096,1024]{1,0:T(8,128)(2,1)S(1)}, u32[]{:S(2)}, u32[]{:S(2)}) collective-permute-start(bf16[4096,1024]{1,0:T(8,128)(2,1)} %w_ref.3), channel_id=1, source_target_pairs={{0,1},{1,0},{2,3},{3,2},{4,5},{5,4},{6,7},{7,6},{8,9},{9,8},{10,11... | collective-permute-start | bytes 25165832 | tf_op jit(solution)/shard_map/ppermute | solution.py:21
  11.8 24.9 %collective-permute-start.1 = (f32[288,1024]{1,0:T(8,128)S(1)}, f32[288,1024]{1,0:T(8,128)S(1)}, u32[]{:S(2)}, u32[]{:S(2)}) collective-permute-start(f32[288,1024]{1,0:T(8,128)S(1)} %get-tuple-element.56.unit_ref), channel_id=1, source_target_pairs={{0,1},{1,0},{2,3},{3,2},{4,5},{5,4},{6,7},{7,6},{8,9},{9,8},{10,11... | collective-permute-start | bytes 3538952 | tf_op jit(solution)/shard_map/ppermute | solution.py:21
  36.7 14.7 %collective-permute-start.3 = (bf16[256,1152]{1,0:T(8,128)(2,1)S(1)}, bf16[256,1152]{1,0:T(8,128)(2,1)S(1)}, u32[]{:S(2)}, u32[]{:S(2)}) collective-permute-start(bf16[256,1152]{1,0:T(8,128)(2,1)S(1)} %bitcast.21), channel_id=1, source_target_pairs={{0,16},{16,32},{32,48},{48,0},{1,17},{17,33},{33,49},{49,1},{2,18}... | collective-permute-start | bytes 1769480 | tf_op jit(solution)/shard_map/ppermute | solution.py:21
  38.0 13.6 %collective-permute-start.5 = (bf16[256,1152]{1,0:T(8,128)(2,1)S(1)}, bf16[256,1152]{1,0:T(8,128)(2,1)S(1)}, u32[]{:S(2)}, u32[]{:S(2)}) collective-permute-start(bf16[256,1152]{1,0:T(8,128)(2,1)S(1)} %bitcast.22), channel_id=1, source_target_pairs={{0,48},{16,0},{32,16},{48,32},{1,49},{17,1},{33,17},{49,33},{2,50}... | collective-permute-start | bytes 1769480 | tf_op jit(solution)/shard_map/ppermute | solution.py:21
  39.5 14.9 %collective-permute-start.7 = (bf16[256,1024]{1,0:T(8,128)(2,1)S(1)}, bf16[256,1024]{1,0:T(8,128)(2,1)S(1)}, u32[]{:S(2)}, u32[]{:S(2)}) collective-permute-start(bf16[256,1024]{1,0:T(8,128)(2,1)S(1)} %get-tuple-element.59.refs_6_.refs_7_), channel_id=1, source_target_pairs={{0,64},{64,128},{128,192},{192,0},{1,65},{65,129},{129,193},{193,1... | collective-permute-start | bytes 1572872 | tf_op jit(solution)/shard_map/ppermute | solution.py:21
  40.8 23.9 %collective-permute-start.8 = (bf16[256,1024]{1,0:T(8,128)(2,1)S(1)}, bf16[256,1024]{1,0:T(8,128)(2,1)S(1)}, u32[]{:S(2)}, u32[]{:S(2)}) collective-permute-start(bf16[256,1024]{1,0:T(8,128)(2,1)S(1)} %get-tuple-element.59.refs_6_.refs_7_), channel_id=1, source_target_pairs={{0,128},{64,192},{128,0},{192,64},{1,129},{65,193},{129,1},{193,65... | collective-permute-start | bytes 1572872 | tf_op jit(solution)/shard_map/ppermute | solution.py:21
  43.4 22.0 %collective-permute-start.9 = (bf16[256,1024]{1,0:T(8,128)(2,1)S(1)}, bf16[256,1024]{1,0:T(8,128)(2,1)S(1)}, u32[]{:S(2)}, u32[]{:S(2)}) collective-permute-start(bf16[256,1024]{1,0:T(8,128)(2,1)S(1)} %get-tuple-element.59.refs_6_.refs_7_), channel_id=1, source_target_pairs={{0,192},{64,0},{128,64},{192,128},{1,193},{65,1},{129,65},{193,129... | collective-permute-start | bytes 1572872 | tf_op jit(solution)/shard_map/ppermute | solution.py:21
  51.5 13.9 %collective-permute-start.4 = (bf16[128,1152]{1,0:T(8,128)(2,1)S(1)}, bf16[128,1152]{1,0:T(8,128)(2,1)S(1)}, u32[]{:S(2)}, u32[]{:S(2)}) collective-permute-start(bf16[128,1152]{1,0:T(8,128)(2,1)S(1)} %slice.12), channel_id=1, source_target_pairs={{0,16},{16,32},{32,48},{48,0},{1,17},{17,33},{33,49},{49,1},{2,18}... | collective-permute-start | bytes 884744 | tf_op jit(solution)/shard_map/ppermute | solution.py:21
  51.6 13.8 %collective-permute-start.6 = (bf16[128,1152]{1,0:T(8,128)(2,1)S(1)}, bf16[128,1152]{1,0:T(8,128)(2,1)S(1)}, u32[]{:S(2)}, u32[]{:S(2)}) collective-permute-start(bf16[128,1152]{1,0:T(8,128)(2,1)S(1)} %slice.13), channel_id=1, source_target_pairs={{0,48},{16,0},{32,16},{48,32},{1,49},{17,1},{33,17},{49,33},{2,50}... | collective-permute-start | bytes 884744 | tf_op jit(solution)/shard_map/ppermute | solution.py:21
  67.3 10.8 %collective-permute-start.10 = (f32[1024,512]{1,0:T(8,128)S(1)}, f32[1024,512]{1,0:T(8,128)S(1)}, u32[]{:S(2)}, u32[]{:S(2)}) collective-permute-start(f32[1024,512]{1,0:T(8,128)S(1)} %get-tuple-element.64), channel_id=1, source_target_pairs={{0,1},{1,0},{2,3},{3,2},{4,5},{5,4},{6,7},{7,6},{8,9},{9,8},{10,11... | collective-permute-start | bytes 6291464 | tf_op jit(solution)/shard_map/ppermute | solution.py:21
  70.3 7.7 %collective-permute-start.11 = (f32[8,256]{1,0:T(8,128)S(1)}, f32[8,256]{1,0:T(8,128)S(1)}, u32[]{:S(2)}, u32[]{:S(2)}) collective-permute-start(f32[8,256]{1,0:T(8,128)S(1)} %get-tuple-element.66.refs_5_), channel_id=1, source_target_pairs={{0,64},{64,128},{128,192},{192,0},{1,65},{65,129},{129,193},{193,1... | collective-permute-start | bytes 24584 | tf_op jit(solution)/shard_map/ppermute | solution.py:21
  71.3 6.8 %collective-permute-start.12 = (f32[8,256]{1,0:T(8,128)S(1)}, f32[8,256]{1,0:T(8,128)S(1)}, u32[]{:S(2)}, u32[]{:S(2)}) collective-permute-start(f32[8,256]{1,0:T(8,128)S(1)} %get-tuple-element.66.refs_5_), channel_id=1, source_target_pairs={{0,128},{64,192},{128,0},{192,64},{1,129},{65,193},{129,1},{193,65... | collective-permute-start | bytes 24584 | tf_op jit(solution)/shard_map/ppermute | solution.py:21
  73.4 4.7 %collective-permute-start.13 = (f32[8,256]{1,0:T(8,128)S(1)}, f32[8,256]{1,0:T(8,128)S(1)}, u32[]{:S(2)}, u32[]{:S(2)}) collective-permute-start(f32[8,256]{1,0:T(8,128)S(1)} %get-tuple-element.66.refs_5_), channel_id=1, source_target_pairs={{0,192},{64,0},{128,64},{192,128},{1,193},{65,1},{129,65},{193,129... | collective-permute-start | bytes 24584 | tf_op jit(solution)/shard_map/ppermute | solution.py:21
  93.1 4.6 %collective-permute-start.14 = (bf16[1024,512]{1,0:T(8,128)(2,1)S(1)}, bf16[1024,512]{1,0:T(8,128)(2,1)S(1)}, u32[]{:S(2)}, u32[]{:S(2)}) collective-permute-start(bf16[1024,512]{1,0:T(8,128)(2,1)S(1)} %get-tuple-element.69.grad_ref.refs_1_), channel_id=1, source_target_pairs={{0,1},{1,0},{2,3},{3,2},{4,5},{5,4},{6,7},{7,6},{8,9},{9,8},{10,11... | collective-permute-start | bytes 3145736 | tf_op jit(solution)/shard_map/ppermute | solution.py:21
  99.2 10.7 %collective-permute-start.15 = (bf16[128,1024]{1,0:T(8,128)(2,1)S(1)}, bf16[128,1024]{1,0:T(8,128)(2,1)S(1)}, u32[]{:S(2)}, u32[]{:S(2)}) collective-permute-start(bf16[128,1024]{1,0:T(8,128)(2,1)S(1)} %bitcast.30), channel_id=1, source_target_pairs={{0,16},{16,32},{32,48},{48,0},{1,17},{17,33},{33,49},{49,1},{2,18}... | collective-permute-start | bytes 786440 | tf_op jit(solution)/shard_map/ppermute | solution.py:21
  99.6 10.3 %collective-permute-start.16 = (bf16[128,1024]{1,0:T(8,128)(2,1)S(1)}, bf16[128,1024]{1,0:T(8,128)(2,1)S(1)}, u32[]{:S(2)}, u32[]{:S(2)}) collective-permute-start(bf16[128,1024]{1,0:T(8,128)(2,1)S(1)} %bitcast.29), channel_id=1, source_target_pairs={{0,48},{16,0},{32,16},{48,32},{1,49},{17,1},{33,17},{49,33},{2,50}... | collective-permute-start | bytes 786440 | tf_op jit(solution)/shard_map/ppermute | solution.py:21
  103.2 9.6 %collective-permute-start.19 = (bf16[128,1024]{1,0:T(8,128)(2,1)S(1)}, bf16[128,1024]{1,0:T(8,128)(2,1)S(1)}, u32[]{:S(2)}, u32[]{:S(2)}) collective-permute-start(bf16[128,1024]{1,0:T(8,128)(2,1)S(1)} %get-tuple-element.76), channel_id=1, source_target_pairs={{0,64},{64,128},{128,192},{192,0},{1,65},{65,129},{129,193},{193,1... | collective-permute-start | bytes 786440 | tf_op jit(solution)/shard_map/ppermute | solution.py:21
  103.3 9.5 %collective-permute-start.20 = (bf16[128,1024]{1,0:T(8,128)(2,1)S(1)}, bf16[128,1024]{1,0:T(8,128)(2,1)S(1)}, u32[]{:S(2)}, u32[]{:S(2)}) collective-permute-start(bf16[128,1024]{1,0:T(8,128)(2,1)S(1)} %get-tuple-element.87), channel_id=1, source_target_pairs={{0,192},{64,0},{128,64},{192,128},{1,193},{65,1},{129,65},{193,129... | collective-permute-start | bytes 786440 | tf_op jit(solution)/shard_map/ppermute | solution.py:21
  110.0 13.2 %collective-permute-start.17 = (bf16[256,1024]{1,0:T(8,128)(2,1)S(1)}, bf16[256,1024]{1,0:T(8,128)(2,1)S(1)}, u32[]{:S(2)}, u32[]{:S(2)}) collective-permute-start(bf16[256,1024]{1,0:T(8,128)(2,1)S(1)} %get-tuple-element.82), channel_id=1, source_target_pairs={{0,16},{16,32},{32,48},{48,0},{1,17},{17,33},{33,49},{49,1},{2,18}... | collective-permute-start | bytes 1572872 | tf_op jit(solution)/shard_map/ppermute | solution.py:21
  110.1 13.1 %collective-permute-start.18 = (bf16[256,1024]{1,0:T(8,128)(2,1)S(1)}, bf16[256,1024]{1,0:T(8,128)(2,1)S(1)}, u32[]{:S(2)}, u32[]{:S(2)}) collective-permute-start(bf16[256,1024]{1,0:T(8,128)(2,1)S(1)} %get-tuple-element.83), channel_id=1, source_target_pairs={{0,48},{16,0},{32,16},{48,32},{1,49},{17,1},{33,17},{49,33},{2,50}... | collective-permute-start | bytes 1572872 | tf_op jit(solution)/shard_map/ppermute | solution.py:21
  112.9 12.7 %collective-permute-start.21 = (bf16[256,1024]{1,0:T(8,128)(2,1)S(1)}, bf16[256,1024]{1,0:T(8,128)(2,1)S(1)}, u32[]{:S(2)}, u32[]{:S(2)}) collective-permute-start(bf16[256,1024]{1,0:T(8,128)(2,1)S(1)} %get-tuple-element.88), channel_id=1, source_target_pairs={{0,64},{64,128},{128,192},{192,0},{1,65},{65,129},{129,193},{193,1... | collective-permute-start | bytes 1572872 | tf_op jit(solution)/shard_map/ppermute | solution.py:21
  113.0 12.6 %collective-permute-start.22 = (bf16[256,1024]{1,0:T(8,128)(2,1)S(1)}, bf16[256,1024]{1,0:T(8,128)(2,1)S(1)}, u32[]{:S(2)}, u32[]{:S(2)}) collective-permute-start(bf16[256,1024]{1,0:T(8,128)(2,1)S(1)} %get-tuple-element.89), channel_id=1, source_target_pairs={{0,192},{64,0},{128,64},{192,128},{1,193},{65,1},{129,65},{193,129... | collective-permute-start | bytes 1572872 | tf_op jit(solution)/shard_map/ppermute | solution.py:21
  141.9 6.9 %collective-permute-start.24 = (bf16[256,1024]{1,0:T(8,128)(2,1)S(1)}, bf16[256,1024]{1,0:T(8,128)(2,1)S(1)}, u32[]{:S(2)}, u32[]{:S(2)}) collective-permute-start(bf16[256,1024]{1,0:T(8,128)(2,1)S(1)} %shard_map.102.pg_ref), channel_id=1, source_target_pairs={{0,1},{1,0},{2,3},{3,2},{4,5},{5,4},{6,7},{7,6},{8,9},{9,8},{10,11... | collective-permute-start | bytes 1572872 | tf_op jit(solution)/shard_map/ppermute | solution.py:21
  (5 other events, 69.9 us)

commit v6 on v5

--- a/solution.py
+++ b/solution.py
@@ -596,7 +596,7 @@
     own, got = qg_ref[n_q : n_q + 1, :128], qgo_ref[n_q : n_q + 1, :128]
     low, high = jnp.where(first, own, got), jnp.where(first, got, own)
     lane = lax.broadcasted_iota(jnp.int32, (1, 128), 1)
-    loss_out[...] = jnp.where(lane < part, low, pltpu.roll(high, part, 1))
+    loss_out[...] = jnp.where(lane < part, low, pltpu.roll(high, part, 1))[:, :n_q]
     for at in spans(pg_ref.shape[0], 64):
         to = slice(n_q + at.start, n_q + at.stop)
         here_ref[to], there_ref[to] = tangent(
@@ -615,7 +615,7 @@
     return call(
         finish_body,
         [meta, *rows_in, weight, weight_got],
-        [struct((n - n_p, out_width), bf16), struct((n_p, out_width), bf16), struct((1, 128))],
+        [struct((n - n_p, out_width), bf16), struct((n_p, out_width), bf16), struct((1, n - n_p))],
         [
             pltpu.VMEM((n, width), bf16),
             pltpu.VMEM((n, width), bf16),
@@ -671,7 +671,7 @@
     grad_got = shifted(grad, "mp", 1)
     q_part = query_part(meta, grad, p_all)
     grad_got = after(grad_got, q_part)
-    far, near = ((2, 3), (0, 1, 4)) if len(q_shapes) > 2 else ((1,), (0,))
+    far, near = ((2, 3), (1, 4)) if len(q_shapes) > 2 else ((1,), ())
     q_parts, p_parts = [None] * len(q_shapes), [None] * len(p_shapes)
 
     def fill(parts, chosen, values):
@@ -684,14 +684,19 @@
     fill(p_parts, far, passage_part(meta, grad, grad_next, q_own, q_other, p_shapes, far))
     p_far = return_far(p_parts, "y")
     grad_last = after(grad_got, p_parts[far[0]])
-    fill(q_parts, near, query_rest(meta, grad_last, p_all, q_part, q_shapes, near))
-    fill(p_parts, near, passage_part(meta, grad, grad_last, q_own, q_other, p_shapes, near))
+    if near:
+        fill(q_parts, near, query_rest(meta, grad_last, p_all, q_part, q_shapes, near))
+    if near:
+        fill(p_parts, near, passage_part(meta, grad, grad_last, q_own, q_other, p_shapes, near))
     q_leaving = join(q_parts, q_far)
     p_leaving = join(p_parts, [after(p_far[0], *q_leaving)] + p_far[1:])
     p_coming = near_coming(p_leaving, "y")
+    grad_own = after(grad_got, *p_leaving)
+    fill(q_parts, (0,), query_rest(meta, grad_own, p_all, q_part, q_shapes, (0,)))
+    fill(p_parts, (0,), passage_part(meta, grad, grad_own, q_own, q_other, p_shapes, (0,)))
     q_part = return_near(q_parts, q_leaving, "x")
     weight, weight_got = head_rows(after(meta, *q_leaving), head_weight, weight_got)
-    q_part = after(q_part, *p_coming, weight, weight_got)
+    q_part = after(q_part, p_parts[0], *p_coming, weight, weight_got)
     back = exchanged(q_part.reshape(n_z, q_rows, width), "z")
     p_grad = total([after(p_parts[0], back)] + p_coming, bf16)
     p_grad_got = shifted(p_grad, "mp", 1)
@@ -700,7 +705,7 @@
     query_grads, passage_grads, losses = finish(
         meta, (q_grad, q_grad_got, p_grad, p_grad_got, unit, unit_got, inv), weight, weight_got
     )
-    return losses[0, :q_rows], query_grads, passage_grads
+    return losses.reshape(q_rows), query_grads, passage_grads
 
 
 def solution(mesh):

time: 154 us -> 153 us (level)
  waiting for transfers between devices: 25.8 us -> 23.4 us
  Pallas kernels: 33.1 us -> 34.9 us
    ppermute x25, waiting for transfers between devices: 25.8 us -> 23.4 us  [shifted(): return lax.ppermute(value, axis, [(i, (i + shift) % n) for i in range(n)])]
    pallas_call x19 -> x21, Pallas kernels: 33.1 us -> 34.9 us  [call(): pl.pallas_call(body, in_specs=specs, out_specs=[pl.BlockSpec(memory_space...]
  transfers between devices with their start and end apart: 25 -> 25, of which waited for: 8 -> 8; matrix products, arithmetic and copies ran while one was open for 0% -> 0% of each run, Pallas kernels for 11% -> 12%
where the time goes in v6:
time: 153 us
  blocking collectives  53.3 us (35%)
  starting transfers between devices  39.4 us (26%)
  Pallas kernels  34.9 us (23%)
  waiting for transfers between devices  23.4 us (15%)
    all_to_all x3, blocking collectives, exchanged(): return lax.all_to_all(parts, axis, split_axis=0, concat_axis=0, tiled=True)  53.3 us
    ppermute x25, starting transfers between devices, shifted(): return lax.ppermute(value, axis, [(i, (i + shift) % n) for i in range(n)])  39.4 us
    pallas_call x21, Pallas kernels, call(): pl.pallas_call(body, in_specs=specs, out_specs=[pl.BlockSpec(memory_space...  34.9 us
    ppermute x25, waiting for transfers between devices, shifted(): return lax.ppermute(value, axis, [(i, (i + shift) % n) for i in range(n)])  23.4 us
  transfers between devices with their start and end apart: 25, of which 8 were waited for; matrix products, arithmetic and copies ran while one was open for 0% of the time, Pallas kernels for 12%

profile of v6, /device:TPU:1, one launch (start us, length us, event | category | flops | bytes accessed | tf_op | source)
XLA Modules:
  0.0 152.7 jit_solution(18331653375504760067)
XLA Ops:
  0.7 5.6 %shard_map.85 = (f32[32,1024]{1,0:T(8,128)S(1)}, f32[256,1024]{1,0:T(8,128)S(1)}, f32[1,384]{1,0:T(1,128)S(1)}) custom-call(s32[5]{0:T(128)S(1)} %stack.23.meta.refs_0_, bf16[32,4096]{1,0:T(8,128)(2,1)} %q_ref.1, bf16[256,4096]{1,0:T(8,128)(2,1)} %p_ref.1, bf16[4096,1024]{1,0:T(8,128)(2,1)} %w_ref.3), custom_call_target="tpu_custom_call" | custom-call | flops 2415919104 | tf_op jit(solution)/shard_map/pallas_call | solution.py:92
  6.4 3.3 %collective-permute-start = (f32[1,384]{1,0:T(1,128)S(1)}, f32[1,384]{1,0:T(1,128)S(1)}, u32[]{:S(2)}, u32[]{:S(2)}) collective-permute-start(f32[1,384]{1,0:T(1,128)S(1)} %get-tuple-element.53.own_ref), channel_id=1, source_target_pairs={{0,1},{1,0},{2,3},{3,2},{4,5},{5,4},{6,7},{7,6},{8,9},{9,8},{10,11... | collective-permute-start | bytes 4616 | tf_op jit(solution)/shard_map/ppermute | solution.py:21
  12.0 24.7 %all_to_all.15 = bf16[8,32,1152]{2,1,0:T(8,128)(2,1)S(1)} all-to-all(bf16[8,32,1152]{2,1,0:T(8,128)(2,1)S(1)} %get-tuple-element.54), channel_id=1, replica_groups=mesh['y'=4,'x'=4,'z'=8,'mp'=2] {'z'}, dimensions={0} | all-to-all | bytes 1179648 | tf_op jit(solution)/shard_map/all_to_all | solution.py:25
  40.8 2.6 %collective-permute-start.8 = (bf16[256,1024]{1,0:T(8,128)(2,1)S(1)}, bf16[256,1024]{1,0:T(8,128)(2,1)S(1)}, u32[]{:S(2)}, u32[]{:S(2)}) collective-permute-start(bf16[256,1024]{1,0:T(8,128)(2,1)S(1)} %get-tuple-element.58.refs_6_.refs_7_), channel_id=1, source_target_pairs={{0,128},{64,192},{128,0},{192,64},{1,129},{65,193},{129,1},{193,65... | collective-permute-start | bytes 1572872 | tf_op jit(solution)/shard_map/ppermute | solution.py:21
  44.5 7.0 %collective-permute-done.3.refs_2_.refs_3_ = bf16[256,1152]{1,0:T(8,128)(2,1)S(1)} collective-permute-done((bf16[256,1152]{1,0:T(8,128)(2,1)S(1)}, bf16[256,1152]{1,0:T(8,128)(2,1)S(1)}, u32[]{:S(2)}, u32[]{:S(2)}) %collective-permute-start.3) | collective-permute-done | bytes 589856 | tf_op jit(solution)/shard_map/ppermute | solution.py:21
  51.6 2.7 %collective-permute-start.6 = (bf16[128,1152]{1,0:T(8,128)(2,1)S(1)}, bf16[128,1152]{1,0:T(8,128)(2,1)S(1)}, u32[]{:S(2)}, u32[]{:S(2)}) collective-permute-start(bf16[128,1152]{1,0:T(8,128)(2,1)S(1)} %slice.9), channel_id=1, source_target_pairs={{0,48},{16,0},{32,16},{48,32},{1,49},{17,1},{33,17},{49,33},{2,50}... | collective-permute-start | bytes 884744 | tf_op jit(solution)/shard_map/ppermute | solution.py:21
  54.3 10.3 %collective-permute-done.8.refs_8_.refs_9_ = bf16[256,1024]{1,0:T(8,128)(2,1)S(1)} collective-permute-done((bf16[256,1024]{1,0:T(8,128)(2,1)S(1)}, bf16[256,1024]{1,0:T(8,128)(2,1)S(1)}, u32[]{:S(2)}, u32[]{:S(2)}) %collective-permute-start.8) | collective-permute-done | bytes 524320 | tf_op jit(solution)/shard_map/ppermute | solution.py:21
  65.4 1.9 %shard_map.87 = (f32[1024,512]{1,0:T(8,128)S(1)}, bf16[512,1024]{1,0:T(8,128)(2,1)S(1)}, f32[512,128]{1,0:T(8,128)S(1)}, f32[512,128]{1,0:T(8,128)S(1)}) custom-call(s32[5]{0:T(128)S(1)} %stack.23.meta.refs_0_, bf16[256,1152]{1,0:T(8,128)(2,1)S(1)} %bitcast.22, bf16[256,1152]{1,0:T(8,128)(2,1)S(1)} %collective-permute-done.3.refs_2_.refs_3_, ...), custom_call_target="tpu_custom_call" | custom-call | flops 1073741824 | tf_op jit(solution)/shard_map/pallas_call | solution.py:92
  67.3 2.2 %collective-permute-start.10 = (f32[1024,512]{1,0:T(8,128)S(1)}, f32[1024,512]{1,0:T(8,128)S(1)}, u32[]{:S(2)}, u32[]{:S(2)}) collective-permute-start(f32[1024,512]{1,0:T(8,128)S(1)} %get-tuple-element.63), channel_id=1, source_target_pairs={{0,1},{1,0},{2,3},{3,2},{4,5},{5,4},{6,7},{7,6},{8,9},{9,8},{10,11... | collective-permute-start | bytes 6291464 | tf_op jit(solution)/shard_map/ppermute | solution.py:21
  71.3 2.1 %collective-permute-start.12 = (f32[8,256]{1,0:T(8,128)S(1)}, f32[8,256]{1,0:T(8,128)S(1)}, u32[]{:S(2)}, u32[]{:S(2)}) collective-permute-start(f32[8,256]{1,0:T(8,128)S(1)} %get-tuple-element.65.refs_5_), channel_id=1, source_target_pairs={{0,128},{64,192},{128,0},{192,64},{1,129},{65,193},{129,1},{193,65... | collective-permute-start | bytes 24584 | tf_op jit(solution)/shard_map/ppermute | solution.py:21
  74.8 3.3 %shard_map.89 = (f32[1024,512]{1,0:T(8,128)S(1)}, f32[1024,512]{1,0:T(8,128)S(1)}, bf16[512,1024]{1,0:T(8,128)(2,1)S(1)}, bf16[1024,1024]{1,0:T(8,128)(2,1)S(1)}) custom-call(s32[5]{0:T(128)S(1)} %stack.23.meta.refs_0_, f32[128,512]{1,0:T(8,128)S(1)} %get-tuple-element.61.refs_1_.refs_4_.refs_3_, bf16[256,1152]{1,0:T(8,128)(2,1)S(1)} %bitcast.23, ...), custom_call_target="tpu_custom_call" | custom-call | flops 2147483648 | tf_op jit(solution)/shard_map/pallas_call | solution.py:92
  79.7 12.5 %all_to_all.16.refs_2_ = f32[32,2,512]{2,1,0:T(2,128)S(1)} all-to-all(f32[32,2,512]{2,1,0:T(2,128)S(1)} %broadcast_in_dim.22), channel_id=1, replica_groups=mesh['y'=4,'x'=4,'z'=8,'mp'=2] {'x','z'}, dimensions={0} | all-to-all | bytes 262144 | tf_op jit(solution)/shard_map/all_to_all | solution.py:25
  93.2 2.3 %collective-permute-start.14 = (bf16[1024,512]{1,0:T(8,128)(2,1)S(1)}, bf16[1024,512]{1,0:T(8,128)(2,1)S(1)}, u32[]{:S(2)}, u32[]{:S(2)}) collective-permute-start(bf16[1024,512]{1,0:T(8,128)(2,1)S(1)} %get-tuple-element.68.grad_ref.refs_1_), channel_id=1, source_target_pairs={{0,1},{1,0},{2,3},{3,2},{4,5},{5,4},{6,7},{7,6},{8,9},{9,8},{10,11... | collective-permute-start | bytes 3145736 | tf_op jit(solution)/shard_map/ppermute | solution.py:21
  95.5 1.8 %shard_map.92.refs_3_ = bf16[512,1024]{1,0:T(8,128)(2,1)S(1)} custom-call(s32[5]{0:T(128)S(1)} %stack.23.meta.refs_0_, bf16[1024,512]{1,0:T(8,128)(2,1)S(1)} %get-tuple-element.68.grad_ref.refs_1_, bf16[1024,1024]{1,0:T(8,128)(2,1)S(1)} %get-tuple-element.69.p_ref.refs_2_), custom_call_target="tpu_custom_call" | custom-call | flops 1073741824 | tf_op jit(solution)/shard_map/pallas_call | solution.py:92
  99.7 2.3 %collective-permute-start.17 = (bf16[128,1024]{1,0:T(8,128)(2,1)S(1)}, bf16[128,1024]{1,0:T(8,128)(2,1)S(1)}, u32[]{:S(2)}, u32[]{:S(2)}) collective-permute-start(bf16[128,1024]{1,0:T(8,128)(2,1)S(1)} %bitcast.28), channel_id=1, source_target_pairs={{0,48},{16,0},{32,16},{48,32},{1,49},{17,1},{33,17},{49,33},{2,50}... | collective-permute-start | bytes 786440 | tf_op jit(solution)/shard_map/ppermute | solution.py:21
  103.4 2.6 %collective-permute-start.18 = (bf16[128,1024]{1,0:T(8,128)(2,1)S(1)}, bf16[128,1024]{1,0:T(8,128)(2,1)S(1)}, u32[]{:S(2)}, u32[]{:S(2)}) collective-permute-start(bf16[128,1024]{1,0:T(8,128)(2,1)S(1)} %get-tuple-element.85), channel_id=1, source_target_pairs={{0,192},{64,0},{128,64},{192,128},{1,193},{65,1},{129,65},{193,129... | collective-permute-start | bytes 786440 | tf_op jit(solution)/shard_map/ppermute | solution.py:21
  107.4 1.8 %shard_map.95 = (bf16[256,1024]{1,0:T(8,128)(2,1)S(1)}, bf16[256,1024]{1,0:T(8,128)(2,1)S(1)}) custom-call(s32[5]{0:T(128)S(1)} %stack.23.meta.refs_0_, bf16[1024,512]{1,0:T(8,128)(2,1)S(1)} %get-tuple-element.68.grad_ref.refs_1_, bf16[1024,512]{1,0:T(8,128)(2,1)S(1)} %collective-permute-done.14.refs_1_.refs_2_, ...), custom_call_target="tpu_custom_call" | custom-call | flops 1073741824 | tf_op jit(solution)/shard_map/pallas_call | solution.py:92
  109.5 2.7 %collective-permute-start.20 = (bf16[256,1024]{1,0:T(8,128)(2,1)S(1)}, bf16[256,1024]{1,0:T(8,128)(2,1)S(1)}, u32[]{:S(2)}, u32[]{:S(2)}) collective-permute-start(bf16[256,1024]{1,0:T(8,128)(2,1)S(1)} %get-tuple-element.82), channel_id=1, source_target_pairs={{0,48},{16,0},{32,16},{48,32},{1,49},{17,1},{33,17},{49,33},{2,50}... | collective-permute-start | bytes 1572872 | tf_op jit(solution)/shard_map/ppermute | solution.py:21
  112.4 2.7 %collective-permute-start.22 = (bf16[256,1024]{1,0:T(8,128)(2,1)S(1)}, bf16[256,1024]{1,0:T(8,128)(2,1)S(1)}, u32[]{:S(2)}, u32[]{:S(2)}) collective-permute-start(bf16[256,1024]{1,0:T(8,128)(2,1)S(1)} %get-tuple-element.87), channel_id=1, source_target_pairs={{0,192},{64,0},{128,64},{192,128},{1,193},{65,1},{129,65},{193,129... | collective-permute-start | bytes 1572872 | tf_op jit(solution)/shard_map/ppermute | solution.py:21
  115.1 4.0 %shard_map.102 = (bf16[2048,1024]{1,0:T(8,128)(2,1)S(1)}, bf16[2048,1024]{1,0:T(8,128)(2,1)S(1)}) custom-call(s32[5]{0:T(128)S(1)} %stack.23.meta.refs_0_, bf16[4096,1024]{1,0:T(8,128)(2,1)} %w_ref.3, bf16[4096,1024]{1,0:T(8,128)(2,1)} %copy-done), custom_call_target="tpu_custom_call" | custom-call | tf_op jit(solution)/shard_map/pallas_call | solution.py:92
  122.8 2.2 %collective-permute-done.21.refs_1_ = bf16[256,1024]{1,0:T(8,128)(2,1)S(1)} collective-permute-done((bf16[256,1024]{1,0:T(8,128)(2,1)S(1)}, bf16[256,1024]{1,0:T(8,128)(2,1)S(1)}, u32[]{:S(2)}, u32[]{:S(2)}) %collective-permute-start.21) | collective-permute-done | bytes 524320 | tf_op jit(solution)/shard_map/ppermute | solution.py:21
  125.0 16.1 %all_to_all.17.refs_1_ = bf16[8,32,1024]{2,1,0:T(8,128)(2,1)S(1)} all-to-all(bf16[8,32,1024]{2,1,0:T(8,128)(2,1)S(1)} %bitcast.25), channel_id=1, replica_groups=mesh['y'=4,'x'=4,'z'=8,'mp'=2] {'z'}, dimensions={0} | all-to-all | bytes 1048576 | tf_op jit(solution)/shard_map/all_to_all | solution.py:25
  141.2 4.8 %collective-permute-start.24 = (bf16[256,1024]{1,0:T(8,128)(2,1)S(1)}, bf16[256,1024]{1,0:T(8,128)(2,1)S(1)}, u32[]{:S(2)}, u32[]{:S(2)}) collective-permute-start(bf16[256,1024]{1,0:T(8,128)(2,1)S(1)} %shard_map.104.pg_ref), channel_id=1, source_target_pairs={{0,1},{1,0},{2,3},{3,2},{4,5},{5,4},{6,7},{7,6},{8,9},{9,8},{10,11... | collective-permute-start | bytes 1572872 | tf_op jit(solution)/shard_map/ppermute | solution.py:21
  148.2 4.5 %shard_map.105 = (bf16[32,2048]{1,0:T(8,128)(2,1)}, bf16[256,2048]{1,0:T(8,128)(2,1)}, f32[1,32]{1,0:T(1,128)}) custom-call(s32[5]{0:T(128)S(1)} %stack.23.meta.refs_0_, f32[40,1024]{1,0:T(8,128)S(1)} %shard_map.103.qg_ref, f32[40,1024]{1,0:T(8,128)S(1)} %collective-permute-done.23.qgo_ref, bf16[256,1024]{1,0:T(8,128)(2,1)S(1)} %shard_map.104.pg_ref, ...), custom_call_target="tpu_custom_call" | custom-call | flops 2415919104 | tf_op jit(solution)/shard_map/pallas_call | solution.py:92
  (73 shorter events, 25.5 us)
Async XLA Ops:
  6.4 4.1 %collective-permute-start = (f32[1,384]{1,0:T(1,128)S(1)}, f32[1,384]{1,0:T(1,128)S(1)}, u32[]{:S(2)}, u32[]{:S(2)}) collective-permute-start(f32[1,384]{1,0:T(1,128)S(1)} %get-tuple-element.53.own_ref), channel_id=1, source_target_pairs={{0,1},{1,0},{2,3},{3,2},{4,5},{5,4},{6,7},{7,6},{8,9},{9,8},{10,11... | collective-permute-start | bytes 4616 | tf_op jit(solution)/shard_map/ppermute | solution.py:21
  11.4 25.3 %collective-permute-start.2 = (bf16[4096,1024]{1,0:T(8,128)(2,1)}, bf16[4096,1024]{1,0:T(8,128)(2,1)S(1)}, u32[]{:S(2)}, u32[]{:S(2)}) collective-permute-start(bf16[4096,1024]{1,0:T(8,128)(2,1)} %w_ref.3), channel_id=1, source_target_pairs={{0,1},{1,0},{2,3},{3,2},{4,5},{5,4},{6,7},{7,6},{8,9},{9,8},{10,11... | collective-permute-start | bytes 25165832 | tf_op jit(solution)/shard_map/ppermute | solution.py:21
  11.8 24.9 %collective-permute-start.1 = (f32[288,1024]{1,0:T(8,128)S(1)}, f32[288,1024]{1,0:T(8,128)S(1)}, u32[]{:S(2)}, u32[]{:S(2)}) collective-permute-start(f32[288,1024]{1,0:T(8,128)S(1)} %get-tuple-element.55.unit_ref), channel_id=1, source_target_pairs={{0,1},{1,0},{2,3},{3,2},{4,5},{5,4},{6,7},{7,6},{8,9},{9,8},{10,11... | collective-permute-start | bytes 3538952 | tf_op jit(solution)/shard_map/ppermute | solution.py:21
  36.7 14.7 %collective-permute-start.3 = (bf16[256,1152]{1,0:T(8,128)(2,1)S(1)}, bf16[256,1152]{1,0:T(8,128)(2,1)S(1)}, u32[]{:S(2)}, u32[]{:S(2)}) collective-permute-start(bf16[256,1152]{1,0:T(8,128)(2,1)S(1)} %bitcast.20), channel_id=1, source_target_pairs={{0,16},{16,32},{32,48},{48,0},{1,17},{17,33},{33,49},{49,1},{2,18}... | collective-permute-start | bytes 1769480 | tf_op jit(solution)/shard_map/ppermute | solution.py:21
  38.0 13.6 %collective-permute-start.5 = (bf16[256,1152]{1,0:T(8,128)(2,1)S(1)}, bf16[256,1152]{1,0:T(8,128)(2,1)S(1)}, u32[]{:S(2)}, u32[]{:S(2)}) collective-permute-start(bf16[256,1152]{1,0:T(8,128)(2,1)S(1)} %bitcast.21), channel_id=1, source_target_pairs={{0,48},{16,0},{32,16},{48,32},{1,49},{17,1},{33,17},{49,33},{2,50}... | collective-permute-start | bytes 1769480 | tf_op jit(solution)/shard_map/ppermute | solution.py:21
  39.5 14.9 %collective-permute-start.7 = (bf16[256,1024]{1,0:T(8,128)(2,1)S(1)}, bf16[256,1024]{1,0:T(8,128)(2,1)S(1)}, u32[]{:S(2)}, u32[]{:S(2)}) collective-permute-start(bf16[256,1024]{1,0:T(8,128)(2,1)S(1)} %get-tuple-element.58.refs_6_.refs_7_), channel_id=1, source_target_pairs={{0,64},{64,128},{128,192},{192,0},{1,65},{65,129},{129,193},{193,1... | collective-permute-start | bytes 1572872 | tf_op jit(solution)/shard_map/ppermute | solution.py:21
  40.8 23.9 %collective-permute-start.8 = (bf16[256,1024]{1,0:T(8,128)(2,1)S(1)}, bf16[256,1024]{1,0:T(8,128)(2,1)S(1)}, u32[]{:S(2)}, u32[]{:S(2)}) collective-permute-start(bf16[256,1024]{1,0:T(8,128)(2,1)S(1)} %get-tuple-element.58.refs_6_.refs_7_), channel_id=1, source_target_pairs={{0,128},{64,192},{128,0},{192,64},{1,129},{65,193},{129,1},{193,65... | collective-permute-start | bytes 1572872 | tf_op jit(solution)/shard_map/ppermute | solution.py:21
  43.4 22.0 %collective-permute-start.9 = (bf16[256,1024]{1,0:T(8,128)(2,1)S(1)}, bf16[256,1024]{1,0:T(8,128)(2,1)S(1)}, u32[]{:S(2)}, u32[]{:S(2)}) collective-permute-start(bf16[256,1024]{1,0:T(8,128)(2,1)S(1)} %get-tuple-element.58.refs_6_.refs_7_), channel_id=1, source_target_pairs={{0,192},{64,0},{128,64},{192,128},{1,193},{65,1},{129,65},{193,129... | collective-permute-start | bytes 1572872 | tf_op jit(solution)/shard_map/ppermute | solution.py:21
  51.5 13.9 %collective-permute-start.4 = (bf16[128,1152]{1,0:T(8,128)(2,1)S(1)}, bf16[128,1152]{1,0:T(8,128)(2,1)S(1)}, u32[]{:S(2)}, u32[]{:S(2)}) collective-permute-start(bf16[128,1152]{1,0:T(8,128)(2,1)S(1)} %slice.8), channel_id=1, source_target_pairs={{0,16},{16,32},{32,48},{48,0},{1,17},{17,33},{33,49},{49,1},{2,18}... | collective-permute-start | bytes 884744 | tf_op jit(solution)/shard_map/ppermute | solution.py:21
  51.6 13.8 %collective-permute-start.6 = (bf16[128,1152]{1,0:T(8,128)(2,1)S(1)}, bf16[128,1152]{1,0:T(8,128)(2,1)S(1)}, u32[]{:S(2)}, u32[]{:S(2)}) collective-permute-start(bf16[128,1152]{1,0:T(8,128)(2,1)S(1)} %slice.9), channel_id=1, source_target_pairs={{0,48},{16,0},{32,16},{48,32},{1,49},{17,1},{33,17},{49,33},{2,50}... | collective-permute-start | bytes 884744 | tf_op jit(solution)/shard_map/ppermute | solution.py:21
  67.3 10.8 %collective-permute-start.10 = (f32[1024,512]{1,0:T(8,128)S(1)}, f32[1024,512]{1,0:T(8,128)S(1)}, u32[]{:S(2)}, u32[]{:S(2)}) collective-permute-start(f32[1024,512]{1,0:T(8,128)S(1)} %get-tuple-element.63), channel_id=1, source_target_pairs={{0,1},{1,0},{2,3},{3,2},{4,5},{5,4},{6,7},{7,6},{8,9},{9,8},{10,11... | collective-permute-start | bytes 6291464 | tf_op jit(solution)/shard_map/ppermute | solution.py:21
  70.3 7.8 %collective-permute-start.11 = (f32[8,256]{1,0:T(8,128)S(1)}, f32[8,256]{1,0:T(8,128)S(1)}, u32[]{:S(2)}, u32[]{:S(2)}) collective-permute-start(f32[8,256]{1,0:T(8,128)S(1)} %get-tuple-element.65.refs_5_), channel_id=1, source_target_pairs={{0,64},{64,128},{128,192},{192,0},{1,65},{65,129},{129,193},{193,1... | collective-permute-start | bytes 24584 | tf_op jit(solution)/shard_map/ppermute | solution.py:21
  71.3 6.8 %collective-permute-start.12 = (f32[8,256]{1,0:T(8,128)S(1)}, f32[8,256]{1,0:T(8,128)S(1)}, u32[]{:S(2)}, u32[]{:S(2)}) collective-permute-start(f32[8,256]{1,0:T(8,128)S(1)} %get-tuple-element.65.refs_5_), channel_id=1, source_target_pairs={{0,128},{64,192},{128,0},{192,64},{1,129},{65,193},{129,1},{193,65... | collective-permute-start | bytes 24584 | tf_op jit(solution)/shard_map/ppermute | solution.py:21
  73.4 4.8 %collective-permute-start.13 = (f32[8,256]{1,0:T(8,128)S(1)}, f32[8,256]{1,0:T(8,128)S(1)}, u32[]{:S(2)}, u32[]{:S(2)}) collective-permute-start(f32[8,256]{1,0:T(8,128)S(1)} %get-tuple-element.65.refs_5_), channel_id=1, source_target_pairs={{0,192},{64,0},{128,64},{192,128},{1,193},{65,1},{129,65},{193,129... | collective-permute-start | bytes 24584 | tf_op jit(solution)/shard_map/ppermute | solution.py:21
  93.2 4.6 %collective-permute-start.14 = (bf16[1024,512]{1,0:T(8,128)(2,1)S(1)}, bf16[1024,512]{1,0:T(8,128)(2,1)S(1)}, u32[]{:S(2)}, u32[]{:S(2)}) collective-permute-start(bf16[1024,512]{1,0:T(8,128)(2,1)S(1)} %get-tuple-element.68.grad_ref.refs_1_), channel_id=1, source_target_pairs={{0,1},{1,0},{2,3},{3,2},{4,5},{5,4},{6,7},{7,6},{8,9},{9,8},{10,11... | collective-permute-start | bytes 3145736 | tf_op jit(solution)/shard_map/ppermute | solution.py:21
  99.2 10.0 %collective-permute-start.16 = (bf16[128,1024]{1,0:T(8,128)(2,1)S(1)}, bf16[128,1024]{1,0:T(8,128)(2,1)S(1)}, u32[]{:S(2)}, u32[]{:S(2)}) collective-permute-start(bf16[128,1024]{1,0:T(8,128)(2,1)S(1)} %bitcast.29), channel_id=1, source_target_pairs={{0,16},{16,32},{32,48},{48,0},{1,17},{17,33},{33,49},{49,1},{2,18}... | collective-permute-start | bytes 786440 | tf_op jit(solution)/shard_map/ppermute | solution.py:21
  99.7 9.6 %collective-permute-start.17 = (bf16[128,1024]{1,0:T(8,128)(2,1)S(1)}, bf16[128,1024]{1,0:T(8,128)(2,1)S(1)}, u32[]{:S(2)}, u32[]{:S(2)}) collective-permute-start(bf16[128,1024]{1,0:T(8,128)(2,1)S(1)} %bitcast.28), channel_id=1, source_target_pairs={{0,48},{16,0},{32,16},{48,32},{1,49},{17,1},{33,17},{49,33},{2,50}... | collective-permute-start | bytes 786440 | tf_op jit(solution)/shard_map/ppermute | solution.py:21
  103.3 8.9 %collective-permute-start.15 = (bf16[128,1024]{1,0:T(8,128)(2,1)S(1)}, bf16[128,1024]{1,0:T(8,128)(2,1)S(1)}, u32[]{:S(2)}, u32[]{:S(2)}) collective-permute-start(bf16[128,1024]{1,0:T(8,128)(2,1)S(1)} %get-tuple-element.75), channel_id=1, source_target_pairs={{0,64},{64,128},{128,192},{192,0},{1,65},{65,129},{129,193},{193,1... | collective-permute-start | bytes 786440 | tf_op jit(solution)/shard_map/ppermute | solution.py:21
  103.4 8.7 %collective-permute-start.18 = (bf16[128,1024]{1,0:T(8,128)(2,1)S(1)}, bf16[128,1024]{1,0:T(8,128)(2,1)S(1)}, u32[]{:S(2)}, u32[]{:S(2)}) collective-permute-start(bf16[128,1024]{1,0:T(8,128)(2,1)S(1)} %get-tuple-element.85), channel_id=1, source_target_pairs={{0,192},{64,0},{128,64},{192,128},{1,193},{65,1},{129,65},{193,129... | collective-permute-start | bytes 786440 | tf_op jit(solution)/shard_map/ppermute | solution.py:21
  109.4 13.2 %collective-permute-start.19 = (bf16[256,1024]{1,0:T(8,128)(2,1)S(1)}, bf16[256,1024]{1,0:T(8,128)(2,1)S(1)}, u32[]{:S(2)}, u32[]{:S(2)}) collective-permute-start(bf16[256,1024]{1,0:T(8,128)(2,1)S(1)} %get-tuple-element.81), channel_id=1, source_target_pairs={{0,16},{16,32},{32,48},{48,0},{1,17},{17,33},{33,49},{49,1},{2,18}... | collective-permute-start | bytes 1572872 | tf_op jit(solution)/shard_map/ppermute | solution.py:21
  109.5 13.1 %collective-permute-start.20 = (bf16[256,1024]{1,0:T(8,128)(2,1)S(1)}, bf16[256,1024]{1,0:T(8,128)(2,1)S(1)}, u32[]{:S(2)}, u32[]{:S(2)}) collective-permute-start(bf16[256,1024]{1,0:T(8,128)(2,1)S(1)} %get-tuple-element.82), channel_id=1, source_target_pairs={{0,48},{16,0},{32,16},{48,32},{1,49},{17,1},{33,17},{49,33},{2,50}... | collective-permute-start | bytes 1572872 | tf_op jit(solution)/shard_map/ppermute | solution.py:21
  112.3 12.6 %collective-permute-start.21 = (bf16[256,1024]{1,0:T(8,128)(2,1)S(1)}, bf16[256,1024]{1,0:T(8,128)(2,1)S(1)}, u32[]{:S(2)}, u32[]{:S(2)}) collective-permute-start(bf16[256,1024]{1,0:T(8,128)(2,1)S(1)} %get-tuple-element.86), channel_id=1, source_target_pairs={{0,64},{64,128},{128,192},{192,0},{1,65},{65,129},{129,193},{193,1... | collective-permute-start | bytes 1572872 | tf_op jit(solution)/shard_map/ppermute | solution.py:21
  112.4 12.6 %collective-permute-start.22 = (bf16[256,1024]{1,0:T(8,128)(2,1)S(1)}, bf16[256,1024]{1,0:T(8,128)(2,1)S(1)}, u32[]{:S(2)}, u32[]{:S(2)}) collective-permute-start(bf16[256,1024]{1,0:T(8,128)(2,1)S(1)} %get-tuple-element.87), channel_id=1, source_target_pairs={{0,192},{64,0},{128,64},{192,128},{1,193},{65,1},{129,65},{193,129... | collective-permute-start | bytes 1572872 | tf_op jit(solution)/shard_map/ppermute | solution.py:21
  141.2 7.0 %collective-permute-start.24 = (bf16[256,1024]{1,0:T(8,128)(2,1)S(1)}, bf16[256,1024]{1,0:T(8,128)(2,1)S(1)}, u32[]{:S(2)}, u32[]{:S(2)}) collective-permute-start(bf16[256,1024]{1,0:T(8,128)(2,1)S(1)} %shard_map.104.pg_ref), channel_id=1, source_target_pairs={{0,1},{1,0},{2,3},{3,2},{4,5},{5,4},{6,7},{7,6},{8,9},{9,8},{10,11... | collective-permute-start | bytes 1572872 | tf_op jit(solution)/shard_map/ppermute | solution.py:21
  (5 other events, 70.0 us)

commit v7 on v6

--- a/solution.py
+++ b/solution.py
@@ -651,11 +651,12 @@
     )
     unit_got = shifted(unit, "mp", 1)
     weight_got = shifted(after(head_weight, unit), "mp", 1)
-    p_pieces = [p_embed] + [shifted(p_embed, "y", s) for s in range(1, n_y)]
+    p_near = ring_near(p_embed, "y")
     q_z = exchanged(message, "z").reshape(n_z * q_rows, width + AUX)
     q_z = after(q_z, unit_got, weight_got)
     q_near = ring_near(q_z, "x")
     q_pieces = ring_far(q_z, q_near, "x")
+    p_pieces = ring_far(p_embed, [after(piece, *q_near) for piece in p_near], "y")
     q_shapes = [piece.shape[0] for piece in q_pieces]
     p_shapes = [p_rows, p_rows, p_rows // 2, p_rows // 2, p_rows] if n_y == 4 else [p_rows, p_rows]
     sent, q_other, aux, aux_other = score_sent(meta, q_pieces, p_pieces)

time: 153 us -> 151 us (0.987)
  waiting for transfers between devices: 23.4 us -> 18.7 us
  starting transfers between devices: 39.4 us -> 42.2 us
    ppermute x25 -> x26, waiting for transfers between devices: 23.4 us -> 18.7 us  [shifted(): return lax.ppermute(value, axis, [(i, (i + shift) % n) for i in range(n)])]
    ppermute x25 -> x26, starting transfers between devices: 39.4 us -> 42.2 us  [shifted(): return lax.ppermute(value, axis, [(i, (i + shift) % n) for i in range(n)])]
  transfers between devices with their start and end apart: 25 -> 26, of which waited for: 8 -> 8; matrix products, arithmetic and copies ran while one was open for 0% -> 0% of each run, Pallas kernels for 12% -> 12%
where the time goes in v7:
time: 151 us
  blocking collectives  52.9 us (35%)
  starting transfers between devices  42.2 us (28%)
  Pallas kernels  35.3 us (23%)
  waiting for transfers between devices  18.7 us (12%)
    all_to_all x3, blocking collectives, exchanged(): return lax.all_to_all(parts, axis, split_axis=0, concat_axis=0, tiled=True)  52.9 us
    ppermute x26, starting transfers between devices, shifted(): return lax.ppermute(value, axis, [(i, (i + shift) % n) for i in range(n)])  42.2 us
    pallas_call x21, Pallas kernels, call(): pl.pallas_call(body, in_specs=specs, out_specs=[pl.BlockSpec(memory_space...  35.3 us
    ppermute x26, waiting for transfers between devices, shifted(): return lax.ppermute(value, axis, [(i, (i + shift) % n) for i in range(n)])  18.7 us
  transfers between devices with their start and end apart: 26, of which 8 were waited for; matrix products, arithmetic and copies ran while one was open for 0% of the time, Pallas kernels for 12%

profile of v7, /device:TPU:1, one launch (start us, length us, event | category | flops | bytes accessed | tf_op | source)
XLA Modules:
  0.0 150.9 jit_solution(16920484709666406628)
XLA Ops:
  0.7 5.6 %shard_map.85 = (f32[32,1024]{1,0:T(8,128)S(1)}, f32[256,1024]{1,0:T(8,128)S(1)}, f32[1,384]{1,0:T(1,128)S(1)}) custom-call(s32[5]{0:T(128)S(1)} %stack.23.meta.refs_0_, bf16[32,4096]{1,0:T(8,128)(2,1)} %q_ref.1, bf16[256,4096]{1,0:T(8,128)(2,1)} %p_ref.1, bf16[4096,1024]{1,0:T(8,128)(2,1)} %w_ref.3), custom_call_target="tpu_custom_call" | custom-call | flops 2415919104 | tf_op jit(solution)/shard_map/pallas_call | solution.py:92
  6.4 3.3 %collective-permute-start = (f32[1,384]{1,0:T(1,128)S(1)}, f32[1,384]{1,0:T(1,128)S(1)}, u32[]{:S(2)}, u32[]{:S(2)}) collective-permute-start(f32[1,384]{1,0:T(1,128)S(1)} %get-tuple-element.55.own_ref), channel_id=1, source_target_pairs={{0,1},{1,0},{2,3},{3,2},{4,5},{5,4},{6,7},{7,6},{8,9},{9,8},{10,11... | collective-permute-start | bytes 4616 | tf_op jit(solution)/shard_map/ppermute | solution.py:21
  12.0 24.7 %all_to_all.15 = bf16[8,32,1152]{2,1,0:T(8,128)(2,1)S(1)} all-to-all(bf16[8,32,1152]{2,1,0:T(8,128)(2,1)S(1)} %get-tuple-element.56), channel_id=1, replica_groups=mesh['y'=4,'x'=4,'z'=8,'mp'=2] {'z'}, dimensions={0} | all-to-all | bytes 1179648 | tf_op jit(solution)/shard_map/all_to_all | solution.py:25
  42.2 9.2 %collective-permute-done.3.refs_2_.refs_3_ = bf16[256,1152]{1,0:T(8,128)(2,1)S(1)} collective-permute-done((bf16[256,1152]{1,0:T(8,128)(2,1)S(1)}, bf16[256,1152]{1,0:T(8,128)(2,1)S(1)}, u32[]{:S(2)}, u32[]{:S(2)}) %collective-permute-start.3) | collective-permute-done | bytes 589856 | tf_op jit(solution)/shard_map/ppermute | solution.py:21
  51.6 2.7 %collective-permute-start.6 = (bf16[128,1152]{1,0:T(8,128)(2,1)S(1)}, bf16[128,1152]{1,0:T(8,128)(2,1)S(1)}, u32[]{:S(2)}, u32[]{:S(2)}) collective-permute-start(bf16[128,1152]{1,0:T(8,128)(2,1)S(1)} %slice.17), channel_id=1, source_target_pairs={{0,48},{16,0},{32,16},{48,32},{1,49},{17,1},{33,17},{49,33},{2,50}... | collective-permute-start | bytes 884744 | tf_op jit(solution)/shard_map/ppermute | solution.py:21
  55.8 1.5 %collective-permute-start.10 = (bf16[128,1024]{1,0:T(8,128)(2,1)S(1)}, bf16[128,1024]{1,0:T(8,128)(2,1)S(1)}, u32[]{:S(2)}, u32[]{:S(2)}) collective-permute-start(bf16[128,1024]{1,0:T(8,128)(2,1)S(1)} %slice.15), channel_id=1, source_target_pairs={{0,192},{64,0},{128,64},{192,128},{1,193},{65,1},{129,65},{193,129... | collective-permute-start | bytes 786440 | tf_op jit(solution)/shard_map/ppermute | solution.py:21
  57.3 3.9 %collective-permute-done.8.refs_8_.refs_9_ = bf16[128,1024]{1,0:T(8,128)(2,1)S(1)} collective-permute-done((bf16[128,1024]{1,0:T(8,128)(2,1)S(1)}, bf16[128,1024]{1,0:T(8,128)(2,1)S(1)}, u32[]{:S(2)}, u32[]{:S(2)}) %collective-permute-start.8) | collective-permute-done | bytes 262176 | tf_op jit(solution)/shard_map/ppermute | solution.py:21
  61.4 2.3 %shard_map.87 = (f32[1024,512]{1,0:T(8,128)S(1)}, bf16[512,1024]{1,0:T(8,128)(2,1)S(1)}, f32[512,128]{1,0:T(8,128)S(1)}, f32[512,128]{1,0:T(8,128)S(1)}) custom-call(s32[5]{0:T(128)S(1)} %stack.23.meta.refs_0_, bf16[256,1152]{1,0:T(8,128)(2,1)S(1)} %bitcast.22, bf16[256,1152]{1,0:T(8,128)(2,1)S(1)} %collective-permute-done.3.refs_2_.refs_3_, ...), custom_call_target="tpu_custom_call" | custom-call | flops 1073741824 | tf_op jit(solution)/shard_map/pallas_call | solution.py:92
  63.7 4.2 %collective-permute-start.11 = (f32[1024,512]{1,0:T(8,128)S(1)}, f32[1024,512]{1,0:T(8,128)S(1)}, u32[]{:S(2)}, u32[]{:S(2)}) collective-permute-start(f32[1024,512]{1,0:T(8,128)S(1)} %get-tuple-element.67), channel_id=1, source_target_pairs={{0,1},{1,0},{2,3},{3,2},{4,5},{5,4},{6,7},{7,6},{8,9},{9,8},{10,11... | collective-permute-start | bytes 6291464 | tf_op jit(solution)/shard_map/ppermute | solution.py:21
  70.1 2.5 %collective-permute-start.13 = (f32[8,256]{1,0:T(8,128)S(1)}, f32[8,256]{1,0:T(8,128)S(1)}, u32[]{:S(2)}, u32[]{:S(2)}) collective-permute-start(f32[8,256]{1,0:T(8,128)S(1)} %get-tuple-element.69.refs_5_), channel_id=1, source_target_pairs={{0,128},{64,192},{128,0},{192,64},{1,129},{65,193},{129,1},{193,65... | collective-permute-start | bytes 24584 | tf_op jit(solution)/shard_map/ppermute | solution.py:21
  73.5 3.3 %shard_map.89 = (f32[1024,512]{1,0:T(8,128)S(1)}, f32[1024,512]{1,0:T(8,128)S(1)}, bf16[512,1024]{1,0:T(8,128)(2,1)S(1)}, bf16[1024,1024]{1,0:T(8,128)(2,1)S(1)}) custom-call(s32[5]{0:T(128)S(1)} %stack.23.meta.refs_0_, f32[128,512]{1,0:T(8,128)S(1)} %get-tuple-element.65.refs_1_.refs_4_.refs_3_, bf16[256,1152]{1,0:T(8,128)(2,1)S(1)} %bitcast.23, ...), custom_call_target="tpu_custom_call" | custom-call | flops 2147483648 | tf_op jit(solution)/shard_map/pallas_call | solution.py:92
  78.4 12.2 %all_to_all.16.refs_2_ = f32[32,2,512]{2,1,0:T(2,128)S(1)} all-to-all(f32[32,2,512]{2,1,0:T(2,128)S(1)} %broadcast_in_dim.22), channel_id=1, replica_groups=mesh['y'=4,'x'=4,'z'=8,'mp'=2] {'x','z'}, dimensions={0} | all-to-all | bytes 262144 | tf_op jit(solution)/shard_map/all_to_all | solution.py:25
  91.6 2.0 %collective-permute-start.15 = (bf16[1024,512]{1,0:T(8,128)(2,1)S(1)}, bf16[1024,512]{1,0:T(8,128)(2,1)S(1)}, u32[]{:S(2)}, u32[]{:S(2)}) collective-permute-start(bf16[1024,512]{1,0:T(8,128)(2,1)S(1)} %get-tuple-element.72.grad_ref.refs_1_), channel_id=1, source_target_pairs={{0,1},{1,0},{2,3},{3,2},{4,5},{5,4},{6,7},{7,6},{8,9},{9,8},{10,11... | collective-permute-start | bytes 3145736 | tf_op jit(solution)/shard_map/ppermute | solution.py:21
  93.6 1.8 %shard_map.92.refs_3_ = bf16[512,1024]{1,0:T(8,128)(2,1)S(1)} custom-call(s32[5]{0:T(128)S(1)} %stack.23.meta.refs_0_, bf16[1024,512]{1,0:T(8,128)(2,1)S(1)} %get-tuple-element.72.grad_ref.refs_1_, bf16[1024,1024]{1,0:T(8,128)(2,1)S(1)} %get-tuple-element.73.p_ref.refs_2_), custom_call_target="tpu_custom_call" | custom-call | flops 1073741824 | tf_op jit(solution)/shard_map/pallas_call | solution.py:92
  97.8 2.3 %collective-permute-start.18 = (bf16[128,1024]{1,0:T(8,128)(2,1)S(1)}, bf16[128,1024]{1,0:T(8,128)(2,1)S(1)}, u32[]{:S(2)}, u32[]{:S(2)}) collective-permute-start(bf16[128,1024]{1,0:T(8,128)(2,1)S(1)} %bitcast.28), channel_id=1, source_target_pairs={{0,48},{16,0},{32,16},{48,32},{1,49},{17,1},{33,17},{49,33},{2,50}... | collective-permute-start | bytes 786440 | tf_op jit(solution)/shard_map/ppermute | solution.py:21
  102.0 2.1 %collective-permute-start.19 = (bf16[128,1024]{1,0:T(8,128)(2,1)S(1)}, bf16[128,1024]{1,0:T(8,128)(2,1)S(1)}, u32[]{:S(2)}, u32[]{:S(2)}) collective-permute-start(bf16[128,1024]{1,0:T(8,128)(2,1)S(1)} %get-tuple-element.89), channel_id=1, source_target_pairs={{0,192},{64,0},{128,64},{192,128},{1,193},{65,1},{129,65},{193,129... | collective-permute-start | bytes 786440 | tf_op jit(solution)/shard_map/ppermute | solution.py:21
  105.5 1.8 %shard_map.95 = (bf16[256,1024]{1,0:T(8,128)(2,1)S(1)}, bf16[256,1024]{1,0:T(8,128)(2,1)S(1)}) custom-call(s32[5]{0:T(128)S(1)} %stack.23.meta.refs_0_, bf16[1024,512]{1,0:T(8,128)(2,1)S(1)} %get-tuple-element.72.grad_ref.refs_1_, bf16[1024,512]{1,0:T(8,128)(2,1)S(1)} %collective-permute-done.15.refs_1_.refs_2_, ...), custom_call_target="tpu_custom_call" | custom-call | flops 1073741824 | tf_op jit(solution)/shard_map/pallas_call | solution.py:92
  107.6 2.7 %collective-permute-start.21 = (bf16[256,1024]{1,0:T(8,128)(2,1)S(1)}, bf16[256,1024]{1,0:T(8,128)(2,1)S(1)}, u32[]{:S(2)}, u32[]{:S(2)}) collective-permute-start(bf16[256,1024]{1,0:T(8,128)(2,1)S(1)} %get-tuple-element.86), channel_id=1, source_target_pairs={{0,48},{16,0},{32,16},{48,32},{1,49},{17,1},{33,17},{49,33},{2,50}... | collective-permute-start | bytes 1572872 | tf_op jit(solution)/shard_map/ppermute | solution.py:21
  110.5 2.7 %collective-permute-start.23 = (bf16[256,1024]{1,0:T(8,128)(2,1)S(1)}, bf16[256,1024]{1,0:T(8,128)(2,1)S(1)}, u32[]{:S(2)}, u32[]{:S(2)}) collective-permute-start(bf16[256,1024]{1,0:T(8,128)(2,1)S(1)} %get-tuple-element.91), channel_id=1, source_target_pairs={{0,192},{64,0},{128,64},{192,128},{1,193},{65,1},{129,65},{193,129... | collective-permute-start | bytes 1572872 | tf_op jit(solution)/shard_map/ppermute | solution.py:21
  113.2 4.0 %shard_map.102 = (bf16[2048,1024]{1,0:T(8,128)(2,1)S(1)}, bf16[2048,1024]{1,0:T(8,128)(2,1)S(1)}) custom-call(s32[5]{0:T(128)S(1)} %stack.23.meta.refs_0_, bf16[4096,1024]{1,0:T(8,128)(2,1)} %w_ref.3, bf16[4096,1024]{1,0:T(8,128)(2,1)} %copy-done), custom_call_target="tpu_custom_call" | custom-call | tf_op jit(solution)/shard_map/pallas_call | solution.py:92
  120.9 2.2 %collective-permute-done.22.refs_1_ = bf16[256,1024]{1,0:T(8,128)(2,1)S(1)} collective-permute-done((bf16[256,1024]{1,0:T(8,128)(2,1)S(1)}, bf16[256,1024]{1,0:T(8,128)(2,1)S(1)}, u32[]{:S(2)}, u32[]{:S(2)}) %collective-permute-start.22) | collective-permute-done | bytes 524320 | tf_op jit(solution)/shard_map/ppermute | solution.py:21
  123.1 15.9 %all_to_all.17.refs_1_ = bf16[8,32,1024]{2,1,0:T(8,128)(2,1)S(1)} all-to-all(bf16[8,32,1024]{2,1,0:T(8,128)(2,1)S(1)} %bitcast.25), channel_id=1, replica_groups=mesh['y'=4,'x'=4,'z'=8,'mp'=2] {'z'}, dimensions={0} | all-to-all | bytes 1048576 | tf_op jit(solution)/shard_map/all_to_all | solution.py:25
  139.2 5.0 %collective-permute-start.25 = (bf16[256,1024]{1,0:T(8,128)(2,1)S(1)}, bf16[256,1024]{1,0:T(8,128)(2,1)S(1)}, u32[]{:S(2)}, u32[]{:S(2)}) collective-permute-start(bf16[256,1024]{1,0:T(8,128)(2,1)S(1)} %shard_map.104.pg_ref), channel_id=1, source_target_pairs={{0,1},{1,0},{2,3},{3,2},{4,5},{5,4},{6,7},{7,6},{8,9},{9,8},{10,11... | collective-permute-start | bytes 1572872 | tf_op jit(solution)/shard_map/ppermute | solution.py:21
  146.3 4.5 %shard_map.105 = (bf16[32,2048]{1,0:T(8,128)(2,1)}, bf16[256,2048]{1,0:T(8,128)(2,1)}, f32[1,32]{1,0:T(1,128)}) custom-call(s32[5]{0:T(128)S(1)} %stack.23.meta.refs_0_, f32[40,1024]{1,0:T(8,128)S(1)} %shard_map.103.qg_ref, f32[40,1024]{1,0:T(8,128)S(1)} %collective-permute-done.24.qgo_ref, bf16[256,1024]{1,0:T(8,128)(2,1)S(1)} %shard_map.104.pg_ref, ...), custom_call_target="tpu_custom_call" | custom-call | flops 2415919104 | tf_op jit(solution)/shard_map/pallas_call | solution.py:92
  (77 shorter events, 27.2 us)
Async XLA Ops:
  11.4 25.3 %collective-permute-start.2 = (bf16[4096,1024]{1,0:T(8,128)(2,1)}, bf16[4096,1024]{1,0:T(8,128)(2,1)S(1)}, u32[]{:S(2)}, u32[]{:S(2)}) collective-permute-start(bf16[4096,1024]{1,0:T(8,128)(2,1)} %w_ref.3), channel_id=1, source_target_pairs={{0,1},{1,0},{2,3},{3,2},{4,5},{5,4},{6,7},{7,6},{8,9},{9,8},{10,11... | collective-permute-start | bytes 25165832 | tf_op jit(solution)/shard_map/ppermute | solution.py:21
  11.8 24.9 %collective-permute-start.1 = (f32[288,1024]{1,0:T(8,128)S(1)}, f32[288,1024]{1,0:T(8,128)S(1)}, u32[]{:S(2)}, u32[]{:S(2)}) collective-permute-start(f32[288,1024]{1,0:T(8,128)S(1)} %get-tuple-element.57.unit_ref), channel_id=1, source_target_pairs={{0,1},{1,0},{2,3},{3,2},{4,5},{5,4},{6,7},{7,6},{8,9},{9,8},{10,11... | collective-permute-start | bytes 3538952 | tf_op jit(solution)/shard_map/ppermute | solution.py:21
  36.7 14.7 %collective-permute-start.3 = (bf16[256,1152]{1,0:T(8,128)(2,1)S(1)}, bf16[256,1152]{1,0:T(8,128)(2,1)S(1)}, u32[]{:S(2)}, u32[]{:S(2)}) collective-permute-start(bf16[256,1152]{1,0:T(8,128)(2,1)S(1)} %bitcast.20), channel_id=1, source_target_pairs={{0,16},{16,32},{32,48},{48,0},{1,17},{17,33},{33,49},{49,1},{2,18}... | collective-permute-start | bytes 1769480 | tf_op jit(solution)/shard_map/ppermute | solution.py:21
  38.0 13.6 %collective-permute-start.5 = (bf16[256,1152]{1,0:T(8,128)(2,1)S(1)}, bf16[256,1152]{1,0:T(8,128)(2,1)S(1)}, u32[]{:S(2)}, u32[]{:S(2)}) collective-permute-start(bf16[256,1152]{1,0:T(8,128)(2,1)S(1)} %bitcast.21), channel_id=1, source_target_pairs={{0,48},{16,0},{32,16},{48,32},{1,49},{17,1},{33,17},{49,33},{2,50}... | collective-permute-start | bytes 1769480 | tf_op jit(solution)/shard_map/ppermute | solution.py:21
  39.5 14.9 %collective-permute-start.7 = (bf16[256,1024]{1,0:T(8,128)(2,1)S(1)}, bf16[256,1024]{1,0:T(8,128)(2,1)S(1)}, u32[]{:S(2)}, u32[]{:S(2)}) collective-permute-start(bf16[256,1024]{1,0:T(8,128)(2,1)S(1)} %get-tuple-element.60.refs_6_.refs_7_), channel_id=1, source_target_pairs={{0,64},{64,128},{128,192},{192,0},{1,65},{65,129},{129,193},{193,1... | collective-permute-start | bytes 1572872 | tf_op jit(solution)/shard_map/ppermute | solution.py:21
  40.8 15.0 %collective-permute-start.9 = (bf16[256,1024]{1,0:T(8,128)(2,1)S(1)}, bf16[256,1024]{1,0:T(8,128)(2,1)S(1)}, u32[]{:S(2)}, u32[]{:S(2)}) collective-permute-start(bf16[256,1024]{1,0:T(8,128)(2,1)S(1)} %get-tuple-element.60.refs_6_.refs_7_), channel_id=1, source_target_pairs={{0,192},{64,0},{128,64},{192,128},{1,193},{65,1},{129,65},{193,129... | collective-permute-start | bytes 1572872 | tf_op jit(solution)/shard_map/ppermute | solution.py:21
  51.5 9.9 %collective-permute-start.4 = (bf16[128,1152]{1,0:T(8,128)(2,1)S(1)}, bf16[128,1152]{1,0:T(8,128)(2,1)S(1)}, u32[]{:S(2)}, u32[]{:S(2)}) collective-permute-start(bf16[128,1152]{1,0:T(8,128)(2,1)S(1)} %slice.16), channel_id=1, source_target_pairs={{0,16},{16,32},{32,48},{48,0},{1,17},{17,33},{33,49},{49,1},{2,18}... | collective-permute-start | bytes 884744 | tf_op jit(solution)/shard_map/ppermute | solution.py:21
  51.6 9.8 %collective-permute-start.6 = (bf16[128,1152]{1,0:T(8,128)(2,1)S(1)}, bf16[128,1152]{1,0:T(8,128)(2,1)S(1)}, u32[]{:S(2)}, u32[]{:S(2)}) collective-permute-start(bf16[128,1152]{1,0:T(8,128)(2,1)S(1)} %slice.17), channel_id=1, source_target_pairs={{0,48},{16,0},{32,16},{48,32},{1,49},{17,1},{33,17},{49,33},{2,50}... | collective-permute-start | bytes 884744 | tf_op jit(solution)/shard_map/ppermute | solution.py:21
  54.4 6.9 %collective-permute-start.8 = (bf16[128,1024]{1,0:T(8,128)(2,1)S(1)}, bf16[128,1024]{1,0:T(8,128)(2,1)S(1)}, u32[]{:S(2)}, u32[]{:S(2)}) collective-permute-start(bf16[128,1024]{1,0:T(8,128)(2,1)S(1)} %slice.14), channel_id=1, source_target_pairs={{0,64},{64,128},{128,192},{192,0},{1,65},{65,129},{129,193},{193,1... | collective-permute-start | bytes 786440 | tf_op jit(solution)/shard_map/ppermute | solution.py:21
  55.8 5.6 %collective-permute-start.10 = (bf16[128,1024]{1,0:T(8,128)(2,1)S(1)}, bf16[128,1024]{1,0:T(8,128)(2,1)S(1)}, u32[]{:S(2)}, u32[]{:S(2)}) collective-permute-start(bf16[128,1024]{1,0:T(8,128)(2,1)S(1)} %slice.15), channel_id=1, source_target_pairs={{0,192},{64,0},{128,64},{192,128},{1,193},{65,1},{129,65},{193,129... | collective-permute-start | bytes 786440 | tf_op jit(solution)/shard_map/ppermute | solution.py:21
  63.7 13.2 %collective-permute-start.11 = (f32[1024,512]{1,0:T(8,128)S(1)}, f32[1024,512]{1,0:T(8,128)S(1)}, u32[]{:S(2)}, u32[]{:S(2)}) collective-permute-start(f32[1024,512]{1,0:T(8,128)S(1)} %get-tuple-element.67), channel_id=1, source_target_pairs={{0,1},{1,0},{2,3},{3,2},{4,5},{5,4},{6,7},{7,6},{8,9},{9,8},{10,11... | collective-permute-start | bytes 6291464 | tf_op jit(solution)/shard_map/ppermute | solution.py:21
  68.8 8.1 %collective-permute-start.12 = (f32[8,256]{1,0:T(8,128)S(1)}, f32[8,256]{1,0:T(8,128)S(1)}, u32[]{:S(2)}, u32[]{:S(2)}) collective-permute-start(f32[8,256]{1,0:T(8,128)S(1)} %get-tuple-element.69.refs_5_), channel_id=1, source_target_pairs={{0,64},{64,128},{128,192},{192,0},{1,65},{65,129},{129,193},{193,1... | collective-permute-start | bytes 24584 | tf_op jit(solution)/shard_map/ppermute | solution.py:21
  70.1 6.7 %collective-permute-start.13 = (f32[8,256]{1,0:T(8,128)S(1)}, f32[8,256]{1,0:T(8,128)S(1)}, u32[]{:S(2)}, u32[]{:S(2)}) collective-permute-start(f32[8,256]{1,0:T(8,128)S(1)} %get-tuple-element.69.refs_5_), channel_id=1, source_target_pairs={{0,128},{64,192},{128,0},{192,64},{1,129},{65,193},{129,1},{193,65... | collective-permute-start | bytes 24584 | tf_op jit(solution)/shard_map/ppermute | solution.py:21
  72.6 4.2 %collective-permute-start.14 = (f32[8,256]{1,0:T(8,128)S(1)}, f32[8,256]{1,0:T(8,128)S(1)}, u32[]{:S(2)}, u32[]{:S(2)}) collective-permute-start(f32[8,256]{1,0:T(8,128)S(1)} %get-tuple-element.69.refs_5_), channel_id=1, source_target_pairs={{0,192},{64,0},{128,64},{192,128},{1,193},{65,1},{129,65},{193,129... | collective-permute-start | bytes 24584 | tf_op jit(solution)/shard_map/ppermute | solution.py:21
  91.6 4.3 %collective-permute-start.15 = (bf16[1024,512]{1,0:T(8,128)(2,1)S(1)}, bf16[1024,512]{1,0:T(8,128)(2,1)S(1)}, u32[]{:S(2)}, u32[]{:S(2)}) collective-permute-start(bf16[1024,512]{1,0:T(8,128)(2,1)S(1)} %get-tuple-element.72.grad_ref.refs_1_), channel_id=1, source_target_pairs={{0,1},{1,0},{2,3},{3,2},{4,5},{5,4},{6,7},{7,6},{8,9},{9,8},{10,11... | collective-permute-start | bytes 3145736 | tf_op jit(solution)/shard_map/ppermute | solution.py:21
  97.4 10.0 %collective-permute-start.17 = (bf16[128,1024]{1,0:T(8,128)(2,1)S(1)}, bf16[128,1024]{1,0:T(8,128)(2,1)S(1)}, u32[]{:S(2)}, u32[]{:S(2)}) collective-permute-start(bf16[128,1024]{1,0:T(8,128)(2,1)S(1)} %bitcast.29), channel_id=1, source_target_pairs={{0,16},{16,32},{32,48},{48,0},{1,17},{17,33},{33,49},{49,1},{2,18}... | collective-permute-start | bytes 786440 | tf_op jit(solution)/shard_map/ppermute | solution.py:21
  97.8 9.6 %collective-permute-start.18 = (bf16[128,1024]{1,0:T(8,128)(2,1)S(1)}, bf16[128,1024]{1,0:T(8,128)(2,1)S(1)}, u32[]{:S(2)}, u32[]{:S(2)}) collective-permute-start(bf16[128,1024]{1,0:T(8,128)(2,1)S(1)} %bitcast.28), channel_id=1, source_target_pairs={{0,48},{16,0},{32,16},{48,32},{1,49},{17,1},{33,17},{49,33},{2,50}... | collective-permute-start | bytes 786440 | tf_op jit(solution)/shard_map/ppermute | solution.py:21
  101.4 8.9 %collective-permute-start.16 = (bf16[128,1024]{1,0:T(8,128)(2,1)S(1)}, bf16[128,1024]{1,0:T(8,128)(2,1)S(1)}, u32[]{:S(2)}, u32[]{:S(2)}) collective-permute-start(bf16[128,1024]{1,0:T(8,128)(2,1)S(1)} %get-tuple-element.79), channel_id=1, source_target_pairs={{0,64},{64,128},{128,192},{192,0},{1,65},{65,129},{129,193},{193,1... | collective-permute-start | bytes 786440 | tf_op jit(solution)/shard_map/ppermute | solution.py:21
  102.0 8.2 %collective-permute-start.19 = (bf16[128,1024]{1,0:T(8,128)(2,1)S(1)}, bf16[128,1024]{1,0:T(8,128)(2,1)S(1)}, u32[]{:S(2)}, u32[]{:S(2)}) collective-permute-start(bf16[128,1024]{1,0:T(8,128)(2,1)S(1)} %get-tuple-element.89), channel_id=1, source_target_pairs={{0,192},{64,0},{128,64},{192,128},{1,193},{65,1},{129,65},{193,129... | collective-permute-start | bytes 786440 | tf_op jit(solution)/shard_map/ppermute | solution.py:21
  107.5 13.2 %collective-permute-start.20 = (bf16[256,1024]{1,0:T(8,128)(2,1)S(1)}, bf16[256,1024]{1,0:T(8,128)(2,1)S(1)}, u32[]{:S(2)}, u32[]{:S(2)}) collective-permute-start(bf16[256,1024]{1,0:T(8,128)(2,1)S(1)} %get-tuple-element.85), channel_id=1, source_target_pairs={{0,16},{16,32},{32,48},{48,0},{1,17},{17,33},{33,49},{49,1},{2,18}... | collective-permute-start | bytes 1572872 | tf_op jit(solution)/shard_map/ppermute | solution.py:21
  107.6 13.1 %collective-permute-start.21 = (bf16[256,1024]{1,0:T(8,128)(2,1)S(1)}, bf16[256,1024]{1,0:T(8,128)(2,1)S(1)}, u32[]{:S(2)}, u32[]{:S(2)}) collective-permute-start(bf16[256,1024]{1,0:T(8,128)(2,1)S(1)} %get-tuple-element.86), channel_id=1, source_target_pairs={{0,48},{16,0},{32,16},{48,32},{1,49},{17,1},{33,17},{49,33},{2,50}... | collective-permute-start | bytes 1572872 | tf_op jit(solution)/shard_map/ppermute | solution.py:21
  110.4 12.6 %collective-permute-start.22 = (bf16[256,1024]{1,0:T(8,128)(2,1)S(1)}, bf16[256,1024]{1,0:T(8,128)(2,1)S(1)}, u32[]{:S(2)}, u32[]{:S(2)}) collective-permute-start(bf16[256,1024]{1,0:T(8,128)(2,1)S(1)} %get-tuple-element.90), channel_id=1, source_target_pairs={{0,64},{64,128},{128,192},{192,0},{1,65},{65,129},{129,193},{193,1... | collective-permute-start | bytes 1572872 | tf_op jit(solution)/shard_map/ppermute | solution.py:21
  110.5 12.6 %collective-permute-start.23 = (bf16[256,1024]{1,0:T(8,128)(2,1)S(1)}, bf16[256,1024]{1,0:T(8,128)(2,1)S(1)}, u32[]{:S(2)}, u32[]{:S(2)}) collective-permute-start(bf16[256,1024]{1,0:T(8,128)(2,1)S(1)} %get-tuple-element.91), channel_id=1, source_target_pairs={{0,192},{64,0},{128,64},{192,128},{1,193},{65,1},{129,65},{193,129... | collective-permute-start | bytes 1572872 | tf_op jit(solution)/shard_map/ppermute | solution.py:21
  139.2 7.1 %collective-permute-start.25 = (bf16[256,1024]{1,0:T(8,128)(2,1)S(1)}, bf16[256,1024]{1,0:T(8,128)(2,1)S(1)}, u32[]{:S(2)}, u32[]{:S(2)}) collective-permute-start(bf16[256,1024]{1,0:T(8,128)(2,1)S(1)} %shard_map.104.pg_ref), channel_id=1, source_target_pairs={{0,1},{1,0},{2,3},{3,2},{4,5},{5,4},{6,7},{7,6},{8,9},{9,8},{10,11... | collective-permute-start | bytes 1572872 | tf_op jit(solution)/shard_map/ppermute | solution.py:21
  (6 other events, 72.9 us)
